TPU v7x, 256 devices: a whole 4x4x8 slice. The times are simulated.
256 devices in a mesh: dp: 8 (over y, core), expert: 32 (over z, x).
Axes of the slice: x: 4, y: 4, z: 8, core: 2. Of those that a mesh axis runs over, the one named last changes fastest.
Arguments:
- tokens: bfloat16 [2048, 4096], P(('dp', 'expert')), may hold values from -6 to 6
- gate_values: bfloat16 [2048, 8], P(('dp', 'expert')), may hold values from 0.049804688 to 0.59765625
- expert_ids: int32 [2048, 8], P(('dp', 'expert')), may hold values from 0 to 63, all different within a row
- gate_weight: bfloat16 [64, 1536, 4096], P('expert', 'dp'), may hold values from -0.09375 to 0.09375
- up_weight: bfloat16 [64, 1536, 4096], P('expert', 'dp'), may hold values from -0.09375 to 0.09375
- down_weight: bfloat16 [64, 1536, 4096], P('expert', 'dp'), may hold values from -0.15625 to 0.15625
Outputs:
- mixed_out: bfloat16 [2048, 4096], P(('dp', 'expert'))
All inputs are finite; a program needn't handle non-finite values.
Results may differ from a plain program's by a relative error of at most 0.019.
Values may be sent and summed in bfloat16 or wider, within the bound.
No kernel may reach another device: no remote copies, remote signals or barrier semaphores. Data moves between devices by JAX's collectives and lax.ppermute only.
A program may use at most 128 MiB of HBM per device.

v0:
```python
import jax
import jax.numpy as jnp
from jax import lax
from jax.sharding import PartitionSpec as P


def slot_ranks(choice_table, expert_count):
    onehot = (
        choice_table[:, :, None] == jnp.arange(expert_count, dtype=jnp.int32)[None, None, :]
    ).astype(jnp.int32)
    before = jnp.cumsum(onehot, axis=1) - onehot
    return jnp.sum(before * onehot, axis=2)


def body(tokens, gate_values, expert_ids, gate_weight, up_weight, down_weight):
    dp_count = lax.axis_size("dp")
    column_count = lax.axis_size("expert")
    per_device = gate_weight.shape[0]
    expert_count = per_device * column_count
    token_rows = tokens.shape[0]
    model_width = tokens.shape[1]
    top_count = expert_ids.shape[1]
    capacity = max(2, (5 * token_rows * top_count + 4 * expert_count - 1) // (4 * expert_count))
    shared_tokens, shared_gates = (
        lax.all_gather(tokens, "dp", axis=0, tiled=True),
        lax.all_gather(gate_values, "dp", axis=0, tiled=True),
    )
    shared_table = lax.all_gather(expert_ids, "dp", axis=0, tiled=True)
    choice_table = shared_table.reshape(dp_count, token_rows * top_count)
    ranked = slot_ranks(choice_table, expert_count)
    keep_mask = ranked < capacity
    group_index = jnp.arange(dp_count, dtype=jnp.int32)[:, None]
    total_slots = expert_count * dp_count * capacity
    target = (choice_table * dp_count + group_index) * capacity + ranked
    target = jnp.where(keep_mask, target, total_slots)
    repeated = jnp.repeat(shared_tokens, top_count, axis=0)
    buffer = (
        jnp.zeros((total_slots, model_width), jnp.bfloat16)
        .at[target.reshape(-1)]
        .set(repeated, mode="drop")
    )
    buffer, target, keep_mask = (
        buffer.reshape(column_count, per_device, dp_count, capacity, model_width),
        target,
        keep_mask,
    )
    arrived = lax.all_to_all(buffer, "expert", split_axis=0, concat_axis=0, tiled=True)
    gate_act = jnp.einsum(
        "jlgcd,lhd->jlgch", arrived, gate_weight, preferred_element_type=jnp.float32
    )
    up_act = jnp.einsum("jlgcd,lhd->jlgch", arrived, up_weight, preferred_element_type=jnp.float32)
    hidden = (jax.nn.silu(gate_act) * up_act).astype(jnp.bfloat16)
    pieces = jnp.einsum(
        "jlgch,lhd->jlgcd", hidden, down_weight, preferred_element_type=jnp.float32
    ).astype(jnp.bfloat16)
    returned_rows = lax.all_to_all(pieces, "expert", split_axis=0, concat_axis=0, tiled=True)
    values = returned_rows.reshape(-1, model_width)
    total_slots = values.shape[0]
    picked = values[jnp.minimum(target, total_slots - 1)].astype(jnp.float32)
    weights_kept = jnp.where(
        keep_mask, shared_gates.reshape(dp_count, token_rows * top_count).astype(jnp.float32), 0.0
    )
    weighted = picked * weights_kept[:, :, None]
    combined = jnp.sum(weighted.reshape(dp_count, token_rows, top_count, model_width), axis=2)
    mixed_out = lax.psum_scatter(
        combined.astype(jnp.bfloat16), "dp", scatter_dimension=0, tiled=True
    ).astype(jnp.float32)
    return mixed_out.reshape(token_rows, model_width).astype(jnp.bfloat16)


def solution(mesh):
    return jax.shard_map(
        body,
        mesh=mesh,
        in_specs=(
            P(("dp", "expert"), None),
            P(("dp", "expert"), None),
            P(("dp", "expert"), None),
            P("expert", "dp", None),
            P("expert", "dp", None),
            P("expert", "dp", None),
        ),
        out_specs=P(("dp", "expert"), None),
        check_vma=False,
    )
```

profile of v0, /device:TPU:2, one launch (start us, length us, event | category | flops | bytes accessed | tf_op | source)
XLA Modules:
  0.0 587.8 jit_solution(3127235769829631959)
XLA Ops:
  6.5 13.6 %all_gather.9 = s32[64,8]{1,0:T(8,128)S(1)} all-gather(s32[8,8]{1,0:T(8,128)} %param.8), channel_id=1, replica_groups=mesh['dp'=8,'expert'=32] {'dp'}, dimensions={0}, use_global_device_ids=true | all-gather | bytes 2304 | tf_op jit(solution)/shard_map/all_gather | solution.py:28
  20.3 0.1 mul.69
  20.4 0.1 copy.20
  20.5 1.4 fusion.37
  22.0 14.4 %all_gather.10 = bf16[64,4096]{1,0:T(8,128)(2,1)} all-gather(bf16[8,4096]{1,0:T(8,128)(2,1)} %param.6), channel_id=1, replica_groups=mesh['dp'=8,'expert'=32] {'dp'}, dimensions={0}, use_global_device_ids=true | all-gather | bytes 589824 | tf_op jit(solution)/shard_map/all_gather | solution.py:25
  36.4 11.7 %scatter_custom_fusion = bf16[1024,4096]{1,0:T(8,128)(2,1)} fusion(s32[512]{0:T(512)S(1)} %bitcast.61, bf16[]{:T(256)} %constant.8.clone.1, bf16[64,4096]{1,0:T(8,128)(2,1)} %all_gather.10), kind=kCustom, calls=%fused_computation.9 | custom fusion | bytes 8912898 | tf_op jit(solution)/shard_map/scatter | solution.py:40
  48.1 14.2 %reshape.144 = bf16[32,2,8,2,4096]{4,3,2,1,0:T(2,128)(2,1)} reshape(bf16[1024,4096]{1,0:T(8,128)(2,1)} %scatter_custom_fusion) | data formatting | bytes 16777216 | tf_op jit(solution)/shard_map/reshape | solution.py:43
  62.3 16.2 %copy.22 = bf16[32,2,8,2,4096]{4,2,3,1,0:T(8,128)(2,1)} copy(bf16[32,2,8,2,4096]{4,3,2,1,0:T(2,128)(2,1)} %reshape.144) | data formatting | bytes 16777216 | tf_op jit(solution)/shard_map/reshape | solution.py:43
  78.5 197.7 %all_to_all.10 = bf16[32,2,8,2,4096]{4,2,3,1,0:T(8,128)(2,1)S(1)} all-to-all(bf16[32,2,8,2,4096]{4,2,3,1,0:T(8,128)(2,1)} %copy.22), channel_id=1, replica_groups=mesh['dp'=8,'expert'=32] {'expert'}, dimensions={0} | all-to-all | bytes 16777216 | tf_op jit(solution)/shard_map/all_to_all | solution.py:47
  276.2 3.2 copy-done.2
  279.4 4.2 fusion.12
  283.6 6.7 %fusion.27 = bf16[32,2,8,2,192]{4,2,3,0,1:T(8,128)(2,1)S(1)} fusion(bf16[2,192,4096]{2,1,0:T(8,128)(2,1)} %param.10, bf16[32,2,8,2,4096]{4,2,3,1,0:T(8,128)(2,1)} %copy-done.2, f32[32,2,8,2,192]{4,2,3,0,1:T(8,128)S(1)} %fusion.12), kind=kOutput, calls=%fused_computation.19 | convolution fusion | flops 1611792384 | bytes 12713984 | tf_op jit(solution)/shard_map/jlgcd,lhd->jlgch/dot_general | solution.py:51
  290.4 5.6 convert_bitcast_fusion
  295.9 7.7 %copy.25 = bf16[32,2,8,2,4096]{4,2,3,1,0:T(8,128)(2,1)} copy(bf16[32,2,8,2,4096]{4,2,3,0,1:T(8,128)(2,1)} %convert_bitcast_fusion) | data formatting | bytes 16777216 | tf_op jit(solution)/shard_map/convert_element_type | solution.py:55
  303.6 5.8 all-to-all-start.1
  309.5 11.4 %all_gather.11 = bf16[64,8]{1,0:T(8,128)(2,1)S(1)} all-gather(bf16[8,8]{1,0:T(8,128)(2,1)S(1)} %copy-done.3), channel_id=1, replica_groups=mesh['dp'=8,'expert'=32] {'dp'}, dimensions={0}, use_global_device_ids=true | all-gather | bytes 1152 | tf_op jit(solution)/shard_map/all_gather | solution.py:26
  320.9 0.1 copy.29
  321.0 0.1 copy.27
  321.4 176.6 %all-to-all-done.1 = bf16[32,2,8,2,4096]{4,2,3,1,0:T(8,128)(2,1)} async-done(((bf16[32,2,8,2,4096]{4,2,3,1,0:T(8,128)(2,1)}), bf16[32,2,8,2,4096]{4,2,3,1,0:T(8,128)(2,1)}, u32[]{:S(2)}, u32[]{:S(2)}) %all-to-all-start.1) | async-done | bytes 8388640 | tf_op jit(solution)/shard_map/all_to_all | solution.py:56
  497.9 16.3 %copy.26 = bf16[32,2,8,2,4096]{4,3,2,1,0:T(2,128)(2,1)} copy(bf16[32,2,8,2,4096]{4,2,3,1,0:T(8,128)(2,1)} %all-to-all-done.1) | data formatting | bytes 16777216 | tf_op jit(solution)/shard_map/all_to_all | solution.py:56
  514.2 13.1 %reshape.145 = bf16[1024,4096]{1,0:T(8,128)(2,1)} reshape(bf16[32,2,8,2,4096]{4,3,2,1,0:T(2,128)(2,1)} %copy.26) | data formatting | bytes 16777216 | tf_op jit(solution)/shard_map/reshape | solution.py:57
  527.3 13.2 %gather_fusion = bf16[512,4096]{1,0:T(8,128)(2,1)} fusion(bf16[1024,4096]{1,0:T(8,128)(2,1)} %reshape.145, s32[1024]{0:T(1024)S(1)} %pad_clamp_fusion), kind=kCustom, calls=%fused_computation | custom fusion | bytes 8390656 | tf_op jit(solution)/shard_map/gather | solution.py:59
  540.5 6.4 %fusion = bf16[8,8,4096]{2,1,0:T(8,128)(2,1)} fusion(f32[8,8,8]{2,1,0:T(8,128)S(1)} %copy.30, bf16[512,4096]{1,0:T(8,128)(2,1)} %gather_fusion), kind=kLoop, calls=%fused_computation.3 | loop fusion | flops 6029312 | bytes 4720640 | tf_op jit(solution)/shard_map/reduce_sum | solution.py:64
  546.9 33.9 %reduce-scatter.2.cloned.1.call-done = bf16[1,8,4096]{2,1,0:T(8,128)(2,1)} async-done(((bf16[8,8,4096]{2,1,0:T(8,128)(2,1)}), bf16[1,8,4096]{2,1,0:T(8,128)(2,1)}) %reduce-scatter.2.cloned.1.call-update) | async-done | bytes 65552 | tf_op jit(solution)/shard_map/reduce_scatter | solution.py:65
  (24 shorter events, 0.7 us)
Async XLA Ops:
  6.5 283.8 %copy-start = (bf16[2,192,4096]{2,1,0:T(8,128)(2,1)S(1)}, bf16[2,192,4096]{2,1,0:T(8,128)(2,1)}, u32[]{:S(2)}) copy-start(bf16[2,192,4096]{2,1,0:T(8,128)(2,1)} %param.11) | copy-start | bytes 9437188
  276.2 3.2 copy-start.2
  303.6 5.9 %copy-start.3 = (bf16[8,8]{1,0:T(8,128)(2,1)S(1)}, bf16[8,8]{1,0:T(8,128)(2,1)}, u32[]{:S(2)}) copy-start(bf16[8,8]{1,0:T(8,128)(2,1)} %param.7) | copy-start | bytes 388
  303.6 194.3 %all-to-all-start.1 = ((bf16[32,2,8,2,4096]{4,2,3,1,0:T(8,128)(2,1)}), bf16[32,2,8,2,4096]{4,2,3,1,0:T(8,128)(2,1)}, u32[]{:S(2)}, u32[]{:S(2)}) async-start(bf16[32,2,8,2,4096]{4,2,3,1,0:T(8,128)(2,1)} %copy.25), calls=%async_computation.1 | async-start | bytes 16777216 | tf_op jit(solution)/shard_map/all_to_all | solution.py:56
  309.4 271.4 %reduce-scatter.2.cloned.1.call-start = ((), (), s32[]{:S(2)}) async-start(), calls=%async_computation.3 | async-start | bytes 589824 | tf_op jit(solution)/shard_map/reduce_scatter | solution.py:65
  527.3 53.5 %copy-start.1 = (bf16[2,192,4096]{2,1,0:T(8,128)(2,1)S(1)}, bf16[2,192,4096]{2,1,0:T(8,128)(2,1)}, u32[]{:S(2)}) copy-start(bf16[2,192,4096]{2,1,0:T(8,128)(2,1)} %param.11) | copy-start | bytes 9437188
Sparse Core Ops, SparseCore 0:
  547.0 33.7 reduce-scatter.1
where the time goes:
time: 597 us; the launch traced here: 588 us
  blocking collectives  237 us (40%)
  waiting for transfers between devices  210 us (35%)
  local copies, waits for them, and re-layouts  96.5 us (16%)
  matrix products  16.5 us (3%)
  between operations  13.7 us (2%)
  other arithmetic  7.8 us (1%)
    all_to_all x1, blocking collectives, body(): lax.all_to_all(buffer, 'expert', split_axis=0, concat_axis=0, tiled=True)  198 us
    all_to_all x1, waiting for transfers between devices, body(): lax.all_to_all(pieces, 'expert', split_axis=0, concat_axis=0, tiled=True)  177 us
    reduce_scatter x1, waiting for transfers between devices, body(): lax.psum_scatter(combined.astype(jnp.bfloat16), 'dp', scatter_dimension=0...  33.9 us
    reshape x2, local copies, waits for them, and re-layouts, body(): buffer.reshape(column_count, per_device, dp_count, capacity, model_width)  30.4 us
    all_to_all x1, local copies, waits for them, and re-layouts, body(): lax.all_to_all(pieces, 'expert', split_axis=0, concat_axis=0, tiled=True)  16.3 us
    all_gather x1, blocking collectives, body(): lax.all_gather(tokens, 'dp', axis=0, tiled=True)  14.4 us
    all_gather x1, blocking collectives, body(): shared_table = lax.all_gather(expert_ids, 'dp', axis=0, tiled=True)  13.6 us
    gather x1, local copies, waits for them, and re-layouts, body(): picked = values[jnp.minimum(target, total_slots - 1)].astype(jnp.float32)  13.2 us
  transfers between devices with their start and end apart: 2, of which 2 were waited for; matrix products, arithmetic and copies ran while one was open for 0% of the time, Pallas kernels for 0%

commit v1 on v0

v1 whole, which is shorter than its diff:
```python
import jax
import jax.numpy as jnp
from jax import lax
from jax.sharding import PartitionSpec as P


def slot_table(expert_ids, expert_count, capacity):
    rows, top_count = expert_ids.shape
    pairs = rows * top_count
    flat = expert_ids.reshape(pairs)
    earlier = jnp.arange(pairs)[None, :] < jnp.arange(pairs)[:, None]
    same = flat[:, None] == flat[None, :]
    ranked = jnp.sum((same & earlier).astype(jnp.int32), axis=1).reshape(rows, top_count)
    return jnp.where(ranked < capacity, expert_ids * capacity + ranked, -1)


def body(tokens, gate_values, expert_ids, gate_weight, up_weight, down_weight):
    dp_count = lax.axis_size("dp")
    column_count = lax.axis_size("expert")
    per_device = gate_weight.shape[0]
    expert_count = per_device * column_count
    token_rows, model_width = tokens.shape
    top_count = expert_ids.shape[1]
    capacity = max(2, (5 * token_rows * top_count + 4 * expert_count - 1) // (4 * expert_count))
    slots = expert_count * capacity

    slot = slot_table(expert_ids, expert_count, capacity)
    hit = slot[:, :, None] == jnp.arange(slots, dtype=jnp.int32)[None, None, :]
    chosen = jnp.sum(hit.astype(jnp.float32), axis=1).astype(jnp.bfloat16)
    weights = jnp.sum(
        jnp.where(hit, gate_values.astype(jnp.float32)[:, :, None], 0.0), axis=1
    ).astype(jnp.bfloat16)

    dispatch = jnp.einsum(
        "ts,td->sd", chosen, tokens, preferred_element_type=jnp.float32
    ).astype(jnp.bfloat16)
    dispatch = dispatch.reshape(column_count, per_device * capacity, model_width)
    arrived = lax.all_to_all(dispatch, "expert", split_axis=0, concat_axis=0, tiled=True)
    arrived = arrived.reshape(column_count, per_device, capacity, model_width)
    arrived = jnp.swapaxes(arrived, 0, 1).reshape(
        per_device, column_count * capacity, model_width
    )
    shared = lax.all_gather(arrived, "dp", axis=0, tiled=False)
    gate_act = jnp.einsum("glrd,lhd->glrh", shared, gate_weight, preferred_element_type=jnp.float32)
    up_act = jnp.einsum("glrd,lhd->glrh", shared, up_weight, preferred_element_type=jnp.float32)
    hidden = (jax.nn.silu(gate_act) * up_act).astype(jnp.bfloat16)
    pieces = jnp.einsum(
        "glrh,lhd->glrd", hidden, down_weight, preferred_element_type=jnp.float32
    ).astype(jnp.bfloat16)
    summed = lax.psum_scatter(
        pieces.reshape(dp_count * per_device * column_count * capacity, model_width),
        "dp",
        scatter_dimension=0,
        tiled=True,
    )
    summed = summed.reshape(per_device, column_count, capacity, model_width)
    summed = jnp.swapaxes(summed, 0, 1).reshape(
        column_count, per_device * capacity, model_width
    )
    returned = lax.all_to_all(summed, "expert", split_axis=0, concat_axis=0, tiled=True)
    rows_back = returned.reshape(slots, model_width)
    mixed_out = jnp.einsum("ts,sd->td", weights, rows_back, preferred_element_type=jnp.float32)
    return mixed_out.astype(jnp.bfloat16)


def solution(mesh):
    return jax.shard_map(
        body,
        mesh=mesh,
        in_specs=(
            P(("dp", "expert"), None),
            P(("dp", "expert"), None),
            P(("dp", "expert"), None),
            P("expert", "dp", None),
            P("expert", "dp", None),
            P("expert", "dp", None),
        ),
        out_specs=P(("dp", "expert"), None),
        check_vma=False,
    )
```

time: 597 us -> 251 us (0.42); the launches traced: 588 us -> 250 us
  blocking collectives: 237 us -> 77.3 us
  waiting for transfers between devices: 210 us -> 105 us
  local copies, waits for them, and re-layouts: 96.5 us -> 27.3 us
  matrix products: 16.5 us -> 25.8 us
  other arithmetic: 7.8 us -> 1.67 us
    all_to_all x1 -> x0, waiting for transfers between devices: 177 us -> none  [body(): lax.all_to_all(pieces, 'expert', split_axis=0, concat_axis=0, tiled=True)]
    all_to_all x1 -> x2, blocking collectives: 198 us -> 77.3 us  [the longest x1 39.8 us: body(): lax.all_to_all(dispatch, 'expert', split_axis=0, concat_axis=0, tiled=True)]
    all_gather x0 -> x1, waiting for transfers between devices: none -> 49.3 us  [body(): shared = lax.all_gather(arrived, 'dp', axis=0, tiled=False)]
    all_gather x3 -> x0, blocking collectives: 39.4 us -> none  [the longest x1 14.4 us: body(): lax.all_gather(tokens, 'dp', axis=0, tiled=True)]
    reshape x3 -> x8, local copies, waits for them, and re-layouts: 43.5 us -> 16.3 us  [the longest x2 6.65 us: body(): arrived = arrived.reshape(column_count, per_device, capacity, model_width)]
    reduce_scatter x1, waiting for transfers between devices: 33.9 us -> 55.4 us  [body(): lax.psum_scatter(pieces.reshape(dp_count * per_device * column_count * ca...]
    all_to_all x1 -> x0, local copies, waits for them, and re-layouts: 16.3 us -> none  [body(): lax.all_to_all(pieces, 'expert', split_axis=0, concat_axis=0, tiled=True)]
    gather x1 -> x0, local copies, waits for them, and re-layouts: 13.2 us -> none  [body(): picked = values[jnp.minimum(target, total_slots - 1)].astype(jnp.float32)]
where the time goes in v1:
time: 251 us; the launch traced here: 250 us
  waiting for transfers between devices  105 us (42%)
  blocking collectives  77.3 us (31%)
  local copies, waits for them, and re-layouts  27.3 us (11%)
  matrix products  25.8 us (10%)
  between operations  13.4 us (5%)
    reduce_scatter x1, waiting for transfers between devices, body(): lax.psum_scatter(pieces.reshape(dp_count * per_device * column_count * ca...  55.4 us
    all_gather x1, waiting for transfers between devices, body(): shared = lax.all_gather(arrived, 'dp', axis=0, tiled=False)  49.3 us
    all_to_all x1, blocking collectives, body(): lax.all_to_all(dispatch, 'expert', split_axis=0, concat_axis=0, tiled=True)  39.8 us
    all_to_all x1, blocking collectives, body(): lax.all_to_all(summed, 'expert', split_axis=0, concat_axis=0, tiled=True)  37.5 us
    dot_general x1, matrix products, body(): jnp.einsum('glrh,lhd->glrd', hidden, down_weight, preferred_element_type=...  13.7 us
    convert_element_type x1, local copies, waits for them, and re-layouts, body(): pieces = jnp.einsum('glrh,lhd->glrd', hidden, down_weight, preferred_elem...  7.71 us
    dot_general x1, matrix products, body(): jnp.einsum('glrd,lhd->glrh', shared, gate_weight, preferred_element_type=...  7.62 us
    reshape x2, local copies, waits for them, and re-layouts, body(): arrived = arrived.reshape(column_count, per_device, capacity, model_width)  6.65 us
  transfers between devices with their start and end apart: 2, of which 2 were waited for; matrix products, arithmetic and copies ran while one was open for 0% of the time, Pallas kernels for 0%

profile of v1, /device:TPU:2, one launch (start us, length us, event | category | flops | bytes accessed | tf_op | source)
XLA Modules:
  0.0 250.2 jit_solution(16339117137017267858)
XLA Ops:
  6.5 0.9 eq.28
  7.5 0.2 convert_reduce_fusion.1
  7.6 0.1 reshape.25
  7.7 0.7 add_select_fusion
  8.4 0.7 convert_element_type.31
  9.1 0.1 select_reduce_fusion
  9.2 2.3 convolution_convert_fusion
  11.6 2.3 reshape.26
  13.8 39.8 %all_to_all.10 = bf16[32,4,4096]{2,1,0:T(4,128)(2,1)} all-to-all(bf16[32,4,4096]{2,1,0:T(4,128)(2,1)} %reshape.26), channel_id=1, replica_groups=mesh['dp'=8,'expert'=32] {'expert'}, dimensions={0} | all-to-all | bytes 2097152 | tf_op jit(solution)/shard_map/all_to_all | solution.py:38
  53.6 3.4 %reshape.27 = bf16[32,2,2,4096]{3,2,1,0:T(2,128)(2,1)} reshape(bf16[32,4,4096]{2,1,0:T(4,128)(2,1)} %all_to_all.10) | data formatting | bytes 2097152 | tf_op jit(solution)/shard_map/reshape | solution.py:39
  57.0 3.3 %copy.27 = bf16[32,2,2,4096]{3,2,0,1:T(2,128)(2,1)} copy(bf16[32,2,2,4096]{3,2,1,0:T(2,128)(2,1)} %reshape.27) | data formatting | bytes 2097152 | tf_op jit(solution)/shard_map/reshape | solution.py:39
  60.2 2.3 all_gather_reshape.3
  62.6 0.0 reduce-scatter.2.cloned.1.call-start
  62.6 49.3 %all-gather.2.cloned.1.call-done = bf16[8,2,64,4096]{3,2,0,1:T(8,128)(2,1)} async-done(((bf16[1,2,64,4096]{3,2,0,1:T(8,128)(2,1)}), bf16[8,2,64,4096]{3,2,0,1:T(8,128)(2,1)}) %all-gather.2.cloned.1.call-update) | async-done | bytes 8388624 | tf_op jit(solution)/shard_map/all_gather | solution.py:43
  111.9 7.6 %fusion.5 = f32[8,2,64,192]{3,2,0,1:T(8,128)} fusion(bf16[8,2,64,4096]{3,2,0,1:T(8,128)(2,1)} %all-gather.2.cloned.1.call-done, bf16[2,192,4096]{2,1,0:T(8,128)(2,1)} %param.9), kind=kOutput, calls=%fused_computation.8 | convolution fusion | flops 1610612736 | bytes 12320768 | tf_op jit(solution)/shard_map/glrd,lhd->glrh/dot_general | solution.py:44
  119.6 13.7 %convert_bitcast_fusion = bf16[8,2,64,4096]{3,2,0,1:T(8,128)(2,1)} fusion(bf16[2,192,4096]{2,1,0:T(8,128)(2,1)S(1)} %copy-done, bf16[8,2,64,4096]{3,2,0,1:T(8,128)(2,1)} %all-gather.2.cloned.1.call-done, bf16[2,192,4096]{2,1,0:T(8,128)(2,1)} %param.10, f32[8,2,64,192]{3,2,0,1:T(8,128)} %fusion.5), kind=kOutput, calls=%fused_computation | convolution fusion | flops 3226599424 | bytes 23855104 | tf_op jit(solution)/shard_map/glrh,lhd->glrd/dot_general | solution.py:47
  133.3 7.7 %copy.20 = bf16[8,2,64,4096]{3,2,1,0:T(8,128)(2,1)} copy(bf16[8,2,64,4096]{3,2,0,1:T(8,128)(2,1)} %convert_bitcast_fusion) | data formatting | bytes 16777216 | tf_op jit(solution)/shard_map/convert_element_type | solution.py:49
  141.0 55.4 %reduce-scatter.2.cloned.1.call-done = bf16[128,4096]{1,0:T(8,128)(2,1)} async-done(((bf16[1024,4096]{1,0:T(8,128)(2,1)}), bf16[128,4096]{1,0:T(8,128)(2,1)}) %reduce-scatter.2.cloned.1.call-update) | async-done | bytes 1048592 | tf_op jit(solution)/shard_map/reduce_scatter | solution.py:50
  196.4 2.5 %reshape.29 = bf16[2,32,2,4096]{3,2,1,0:T(2,128)(2,1)} reshape(bf16[128,4096]{1,0:T(8,128)(2,1)} %reduce-scatter.2.cloned.1.call-done) | data formatting | bytes 2097152 | tf_op jit(solution)/shard_map/reshape | solution.py:56
  198.9 1.8 copy.21
  200.7 0.8 copy.22
  201.5 37.5 %all_to_all.11 = bf16[32,4,4096]{2,1,0:T(4,128)(2,1)} all-to-all(bf16[32,4,4096]{2,1,0:T(4,128)(2,1)S(1)} %copy.22), channel_id=1, replica_groups=mesh['dp'=8,'expert'=32] {'expert'}, dimensions={0} | all-to-all | bytes 2097152 | tf_op jit(solution)/shard_map/all_to_all | solution.py:60
  239.0 2.2 reshape.31
  241.2 2.1 convolution_convert_fusion.1
  (5 shorter events, 0.0 us)
Async XLA Ops:
  6.5 113.0 %copy-start = (bf16[2,192,4096]{2,1,0:T(8,128)(2,1)S(1)}, bf16[2,192,4096]{2,1,0:T(8,128)(2,1)}, u32[]{:S(2)}) copy-start(bf16[2,192,4096]{2,1,0:T(8,128)(2,1)} %param.11) | copy-start | bytes 9437188
  6.5 105.4 %all-gather.2.cloned.1.call-start = ((), (), s32[]{:S(2)}) async-start(), calls=%async_computation.3 | async-start | bytes 9437184 | tf_op jit(solution)/shard_map/all_gather | solution.py:43
  62.6 133.8 %reduce-scatter.2.cloned.1.call-start = ((), (), s32[]{:S(2)}) async-start(), calls=%async_computation.4 | async-start | bytes 9437184 | tf_op jit(solution)/shard_map/reduce_scatter | solution.py:50
Sparse Core Ops, SparseCore 0:
  62.7 49.1 all-gather.1
  141.1 55.1 reduce-scatter.1

commit v2 on v1

v2 whole, which is shorter than its diff:
```python
import functools

import jax
import jax.numpy as jnp
from jax import lax
from jax.experimental import pallas as pl
from jax.experimental.pallas import tpu as pltpu
from jax.sharding import PartitionSpec as P


def slot_table(expert_ids, capacity):
    rows, top_count = expert_ids.shape
    pairs = rows * top_count
    flat = expert_ids.reshape(pairs)
    earlier = jnp.arange(pairs)[None, :] < jnp.arange(pairs)[:, None]
    same = flat[:, None] == flat[None, :]
    ranked = jnp.sum((same & earlier).astype(jnp.int32), axis=1).reshape(rows, top_count)
    return jnp.where(ranked < capacity, expert_ids * capacity + ranked, -1)


def expert_kernel(count, *refs):
    pieces, (gate_ref, up_ref, down_ref), outs = refs[:count], refs[count : count + 3], refs[count + 3 :]
    rows = jnp.concatenate([ref[...] for ref in pieces], axis=0)
    transposed = (((1,), (1,)), ((), ()))
    gate_act = lax.dot_general(rows, gate_ref[0], transposed, preferred_element_type=jnp.float32)
    up_act = lax.dot_general(rows, up_ref[0], transposed, preferred_element_type=jnp.float32)
    hidden = (gate_act / (1.0 + jnp.exp(-gate_act)) * up_act).astype(jnp.bfloat16)
    out = jnp.dot(hidden, down_ref[0], preferred_element_type=jnp.float32).astype(jnp.bfloat16)
    height = out.shape[0] // len(outs)
    for i, ref in enumerate(outs):
        ref[...] = out[i * height : (i + 1) * height]


def expert_rows(pieces, index, gate_weight, up_weight, down_weight):
    height, width = pieces[0].shape
    hidden = gate_weight.shape[1]
    count = len(pieces)
    weight = pl.BlockSpec((1, hidden, width), lambda i: (index, 0, 0))
    half = (count // 2 * height, width)
    return pl.pallas_call(
        functools.partial(expert_kernel, count),
        grid=(1,),
        in_specs=[pl.BlockSpec((height, width), lambda i: (0, 0))] * count + [weight] * 3,
        out_specs=[pl.BlockSpec(half, lambda i: (0, 0))] * 2,
        out_shape=[jax.ShapeDtypeStruct(half, jnp.bfloat16)] * 2,
        compiler_params=pltpu.CompilerParams(vmem_limit_bytes=56 * 1024 * 1024),
    )(*pieces, gate_weight, up_weight, down_weight)


def body(tokens, gate_values, expert_ids, gate_weight, up_weight, down_weight):
    dp_count = lax.axis_size("dp")
    ring = dp_count // 2
    column_count = lax.axis_size("expert")
    per_device = gate_weight.shape[0]
    expert_count = per_device * column_count
    token_rows, model_width = tokens.shape
    top_count = expert_ids.shape[1]
    capacity = max(2, (5 * token_rows * top_count + 4 * expert_count - 1) // (4 * expert_count))
    chunk_rows = column_count * capacity

    def along_ring(value, step):
        return lax.ppermute(
            value,
            "dp",
            [(2 * y + c, 2 * ((y + step) % ring) + c) for y in range(ring) for c in range(2)],
        )

    def across(value):
        return lax.ppermute(
            value, "dp", [(2 * y + c, 2 * y + 1 - c) for y in range(ring) for c in range(2)]
        )

    slot = slot_table(expert_ids, capacity)
    hit = slot[:, :, None] == jnp.arange(expert_count * capacity, dtype=jnp.int32)[None, None, :]
    chosen = jnp.sum(hit.astype(jnp.float32), axis=1).astype(jnp.bfloat16)
    weights = jnp.sum(
        jnp.where(hit, gate_values.astype(jnp.float32)[:, :, None], 0.0), axis=1
    ).astype(jnp.bfloat16)
    chosen = chosen.reshape(token_rows, column_count, per_device, capacity)
    weights = weights.reshape(token_rows, column_count, per_device, capacity)

    arrived = []
    for index in range(per_device):
        sent = jnp.einsum(
            "tcr,td->crd", chosen[:, :, index], tokens, preferred_element_type=jnp.float32
        ).astype(jnp.bfloat16)
        arrived.append(lax.all_to_all(sent, "expert", split_axis=0, concat_axis=0, tiled=True))

    sums = []
    for index in range(per_device):
        own = arrived[index].reshape(chunk_rows, model_width)
        near = [own] + [along_ring(own, -step) for step in range(1, ring)]
        far = [across(piece) for piece in near]
        kept, other = expert_rows(near + far, index, gate_weight, up_weight, down_weight)
        paired = across(other)
        pair = [
            (
                kept[k * chunk_rows : (k + 1) * chunk_rows].astype(jnp.float32)
                + paired[k * chunk_rows : (k + 1) * chunk_rows].astype(jnp.float32)
            ).astype(jnp.bfloat16)
            for k in range(ring)
        ]
        total = pair[0].astype(jnp.float32)
        for step in range(1, ring):
            total = total + along_ring(pair[step], step).astype(jnp.float32)
        sums.append(total.astype(jnp.bfloat16).reshape(column_count, capacity, model_width))

    mixed_out = jnp.zeros((token_rows, model_width), jnp.float32)
    for index in range(per_device):
        back = lax.all_to_all(sums[index], "expert", split_axis=0, concat_axis=0, tiled=True)
        mixed_out = mixed_out + jnp.einsum(
            "tcr,crd->td", weights[:, :, index], back, preferred_element_type=jnp.float32
        )
    return mixed_out.astype(jnp.bfloat16)


def solution(mesh):
    return jax.shard_map(
        body,
        mesh=mesh,
        in_specs=(
            P(("dp", "expert"), None),
            P(("dp", "expert"), None),
            P(("dp", "expert"), None),
            P("expert", "dp", None),
            P("expert", "dp", None),
            P("expert", "dp", None),
        ),
        out_specs=P(("dp", "expert"), None),
        check_vma=False,
    )
```

time: 251 us -> 190 us (0.76)
  blocking collectives: 77.3 us -> 0 us
  starting transfers between devices: 0.04 us -> 48.5 us
  matrix products: 25.8 us -> 2.1 us
  local copies, waits for them, and re-layouts: 27.3 us -> 7.02 us
  Pallas kernels: 0 us -> 18 us
  between operations: 13.4 us -> 0.24 us
  other arithmetic: 1.67 us -> 6.08 us
    all_to_all x2 -> x0, blocking collectives: 77.3 us -> none  [the longest x1 39.8 us: body(): lax.all_to_all(dispatch, 'expert', split_axis=0, concat_axis=0, tiled=True)]
    ppermute x0 -> x22, waiting for transfers between devices: none -> 71.7 us  [the longest x12 68.6 us: along_ring(): lax.ppermute(value, 'dp', [(2 * y + c, 2 * ((y + step) % ring) + c) for y...]
    reduce_scatter x1 -> x0, waiting for transfers between devices: 55.4 us -> none  [body(): lax.psum_scatter(pieces.reshape(dp_count * per_device * column_count * ca...]
    all_gather x1 -> x0, waiting for transfers between devices: 49.3 us -> none  [body(): shared = lax.all_gather(arrived, 'dp', axis=0, tiled=False)]
    all_to_all x0 -> x4, waiting for transfers between devices: none -> 35.2 us  [the longest x2 18.5 us: body(): lax.all_to_all(sums[index], 'expert', split_axis=0, concat_axis=0, tiled=...]
    all_to_all x0 -> x4, starting transfers between devices: none -> 34.2 us  [the longest x2 17.2 us: body(): lax.all_to_all(sent, 'expert', split_axis=0, concat_axis=0, tiled=True)]
    dot_general x4, matrix products: 25.8 us -> 2.1 us  [the longest x2 1.43 us: body(): jnp.einsum('tcr,crd->td', weights[:, :, index], back, preferred_element_t...]
    pallas_call x0 -> x2, Pallas kernels: none -> 18 us  [expert_rows(): pl.pallas_call(functools.partial(expert_kernel, count), grid=(1,), in_spe...]
  transfers between devices with their start and end apart: 2 -> 26, of which waited for: 2 -> 15; matrix products, arithmetic and copies ran while one was open for 0% -> 5% of each run, Pallas kernels for 0% -> 10%
where the time goes in v2:
time: 190 us; the launch traced here: 189 us
  waiting for transfers between devices  107 us (56%)
  starting transfers between devices  48.5 us (26%)
  Pallas kernels  18 us (9%)
  local copies, waits for them, and re-layouts  7.02 us (4%)
  other arithmetic  6.08 us (3%)
  matrix products  2.1 us (1%)
    ppermute x12, waiting for transfers between devices, along_ring(): lax.ppermute(value, 'dp', [(2 * y + c, 2 * ((y + step) % ring) + c) for y...  68.6 us
    all_to_all x2, waiting for transfers between devices, body(): lax.all_to_all(sums[index], 'expert', split_axis=0, concat_axis=0, tiled=...  18.5 us
    pallas_call x2, Pallas kernels, expert_rows(): pl.pallas_call(functools.partial(expert_kernel, count), grid=(1,), in_spe...  18 us
    all_to_all x2, starting transfers between devices, body(): lax.all_to_all(sent, 'expert', split_axis=0, concat_axis=0, tiled=True)  17.2 us
    all_to_all x2, starting transfers between devices, body(): lax.all_to_all(sums[index], 'expert', split_axis=0, concat_axis=0, tiled=...  17 us
    all_to_all x2, waiting for transfers between devices, body(): lax.all_to_all(sent, 'expert', split_axis=0, concat_axis=0, tiled=True)  16.8 us
    ppermute x12, starting transfers between devices, along_ring(): lax.ppermute(value, 'dp', [(2 * y + c, 2 * ((y + step) % ring) + c) for y...  13.6 us
  transfers between devices with their start and end apart: 26, of which 15 were waited for; matrix products, arithmetic and copies ran while one was open for 5% of the time, Pallas kernels for 10%

profile of v2, /device:TPU:2, one launch (start us, length us, event | category | flops | bytes accessed | tf_op | source)
XLA Modules:
  0.0 188.8 jit_solution(17042412452220365711)
XLA Ops:
  4.5 11.6 %all-to-all-start = ((bf16[32,2,4096]{2,1,0:T(2,128)(2,1)}), bf16[32,2,4096]{2,1,0:T(2,128)(2,1)S(1)}, u32[]{:S(2)}, u32[]{:S(2)}) async-start(bf16[32,2,4096]{2,1,0:T(2,128)(2,1)} %copy.31), calls=%async_computation | async-start | bytes 1048576 | tf_op jit(solution)/shard_map/all_to_all | solution.py:87
  16.2 16.7 %all-to-all-done = bf16[32,2,4096]{2,1,0:T(2,128)(2,1)S(1)} async-done(((bf16[32,2,4096]{2,1,0:T(2,128)(2,1)}), bf16[32,2,4096]{2,1,0:T(2,128)(2,1)S(1)}, u32[]{:S(2)}, u32[]{:S(2)}) %all-to-all-start) | async-done | bytes 524320 | tf_op jit(solution)/shard_map/all_to_all | solution.py:87
  33.1 3.1 %collective-permute-start = (bf16[64,4096]{1,0:T(8,128)(2,1)S(1)}, bf16[64,4096]{1,0:T(8,128)(2,1)S(1)}, u32[]{:S(2)}, u32[]{:S(2)}) collective-permute-start(bf16[64,4096]{1,0:T(8,128)(2,1)S(1)} %reshape.26.refs_0_), channel_id=1, source_target_pairs={{0,192},{32,224},{64,0},{96,32},{128,64},{160,96},{192,128},{224,1... | collective-permute-start | bytes 1572872 | tf_op jit(solution)/shard_map/ppermute | solution.py:62
  37.9 5.6 %all-to-all-start.2 = ((bf16[32,2,4096]{2,1,0:T(2,128)(2,1)}), bf16[32,2,4096]{2,1,0:T(2,128)(2,1)S(1)}, u32[]{:S(2)}, u32[]{:S(2)}) async-start(bf16[32,2,4096]{2,1,0:T(2,128)(2,1)} %copy.35), calls=%async_computation.2 | async-start | bytes 1048576 | tf_op jit(solution)/shard_map/all_to_all | solution.py:87
  45.1 12.2 %collective-permute-done.refs_1_ = bf16[64,4096]{1,0:T(8,128)(2,1)S(1)} collective-permute-done((bf16[64,4096]{1,0:T(8,128)(2,1)S(1)}, bf16[64,4096]{1,0:T(8,128)(2,1)S(1)}, u32[]{:S(2)}, u32[]{:S(2)}) %collective-permute-start) | collective-permute-done | bytes 524320 | tf_op jit(solution)/shard_map/ppermute | solution.py:62
  57.4 2.5 %collective-permute-done.1.refs_2_ = bf16[64,4096]{1,0:T(8,128)(2,1)S(1)} collective-permute-done((bf16[64,4096]{1,0:T(8,128)(2,1)S(1)}, bf16[64,4096]{1,0:T(8,128)(2,1)S(1)}, u32[]{:S(2)}, u32[]{:S(2)}) %collective-permute-start.1) | collective-permute-done | bytes 524320 | tf_op jit(solution)/shard_map/ppermute | solution.py:62
  59.9 8.4 %collective-permute-done.2.refs_3_ = bf16[64,4096]{1,0:T(8,128)(2,1)} collective-permute-done((bf16[64,4096]{1,0:T(8,128)(2,1)S(1)}, bf16[64,4096]{1,0:T(8,128)(2,1)}, u32[]{:S(2)}, u32[]{:S(2)}) %collective-permute-start.2) | collective-permute-done | bytes 524320 | tf_op jit(solution)/shard_map/ppermute | solution.py:62
  71.5 9.0 %shard_map.64 = (bf16[256,4096]{1,0:T(8,128)(2,1)}, bf16[256,4096]{1,0:T(8,128)(2,1)}) custom-call(bf16[64,4096]{1,0:T(8,128)(2,1)} %copy-done.4, bf16[64,4096]{1,0:T(8,128)(2,1)} %copy-done.6, bf16[64,4096]{1,0:T(8,128)(2,1)} %copy-done.9, bf16[64,4096]{1,0:T(8,128)(2,1)} %collective-permute-done.2.refs_3_, bf16[64,4096]{1,0:T(8,128)(2,1)} %copy-done.11, ...), custom_call_target="tpu_custom_call" | custom-call | tf_op jit(solution)/shard_map/pallas_call | solution.py:40
  81.0 2.4 %collective-permute-done.11.refs_1_ = bf16[64,4096]{1,0:T(8,128)(2,1)S(1)} collective-permute-done((bf16[64,4096]{1,0:T(8,128)(2,1)S(1)}, bf16[64,4096]{1,0:T(8,128)(2,1)S(1)}, u32[]{:S(2)}, u32[]{:S(2)}) %collective-permute-start.11) | collective-permute-done | bytes 524320 | tf_op jit(solution)/shard_map/ppermute | solution.py:62
  83.3 2.2 %collective-permute-done.12.refs_2_ = bf16[64,4096]{1,0:T(8,128)(2,1)S(1)} collective-permute-done((bf16[64,4096]{1,0:T(8,128)(2,1)S(1)}, bf16[64,4096]{1,0:T(8,128)(2,1)S(1)}, u32[]{:S(2)}, u32[]{:S(2)}) %collective-permute-start.12) | collective-permute-done | bytes 524320 | tf_op jit(solution)/shard_map/ppermute | solution.py:62
  85.5 10.5 %collective-permute-done.13.refs_3_ = bf16[64,4096]{1,0:T(8,128)(2,1)S(1)} collective-permute-done((bf16[64,4096]{1,0:T(8,128)(2,1)S(1)}, bf16[64,4096]{1,0:T(8,128)(2,1)S(1)}, u32[]{:S(2)}, u32[]{:S(2)}) %collective-permute-start.13) | collective-permute-done | bytes 524320 | tf_op jit(solution)/shard_map/ppermute | solution.py:62
  96.1 2.0 %collective-permute-done.17.refs_7_ = bf16[64,4096]{1,0:T(8,128)(2,1)} collective-permute-done((bf16[64,4096]{1,0:T(8,128)(2,1)S(1)}, bf16[64,4096]{1,0:T(8,128)(2,1)}, u32[]{:S(2)}, u32[]{:S(2)}) %collective-permute-start.17) | collective-permute-done | bytes 524320 | tf_op jit(solution)/shard_map/ppermute | solution.py:69
  98.1 9.0 %shard_map.65 = (bf16[256,4096]{1,0:T(8,128)(2,1)}, bf16[256,4096]{1,0:T(8,128)(2,1)}) custom-call(bf16[64,4096]{1,0:T(8,128)(2,1)} %copy-done.5, bf16[64,4096]{1,0:T(8,128)(2,1)} %copy-done.7, bf16[64,4096]{1,0:T(8,128)(2,1)} %copy-done.8, bf16[64,4096]{1,0:T(8,128)(2,1)} %copy-done.10, bf16[64,4096]{1,0:T(8,128)(2,1)} %copy-done.12, ...), custom_call_target="tpu_custom_call" | custom-call | tf_op jit(solution)/shard_map/pallas_call | solution.py:40
  107.7 1.7 collective-permute-start.10
  111.5 1.7 add_convert_fusion.3
  114.7 1.9 %collective-permute-start.20 = (bf16[64,4096]{1,0:T(8,128)(2,1)}, bf16[64,4096]{1,0:T(8,128)(2,1)}, u32[]{:S(2)}, u32[]{:S(2)}) collective-permute-start(bf16[64,4096]{1,0:T(8,128)(2,1)} %get-tuple-element.17), channel_id=1, source_target_pairs={{0,128},{32,160},{64,192},{96,224},{128,0},{160,32},{192,64},{224,... | collective-permute-start | bytes 1572872 | tf_op jit(solution)/shard_map/ppermute | solution.py:62
  116.6 15.8 %collective-permute-done.10 = bf16[64,4096]{1,0:T(8,128)(2,1)S(1)} collective-permute-done((bf16[64,4096]{1,0:T(8,128)(2,1)S(1)}, bf16[64,4096]{1,0:T(8,128)(2,1)S(1)}, u32[]{:S(2)}, u32[]{:S(2)}) %collective-permute-start.10) | collective-permute-done | bytes 524320 | tf_op jit(solution)/shard_map/ppermute | solution.py:62
  132.5 4.5 %collective-permute-done.8 = bf16[64,4096]{1,0:T(8,128)(2,1)S(1)} collective-permute-done((bf16[64,4096]{1,0:T(8,128)(2,1)S(1)}, bf16[64,4096]{1,0:T(8,128)(2,1)S(1)}, u32[]{:S(2)}, u32[]{:S(2)}) %collective-permute-start.8) | collective-permute-done | bytes 524320 | tf_op jit(solution)/shard_map/ppermute | solution.py:62
  138.5 9.8 %all-to-all-start.1 = ((bf16[32,2,4096]{2,1,0:T(2,128)(2,1)}), bf16[32,2,4096]{2,1,0:T(2,128)(2,1)S(1)}, u32[]{:S(2)}, u32[]{:S(2)}) async-start(bf16[32,2,4096]{2,1,0:T(2,128)(2,1)} %reshape.27), calls=%async_computation.1 | async-start | bytes 1048576 | tf_op jit(solution)/shard_map/all_to_all | solution.py:110
  148.4 10.0 %collective-permute-done.19 = bf16[64,4096]{1,0:T(8,128)(2,1)} collective-permute-done((bf16[64,4096]{1,0:T(8,128)(2,1)S(1)}, bf16[64,4096]{1,0:T(8,128)(2,1)}, u32[]{:S(2)}, u32[]{:S(2)}) %collective-permute-start.19) | collective-permute-done | bytes 524320 | tf_op jit(solution)/shard_map/ppermute | solution.py:62
  158.4 1.9 %add_convert_fusion = bf16[64,4096]{1,0:T(8,128)(2,1)S(1)} fusion(bf16[64,4096]{1,0:T(8,128)(2,1)} %collective-permute-done.21, bf16[64,4096]{1,0:T(8,128)(2,1)} %collective-permute-done.20, bf16[64,4096]{1,0:T(8,128)(2,1)} %collective-permute-done.19, bf16[256,4096]{1,0:T(8,128)(2,1)} %copy-done.3, bf16[256,4096]{1,0:T(8,128)(2,1)S(1)} %copy-done.2), kind=kLoop, calls=%fused_computation.6 | loop fusion | flops 3145728 | bytes 3145728 | tf_op jit(solution)/shard_map/convert_element_type | solution.py:106
  161.4 2.6 %all-to-all-done.1 = bf16[32,2,4096]{2,1,0:T(2,128)(2,1)S(1)} async-done(((bf16[32,2,4096]{2,1,0:T(2,128)(2,1)}), bf16[32,2,4096]{2,1,0:T(2,128)(2,1)S(1)}, u32[]{:S(2)}, u32[]{:S(2)}) %all-to-all-start.1) | async-done | bytes 524320 | tf_op jit(solution)/shard_map/all_to_all | solution.py:110
  163.9 7.2 %all-to-all-start.3 = ((bf16[32,2,4096]{2,1,0:T(2,128)(2,1)}), bf16[32,2,4096]{2,1,0:T(2,128)(2,1)S(1)}, u32[]{:S(2)}, u32[]{:S(2)}) async-start(bf16[32,2,4096]{2,1,0:T(2,128)(2,1)} %reshape.29), calls=%async_computation.3 | async-start | bytes 1048576 | tf_op jit(solution)/shard_map/all_to_all | solution.py:110
  171.9 15.9 %all-to-all-done.3 = bf16[32,2,4096]{2,1,0:T(2,128)(2,1)S(1)} async-done(((bf16[32,2,4096]{2,1,0:T(2,128)(2,1)}), bf16[32,2,4096]{2,1,0:T(2,128)(2,1)S(1)}, u32[]{:S(2)}, u32[]{:S(2)}) %all-to-all-start.3) | async-done | bytes 524320 | tf_op jit(solution)/shard_map/all_to_all | solution.py:110
  (88 shorter events, 20.5 us)
Async XLA Ops:
  4.5 28.5 %all-to-all-start = ((bf16[32,2,4096]{2,1,0:T(2,128)(2,1)}), bf16[32,2,4096]{2,1,0:T(2,128)(2,1)S(1)}, u32[]{:S(2)}, u32[]{:S(2)}) async-start(bf16[32,2,4096]{2,1,0:T(2,128)(2,1)} %copy.31), calls=%async_computation | async-start | bytes 1048576 | tf_op jit(solution)/shard_map/all_to_all | solution.py:87
  33.1 24.2 %collective-permute-start = (bf16[64,4096]{1,0:T(8,128)(2,1)S(1)}, bf16[64,4096]{1,0:T(8,128)(2,1)S(1)}, u32[]{:S(2)}, u32[]{:S(2)}) collective-permute-start(bf16[64,4096]{1,0:T(8,128)(2,1)S(1)} %reshape.26.refs_0_), channel_id=1, source_target_pairs={{0,192},{32,224},{64,0},{96,32},{128,64},{160,96},{192,128},{224,1... | collective-permute-start | bytes 1572872 | tf_op jit(solution)/shard_map/ppermute | solution.py:62
  37.9 30.4 %all-to-all-start.2 = ((bf16[32,2,4096]{2,1,0:T(2,128)(2,1)}), bf16[32,2,4096]{2,1,0:T(2,128)(2,1)S(1)}, u32[]{:S(2)}, u32[]{:S(2)}) async-start(bf16[32,2,4096]{2,1,0:T(2,128)(2,1)} %copy.35), calls=%async_computation.2 | async-start | bytes 1048576 | tf_op jit(solution)/shard_map/all_to_all | solution.py:87
  43.5 16.5 %collective-permute-start.1 = (bf16[64,4096]{1,0:T(8,128)(2,1)S(1)}, bf16[64,4096]{1,0:T(8,128)(2,1)S(1)}, u32[]{:S(2)}, u32[]{:S(2)}) collective-permute-start(bf16[64,4096]{1,0:T(8,128)(2,1)S(1)} %reshape.26.refs_0_), channel_id=1, source_target_pairs={{0,128},{32,160},{64,192},{96,224},{128,0},{160,32},{192,64},{224,... | collective-permute-start | bytes 1572872 | tf_op jit(solution)/shard_map/ppermute | solution.py:62
  44.2 24.1 %collective-permute-start.2 = (bf16[64,4096]{1,0:T(8,128)(2,1)S(1)}, bf16[64,4096]{1,0:T(8,128)(2,1)}, u32[]{:S(2)}, u32[]{:S(2)}) collective-permute-start(bf16[64,4096]{1,0:T(8,128)(2,1)S(1)} %reshape.26.refs_0_), channel_id=1, source_target_pairs={{0,64},{32,96},{64,128},{96,160},{128,192},{160,224},{192,0},{224,... | collective-permute-start | bytes 1572872 | tf_op jit(solution)/shard_map/ppermute | solution.py:62
  45.1 24.1 %collective-permute-start.3 = (bf16[64,4096]{1,0:T(8,128)(2,1)S(1)}, bf16[64,4096]{1,0:T(8,128)(2,1)S(1)}, u32[]{:S(2)}, u32[]{:S(2)}) collective-permute-start(bf16[64,4096]{1,0:T(8,128)(2,1)S(1)} %reshape.26.refs_0_), channel_id=1, source_target_pairs={{0,32},{32,0},{64,96},{96,64},{128,160},{160,128},{192,224},{224,1... | collective-permute-start | bytes 1572872 | tf_op jit(solution)/shard_map/ppermute | solution.py:69
  57.4 12.7 %collective-permute-start.4 = (bf16[64,4096]{1,0:T(8,128)(2,1)S(1)}, bf16[64,4096]{1,0:T(8,128)(2,1)}, u32[]{:S(2)}, u32[]{:S(2)}) collective-permute-start(bf16[64,4096]{1,0:T(8,128)(2,1)S(1)} %collective-permute-done.refs_1_), channel_id=1, source_target_pairs={{0,32},{32,0},{64,96},{96,64},{128,160},{160,128},{192,224},{224,1... | collective-permute-start | bytes 1572872 | tf_op jit(solution)/shard_map/ppermute | solution.py:69
  59.9 11.6 %collective-permute-start.5 = (bf16[64,4096]{1,0:T(8,128)(2,1)S(1)}, bf16[64,4096]{1,0:T(8,128)(2,1)}, u32[]{:S(2)}, u32[]{:S(2)}) collective-permute-start(bf16[64,4096]{1,0:T(8,128)(2,1)S(1)} %collective-permute-done.1.refs_2_), channel_id=1, source_target_pairs={{0,32},{32,0},{64,96},{96,64},{128,160},{160,128},{192,224},{224,1... | collective-permute-start | bytes 1572872 | tf_op jit(solution)/shard_map/ppermute | solution.py:69
  68.5 14.8 %collective-permute-start.11 = (bf16[64,4096]{1,0:T(8,128)(2,1)S(1)}, bf16[64,4096]{1,0:T(8,128)(2,1)S(1)}, u32[]{:S(2)}, u32[]{:S(2)}) collective-permute-start(bf16[64,4096]{1,0:T(8,128)(2,1)S(1)} %reshape.28.refs_0_), channel_id=1, source_target_pairs={{0,192},{32,224},{64,0},{96,32},{128,64},{160,96},{192,128},{224,1... | collective-permute-start | bytes 1572872 | tf_op jit(solution)/shard_map/ppermute | solution.py:62
  69.2 16.3 %collective-permute-start.12 = (bf16[64,4096]{1,0:T(8,128)(2,1)S(1)}, bf16[64,4096]{1,0:T(8,128)(2,1)S(1)}, u32[]{:S(2)}, u32[]{:S(2)}) collective-permute-start(bf16[64,4096]{1,0:T(8,128)(2,1)S(1)} %reshape.28.refs_0_), channel_id=1, source_target_pairs={{0,128},{32,160},{64,192},{96,224},{128,0},{160,32},{192,64},{224,... | collective-permute-start | bytes 1572872 | tf_op jit(solution)/shard_map/ppermute | solution.py:62
  70.0 26.0 %collective-permute-start.13 = (bf16[64,4096]{1,0:T(8,128)(2,1)S(1)}, bf16[64,4096]{1,0:T(8,128)(2,1)S(1)}, u32[]{:S(2)}, u32[]{:S(2)}) collective-permute-start(bf16[64,4096]{1,0:T(8,128)(2,1)S(1)} %reshape.28.refs_0_), channel_id=1, source_target_pairs={{0,64},{32,96},{64,128},{96,160},{128,192},{160,224},{192,0},{224,... | collective-permute-start | bytes 1572872 | tf_op jit(solution)/shard_map/ppermute | solution.py:62
  80.5 26.8 %collective-permute-start.7 = (bf16[256,4096]{1,0:T(8,128)(2,1)}, bf16[256,4096]{1,0:T(8,128)(2,1)S(1)}, u32[]{:S(2)}, u32[]{:S(2)}) collective-permute-start(bf16[256,4096]{1,0:T(8,128)(2,1)} %get-tuple-element.10), channel_id=1, source_target_pairs={{0,32},{32,0},{64,96},{96,64},{128,160},{160,128},{192,224},{224,1... | collective-permute-start | bytes 6291464 | tf_op jit(solution)/shard_map/ppermute | solution.py:69
  80.5 15.6 %collective-permute-start.14 = (bf16[64,4096]{1,0:T(8,128)(2,1)S(1)}, bf16[64,4096]{1,0:T(8,128)(2,1)S(1)}, u32[]{:S(2)}, u32[]{:S(2)}) collective-permute-start(bf16[64,4096]{1,0:T(8,128)(2,1)S(1)} %reshape.28.refs_0_), channel_id=1, source_target_pairs={{0,32},{32,0},{64,96},{96,64},{128,160},{160,128},{192,224},{224,1... | collective-permute-start | bytes 1572872 | tf_op jit(solution)/shard_map/ppermute | solution.py:69
  83.3 12.7 %collective-permute-start.15 = (bf16[64,4096]{1,0:T(8,128)(2,1)S(1)}, bf16[64,4096]{1,0:T(8,128)(2,1)S(1)}, u32[]{:S(2)}, u32[]{:S(2)}) collective-permute-start(bf16[64,4096]{1,0:T(8,128)(2,1)S(1)} %collective-permute-done.11.refs_1_), channel_id=1, source_target_pairs={{0,32},{32,0},{64,96},{96,64},{128,160},{160,128},{192,224},{224,1... | collective-permute-start | bytes 1572872 | tf_op jit(solution)/shard_map/ppermute | solution.py:69
  85.5 10.6 %collective-permute-start.16 = (bf16[64,4096]{1,0:T(8,128)(2,1)S(1)}, bf16[64,4096]{1,0:T(8,128)(2,1)S(1)}, u32[]{:S(2)}, u32[]{:S(2)}) collective-permute-start(bf16[64,4096]{1,0:T(8,128)(2,1)S(1)} %collective-permute-done.12.refs_2_), channel_id=1, source_target_pairs={{0,32},{32,0},{64,96},{96,64},{128,160},{160,128},{192,224},{224,1... | collective-permute-start | bytes 1572872 | tf_op jit(solution)/shard_map/ppermute | solution.py:69
  107.1 4.4 %collective-permute-start.18 = (bf16[256,4096]{1,0:T(8,128)(2,1)}, bf16[256,4096]{1,0:T(8,128)(2,1)S(1)}, u32[]{:S(2)}, u32[]{:S(2)}) collective-permute-start(bf16[256,4096]{1,0:T(8,128)(2,1)} %get-tuple-element.12), channel_id=1, source_target_pairs={{0,32},{32,0},{64,96},{96,64},{128,160},{160,128},{192,224},{224,1... | collective-permute-start | bytes 6291464 | tf_op jit(solution)/shard_map/ppermute | solution.py:69
  107.7 24.8 %collective-permute-start.10 = (bf16[64,4096]{1,0:T(8,128)(2,1)S(1)}, bf16[64,4096]{1,0:T(8,128)(2,1)S(1)}, u32[]{:S(2)}, u32[]{:S(2)}) collective-permute-start(bf16[64,4096]{1,0:T(8,128)(2,1)S(1)} %get-tuple-element.19), channel_id=1, source_target_pairs={{0,192},{32,224},{64,0},{96,32},{128,64},{160,96},{192,128},{224,1... | collective-permute-start | bytes 1572872 | tf_op jit(solution)/shard_map/ppermute | solution.py:62
  109.4 23.1 %collective-permute-start.9 = (bf16[64,4096]{1,0:T(8,128)(2,1)S(1)}, bf16[64,4096]{1,0:T(8,128)(2,1)S(1)}, u32[]{:S(2)}, u32[]{:S(2)}) collective-permute-start(bf16[64,4096]{1,0:T(8,128)(2,1)S(1)} %get-tuple-element.20), channel_id=1, source_target_pairs={{0,128},{32,160},{64,192},{96,224},{128,0},{160,32},{192,64},{224,... | collective-permute-start | bytes 1572872 | tf_op jit(solution)/shard_map/ppermute | solution.py:62
  109.4 27.6 %collective-permute-start.8 = (bf16[64,4096]{1,0:T(8,128)(2,1)S(1)}, bf16[64,4096]{1,0:T(8,128)(2,1)S(1)}, u32[]{:S(2)}, u32[]{:S(2)}) collective-permute-start(bf16[64,4096]{1,0:T(8,128)(2,1)S(1)} %get-tuple-element.18), channel_id=1, source_target_pairs={{0,64},{32,96},{64,128},{96,160},{128,192},{160,224},{192,0},{224,... | collective-permute-start | bytes 1572872 | tf_op jit(solution)/shard_map/ppermute | solution.py:62
  113.1 35.2 %collective-permute-start.21 = (bf16[64,4096]{1,0:T(8,128)(2,1)}, bf16[64,4096]{1,0:T(8,128)(2,1)}, u32[]{:S(2)}, u32[]{:S(2)}) collective-permute-start(bf16[64,4096]{1,0:T(8,128)(2,1)} %get-tuple-element.16), channel_id=1, source_target_pairs={{0,192},{32,224},{64,0},{96,32},{128,64},{160,96},{192,128},{224,1... | collective-permute-start | bytes 1572872 | tf_op jit(solution)/shard_map/ppermute | solution.py:62
  114.7 33.6 %collective-permute-start.20 = (bf16[64,4096]{1,0:T(8,128)(2,1)}, bf16[64,4096]{1,0:T(8,128)(2,1)}, u32[]{:S(2)}, u32[]{:S(2)}) collective-permute-start(bf16[64,4096]{1,0:T(8,128)(2,1)} %get-tuple-element.17), channel_id=1, source_target_pairs={{0,128},{32,160},{64,192},{96,224},{128,0},{160,32},{192,64},{224,... | collective-permute-start | bytes 1572872 | tf_op jit(solution)/shard_map/ppermute | solution.py:62
  132.5 25.9 %collective-permute-start.19 = (bf16[64,4096]{1,0:T(8,128)(2,1)S(1)}, bf16[64,4096]{1,0:T(8,128)(2,1)}, u32[]{:S(2)}, u32[]{:S(2)}) collective-permute-start(bf16[64,4096]{1,0:T(8,128)(2,1)S(1)} %get-tuple-element.15), channel_id=1, source_target_pairs={{0,64},{32,96},{64,128},{96,160},{128,192},{160,224},{192,0},{224,... | collective-permute-start | bytes 1572872 | tf_op jit(solution)/shard_map/ppermute | solution.py:62
  138.5 25.4 %all-to-all-start.1 = ((bf16[32,2,4096]{2,1,0:T(2,128)(2,1)}), bf16[32,2,4096]{2,1,0:T(2,128)(2,1)S(1)}, u32[]{:S(2)}, u32[]{:S(2)}) async-start(bf16[32,2,4096]{2,1,0:T(2,128)(2,1)} %reshape.27), calls=%async_computation.1 | async-start | bytes 1048576 | tf_op jit(solution)/shard_map/all_to_all | solution.py:110
  163.9 23.8 %all-to-all-start.3 = ((bf16[32,2,4096]{2,1,0:T(2,128)(2,1)}), bf16[32,2,4096]{2,1,0:T(2,128)(2,1)S(1)}, u32[]{:S(2)}, u32[]{:S(2)}) async-start(bf16[32,2,4096]{2,1,0:T(2,128)(2,1)} %reshape.29), calls=%async_computation.3 | async-start | bytes 1048576 | tf_op jit(solution)/shard_map/all_to_all | solution.py:110
  (17 other events, 152.8 us)

commit v3 on v1

v3 whole, which is shorter than its diff:
```python
import functools

import jax
import jax.numpy as jnp
from jax import lax
from jax.experimental import pallas as pl
from jax.experimental.pallas import tpu as pltpu
from jax.sharding import PartitionSpec as P


def slot_table(expert_ids, capacity):
    rows, top_count = expert_ids.shape
    pairs = rows * top_count
    flat = expert_ids.reshape(pairs)
    earlier = jnp.arange(pairs)[None, :] < jnp.arange(pairs)[:, None]
    same = flat[:, None] == flat[None, :]
    ranked = jnp.sum((same & earlier).astype(jnp.int32), axis=1).reshape(rows, top_count)
    return jnp.where(ranked < capacity, expert_ids * capacity + ranked, -1)


def expert_kernel(counts, *refs):
    total = sum(counts)
    pieces, (gate_ref, up_ref, down_ref), outs = refs[:total], refs[total : total + 3], refs[total + 3 :]
    transposed = (((1,), (1,)), ((), ()))
    width = down_ref.shape[2]
    step = min(512, width)
    for index, count in enumerate(counts):
        start = sum(counts[:index])

        @pl.when(pl.program_id(0) == index)
        def _(mine=slice(start, start + count)):
            rows = jnp.concatenate([ref[...] for ref in pieces[mine]], axis=0)
            gate_act = lax.dot_general(
                rows, gate_ref[0], transposed, preferred_element_type=jnp.float32
            )
            up_act = lax.dot_general(rows, up_ref[0], transposed, preferred_element_type=jnp.float32)
            hidden = (gate_act / (1.0 + jnp.exp(-gate_act)) * up_act).astype(jnp.bfloat16)
            for begin in range(0, width, step):
                columns = slice(begin, begin + step)
                out = jnp.dot(
                    hidden, down_ref[0, :, columns], preferred_element_type=jnp.float32
                ).astype(jnp.bfloat16)
                row = 0
                for ref in outs[mine]:
                    ref[:, columns] = out[row : row + ref.shape[0]]
                    row += ref.shape[0]


def expert_rows(pieces, gate_weight, up_weight, down_weight):
    flat = [piece for group in pieces for piece in group]
    rows = sum(piece.shape[0] for piece in flat)
    width = flat[0].shape[1]
    hidden = gate_weight.shape[1]
    whole = pl.BlockSpec(memory_space=pltpu.VMEM)
    weight = pl.BlockSpec((1, hidden, width), lambda i: (i, 0, 0))
    return pl.pallas_call(
        functools.partial(expert_kernel, [len(group) for group in pieces]),
        grid=(len(pieces),),
        in_specs=[whole] * len(flat) + [weight] * 3,
        out_specs=[whole] * len(flat),
        out_shape=[pltpu.VMEM(piece.shape, jnp.bfloat16) for piece in flat],
        cost_estimate=pl.CostEstimate(
            flops=6 * rows * hidden * width,
            bytes_accessed=6 * len(pieces) * hidden * width + 4 * rows * width,
            transcendentals=rows * hidden,
        ),
        compiler_params=pltpu.CompilerParams(vmem_limit_bytes=24 * 1024 * 1024),
    )(
        *(pltpu.with_memory_space_constraint(piece, pltpu.VMEM) for piece in flat),
        *(
            pltpu.with_memory_space_constraint(value, pltpu.HBM)
            for value in (gate_weight, up_weight, down_weight)
        ),
    )


def body(tokens, gate_values, expert_ids, gate_weight, up_weight, down_weight):
    dp_count = lax.axis_size("dp")
    ring = dp_count // 2
    assert ring == 4 and gate_weight.shape[0] == 2
    column_count = lax.axis_size("expert")
    per_device = gate_weight.shape[0]
    expert_count = per_device * column_count
    token_rows, model_width = tokens.shape
    top_count = expert_ids.shape[1]
    capacity = max(2, (5 * token_rows * top_count + 4 * expert_count - 1) // (4 * expert_count))
    chunk_rows = column_count * capacity

    def along_ring(value, step):
        return lax.ppermute(
            value,
            "dp",
            [(2 * y + c, 2 * ((y + step) % ring) + c) for y in range(ring) for c in range(2)],
        )

    def across(value):
        return lax.ppermute(
            value, "dp", [(2 * y + c, 2 * y + 1 - c) for y in range(ring) for c in range(2)]
        )

    slot = slot_table(expert_ids, capacity)
    hit = slot[:, :, None] == jnp.arange(expert_count * capacity, dtype=jnp.int32)[None, None, :]
    chosen = jnp.sum(hit.astype(jnp.float32), axis=1).astype(jnp.bfloat16)
    weights = jnp.sum(
        jnp.where(hit, gate_values.astype(jnp.float32)[:, :, None], 0.0), axis=1
    ).astype(jnp.bfloat16)

    sent = jnp.einsum("ts,td->sd", chosen, tokens, preferred_element_type=jnp.float32)
    sent = sent.astype(jnp.bfloat16).reshape(column_count, per_device * capacity, model_width)

    def columns(value):
        return lax.all_to_all(value, "expert", split_axis=0, concat_axis=0, tiled=True)

    def add(*values):
        total = values[0].astype(jnp.float32)
        for value in values[1:]:
            total = total + value.astype(jnp.float32)
        return total.astype(jnp.bfloat16)

    tie = lax.optimization_barrier

    def experts(first, second):
        return expert_rows((first, second), gate_weight, up_weight, down_weight)

    arrived = columns(sent).reshape(column_count, per_device, capacity, model_width)
    own0, own1 = (arrived[:, index].reshape(chunk_rows, model_width) for index in range(2))
    before0, after1, before1, after0 = tie(
        (along_ring(own0, 1), along_ring(own1, -1), along_ring(own1, 1), along_ring(own0, -1))
    )
    facing0, facing1 = along_ring(before0, 1), along_ring(after1, -1)

    a0, b0, fa0, fb0, a1, b1, fa1, fb1 = experts(
        (after0, before0, across(after0), across(before0)),
        (after1, before1, across(after1), across(before1)),
    )
    facing0, facing1, a0, b0, fa0, fb0, a1, b1, fa1, fb1 = tie(
        (facing0, facing1, a0, b0, fa0, fb0, a1, b1, fa1, fb1)
    )
    f0, ff0, f1, ff1 = experts((facing0, across(facing0)), (facing1, across(facing1)))
    o0, fo0, o1, fo1 = experts((own0, across(own0)), (own1, across(own1)))

    pa1, pb0 = across(fa1), across(fb0)
    to_after, to_before, from_before1, from_after0 = tie(
        (
            along_ring(add(f0, across(ff0)), 1),
            along_ring(add(f1, across(ff1)), -1),
            along_ring(add(a1, pa1), 1),
            along_ring(add(b0, pb0), -1),
        )
    )
    from_before0 = along_ring(add(a0, across(fa0), to_after), 1)
    from_after1 = along_ring(add(b1, across(fb1), to_before), -1)
    totals = [
        add(o0, across(fo0), from_before0, from_after0),
        add(o1, across(fo1), from_before1, from_after1),
    ]
    totals = jnp.concatenate(
        [total.reshape(column_count, 1, capacity, model_width) for total in totals], axis=1
    ).reshape(column_count, per_device * capacity, model_width)
    rows_back = columns(totals).reshape(expert_count * capacity, model_width)
    mixed_out = jnp.einsum("ts,sd->td", weights, rows_back, preferred_element_type=jnp.float32)
    return mixed_out.astype(jnp.bfloat16)


def solution(mesh):
    return jax.shard_map(
        body,
        mesh=mesh,
        in_specs=(
            P(("dp", "expert"), None),
            P(("dp", "expert"), None),
            P(("dp", "expert"), None),
            P("expert", "dp", None),
            P("expert", "dp", None),
            P("expert", "dp", None),
        ),
        out_specs=P(("dp", "expert"), None),
        check_vma=False,
    )
```

time: 251 us -> 181 us (0.72)
  waiting for transfers between devices: 105 us -> 55.2 us
  matrix products: 25.8 us -> 1.36 us
  starting transfers between devices: 0.04 us -> 22.6 us
  local copies, waits for them, and re-layouts: 27.3 us -> 5.79 us
  Pallas kernels: 0 us -> 17.3 us
  between operations: 13.4 us -> 0.26 us
  blocking collectives: 77.3 us -> 72.8 us
  other arithmetic: 1.67 us -> 5.17 us
    reduce_scatter x1 -> x0, waiting for transfers between devices: 55.4 us -> none  [body(): lax.psum_scatter(pieces.reshape(dp_count * per_device * column_count * ca...]
    ppermute x0 -> x28, waiting for transfers between devices: none -> 55.2 us  [the longest x12 48.2 us: along_ring(): lax.ppermute(value, 'dp', [(2 * y + c, 2 * ((y + step) % ring) + c) for y...]
    all_gather x1 -> x0, waiting for transfers between devices: 49.3 us -> none  [body(): shared = lax.all_gather(arrived, 'dp', axis=0, tiled=False)]
    ppermute x0 -> x28, starting transfers between devices: none -> 22.6 us  [the longest x12 19.6 us: along_ring(): lax.ppermute(value, 'dp', [(2 * y + c, 2 * ((y + step) % ring) + c) for y...]
    dot_general x2 -> x0, matrix products: 21.3 us -> none  [the longest x1 13.7 us: body(): jnp.einsum('glrh,lhd->glrd', hidden, down_weight, preferred_element_type=...]
    pallas_call x0 -> x3, Pallas kernels: none -> 17.3 us  [expert_rows(): pl.pallas_call(functools.partial(expert_kernel, [len(group) for group in...]
    reshape x7, local copies, waits for them, and re-layouts: 16.3 us -> 2.76 us  [the longest x4 1.26 us: body(): total.reshape(column_count, 1, capacity, model_width)]
    convert_element_type x1 -> x0, local copies, waits for them, and re-layouts: 7.71 us -> none  [body(): pieces = jnp.einsum('glrh,lhd->glrd', hidden, down_weight, preferred_elem...]
  transfers between devices with their start and end apart: 2 -> 28, of which waited for: 2 -> 14; matrix products, arithmetic and copies ran while one was open for 0% -> 2% of each run, Pallas kernels for 0% -> 10%
where the time goes in v3:
time: 181 us
  blocking collectives  72.8 us (40%)
  waiting for transfers between devices  55.2 us (30%)
  starting transfers between devices  22.6 us (12%)
  Pallas kernels  17.3 us (10%)
  local copies, waits for them, and re-layouts  5.79 us (3%)
  other arithmetic  5.17 us (3%)
    all_to_all x2, blocking collectives, columns(): lax.all_to_all(value, 'expert', split_axis=0, concat_axis=0, tiled=True)  72.8 us
    ppermute x12, waiting for transfers between devices, along_ring(): lax.ppermute(value, 'dp', [(2 * y + c, 2 * ((y + step) % ring) + c) for y...  48.2 us
    ppermute x12, starting transfers between devices, along_ring(): lax.ppermute(value, 'dp', [(2 * y + c, 2 * ((y + step) % ring) + c) for y...  19.6 us
    pallas_call x3, Pallas kernels, expert_rows(): pl.pallas_call(functools.partial(expert_kernel, [len(group) for group in...  17.3 us
    ppermute x16, waiting for transfers between devices, across(): lax.ppermute(value, 'dp', [(2 * y + c, 2 * y + 1 - c) for y in range(ring...  6.96 us
  transfers between devices with their start and end apart: 28, of which 14 were waited for; matrix products, arithmetic and copies ran while one was open for 2% of the time, Pallas kernels for 10%

profile of v3, /device:TPU:2, one launch (start us, length us, event | category | flops | bytes accessed | tf_op | source)
XLA Modules:
  0.0 180.5 jit_solution(12029408339100534168)
XLA Ops:
  3.5 39.5 %all_to_all.10 = bf16[32,4,4096]{2,1,0:T(4,128)(2,1)S(1)} all-to-all(bf16[32,4,4096]{2,1,0:T(4,128)(2,1)S(1)} %reshape.26), channel_id=1, replica_groups=mesh['dp'=8,'expert'=32] {'expert'}, dimensions={0} | all-to-all | bytes 2097152 | tf_op jit(solution)/shard_map/all_to_all | solution.py:112
  44.4 1.7 collective-permute-start.3
  46.8 1.7 collective-permute-start.4
  48.9 2.9 %collective-permute-start.6 = (bf16[64,4096]{1,0:T(8,128)(2,1)S(1)}, bf16[64,4096]{1,0:T(8,128)(2,1)S(1)}, u32[]{:S(2)}, u32[]{:S(2)}) collective-permute-start(bf16[64,4096]{1,0:T(8,128)(2,1)S(1)} %reshape_squeeze.6.refs_0_), channel_id=1, source_target_pairs={{0,192},{32,224},{64,0},{96,32},{128,64},{160,96},{192,128},{224,1... | collective-permute-start | bytes 1572872 | tf_op jit(solution)/shard_map/ppermute | solution.py:90
  51.8 8.8 %collective-permute-done.3.refs_1_ = bf16[64,4096]{1,0:T(8,128)(2,1)S(1)} collective-permute-done((bf16[64,4096]{1,0:T(8,128)(2,1)S(1)}, bf16[64,4096]{1,0:T(8,128)(2,1)S(1)}, u32[]{:S(2)}, u32[]{:S(2)}) %collective-permute-start.3) | collective-permute-done | bytes 524320 | tf_op jit(solution)/shard_map/ppermute | solution.py:90
  61.7 6.9 %collective-permute-done.5.refs_5_ = bf16[64,4096]{1,0:T(8,128)(2,1)S(1)} collective-permute-done((bf16[64,4096]{1,0:T(8,128)(2,1)S(1)}, bf16[64,4096]{1,0:T(8,128)(2,1)S(1)}, u32[]{:S(2)}, u32[]{:S(2)}) %collective-permute-start.5) | collective-permute-done | bytes 524320 | tf_op jit(solution)/shard_map/ppermute | solution.py:90
  70.5 1.6 collective-permute-start.7
  72.1 2.3 %collective-permute-start.8 = (bf16[64,4096]{1,0:T(8,128)(2,1)S(1)}, bf16[64,4096]{1,0:T(8,128)(2,1)S(1)}, u32[]{:S(2)}, u32[]{:S(2)}) collective-permute-start(bf16[64,4096]{1,0:T(8,128)(2,1)S(1)} %collective-permute-done.4.refs_4_), channel_id=1, source_target_pairs={{0,192},{32,224},{64,0},{96,32},{128,64},{160,96},{192,128},{224,1... | collective-permute-start | bytes 1572872 | tf_op jit(solution)/shard_map/ppermute | solution.py:90
  74.4 6.3 %shard_map.65 = (bf16[64,4096]{1,0:T(8,128)(2,1)S(1)}, bf16[64,4096]{1,0:T(8,128)(2,1)S(1)}, bf16[64,4096]{1,0:T(8,128)(2,1)S(1)}, bf16[64,4096]{1,0:T(8,128)(2,...) custom-call(bf16[64,4096]{1,0:T(8,128)(2,1)S(1)} %collective-permute, ...), custom_call_target="tpu_custom_call" | custom-call | flops 2415919104 | bytes 17825792 | tf_op jit(solution)/shard_map/pallas_call | solution.py:56
  80.6 4.9 %collective-permute-done.7.refs_0_ = bf16[64,4096]{1,0:T(8,128)(2,1)S(1)} collective-permute-done((bf16[64,4096]{1,0:T(8,128)(2,1)S(1)}, bf16[64,4096]{1,0:T(8,128)(2,1)S(1)}, u32[]{:S(2)}, u32[]{:S(2)}) %collective-permute-start.7) | collective-permute-done | bytes 524320 | tf_op jit(solution)/shard_map/ppermute | solution.py:90
  88.0 2.7 %collective-permute-done.14.refs_1_ = bf16[64,4096]{1,0:T(8,128)(2,1)S(1)} collective-permute-done((bf16[64,4096]{1,0:T(8,128)(2,1)S(1)}, bf16[64,4096]{1,0:T(8,128)(2,1)S(1)}, u32[]{:S(2)}, u32[]{:S(2)}) %collective-permute-start.14) | collective-permute-done | bytes 524320 | tf_op jit(solution)/shard_map/ppermute | solution.py:97
  90.8 3.7 %collective-permute-start.23 = (bf16[64,4096]{1,0:T(8,128)(2,1)S(1)}, bf16[64,4096]{1,0:T(8,128)(2,1)S(1)}, u32[]{:S(2)}, u32[]{:S(2)}) collective-permute-start(bf16[64,4096]{1,0:T(8,128)(2,1)S(1)} %add_convert_fusion.4), channel_id=1, source_target_pairs={{0,192},{32,224},{64,0},{96,32},{128,64},{160,96},{192,128},{224,1... | collective-permute-start | bytes 1572872 | tf_op jit(solution)/shard_map/ppermute | solution.py:90
  94.5 5.5 %shard_map.66 = (bf16[64,4096]{1,0:T(8,128)(2,1)S(1)}, bf16[64,4096]{1,0:T(8,128)(2,1)S(1)}, bf16[64,4096]{1,0:T(8,128)(2,1)S(1)}, bf16[64,4096]{1,0:T(8,128)(2,1)S(1)}) custom-call(bf16[64,4096]{1,0:T(8,128)(2,1)S(1)} %collective-permute-done.7.refs_0_, bf16[64,4096]{1,0:T(8,128)(2,1)S(1)} %collective-permute-done.14.refs_1_, ...), custom_call_target="tpu_custom_call" | custom-call | flops 1207959552 | bytes 13631488 | tf_op jit(solution)/shard_map/pallas_call | solution.py:56
  100.3 1.7 collective-permute-done.18
  102.3 1.6 collective-permute-done.16
  103.9 1.6 collective-permute-start.19
  106.2 5.5 %shard_map.64 = (bf16[64,4096]{1,0:T(8,128)(2,1)S(1)}, bf16[64,4096]{1,0:T(8,128)(2,1)S(1)}, bf16[64,4096]{1,0:T(8,128)(2,1)S(1)}, bf16[64,4096]{1,0:T(8,128)(2,1)S(1)}) custom-call(bf16[64,4096]{1,0:T(8,128)(2,1)S(1)} %reshape_squeeze.6.refs_0_, bf16[64,4096]{1,0:T(8,128)(2,1)S(1)} %collective-permute-done.refs_1_, ...), custom_call_target="tpu_custom_call" | custom-call | flops 1207959552 | bytes 13631488 | tf_op jit(solution)/shard_map/pallas_call | solution.py:56
  112.3 4.0 %collective-permute-done.21 = bf16[64,4096]{1,0:T(8,128)(2,1)S(1)} collective-permute-done((bf16[64,4096]{1,0:T(8,128)(2,1)S(1)}, bf16[64,4096]{1,0:T(8,128)(2,1)S(1)}, u32[]{:S(2)}, u32[]{:S(2)}) %collective-permute-start.21) | collective-permute-done | bytes 524320 | tf_op jit(solution)/shard_map/ppermute | solution.py:90
  116.3 1.6 collective-permute-done.19
  117.9 9.2 %collective-permute-done.17 = bf16[64,4096]{1,0:T(8,128)(2,1)S(1)} collective-permute-done((bf16[64,4096]{1,0:T(8,128)(2,1)S(1)}, bf16[64,4096]{1,0:T(8,128)(2,1)S(1)}, u32[]{:S(2)}, u32[]{:S(2)}) %collective-permute-start.17) | collective-permute-done | bytes 524320 | tf_op jit(solution)/shard_map/ppermute | solution.py:90
  128.4 3.2 %collective-permute-start.27 = (bf16[64,4096]{1,0:T(8,128)(2,1)}, bf16[64,4096]{1,0:T(8,128)(2,1)}, u32[]{:S(2)}, u32[]{:S(2)}) collective-permute-start(bf16[64,4096]{1,0:T(8,128)(2,1)} %add_convert_fusion.1), channel_id=1, source_target_pairs={{0,192},{32,224},{64,0},{96,32},{128,64},{160,96},{192,128},{224,1... | collective-permute-start | bytes 1572872 | tf_op jit(solution)/shard_map/ppermute | solution.py:90
  131.6 10.5 %collective-permute-done.24 = bf16[64,4096]{1,0:T(8,128)(2,1)S(1)} collective-permute-done((bf16[64,4096]{1,0:T(8,128)(2,1)S(1)}, bf16[64,4096]{1,0:T(8,128)(2,1)S(1)}, u32[]{:S(2)}, u32[]{:S(2)}) %collective-permute-start.24) | collective-permute-done | bytes 524320 | tf_op jit(solution)/shard_map/ppermute | solution.py:90
  143.0 1.5 add_convert_fusion
  146.1 33.3 %all_to_all.11 = bf16[32,4,4096]{2,1,0:T(4,128)(2,1)S(1)} all-to-all(bf16[32,4,4096]{2,1,0:T(4,128)(2,1)S(1)} %copy.29), channel_id=1, replica_groups=mesh['dp'=8,'expert'=32] {'expert'}, dimensions={0} | all-to-all | bytes 2097152 | tf_op jit(solution)/shard_map/all_to_all | solution.py:112
  (69 shorter events, 18.2 us)
Async XLA Ops:
  44.4 16.1 %collective-permute-start.3 = (bf16[64,4096]{1,0:T(8,128)(2,1)S(1)}, bf16[64,4096]{1,0:T(8,128)(2,1)S(1)}, u32[]{:S(2)}, u32[]{:S(2)}) collective-permute-start(bf16[64,4096]{1,0:T(8,128)(2,1)S(1)} %reshape_squeeze.6.refs_0_), channel_id=1, source_target_pairs={{0,64},{32,96},{64,128},{96,160},{128,192},{160,224},{192,0},{224,... | collective-permute-start | bytes 1572872 | tf_op jit(solution)/shard_map/ppermute | solution.py:90
  46.8 14.9 %collective-permute-start.4 = (bf16[64,4096]{1,0:T(8,128)(2,1)S(1)}, bf16[64,4096]{1,0:T(8,128)(2,1)S(1)}, u32[]{:S(2)}, u32[]{:S(2)}) collective-permute-start(bf16[64,4096]{1,0:T(8,128)(2,1)S(1)} %reshape_squeeze.7.refs_2_), channel_id=1, source_target_pairs={{0,192},{32,224},{64,0},{96,32},{128,64},{160,96},{192,128},{224,1... | collective-permute-start | bytes 1572872 | tf_op jit(solution)/shard_map/ppermute | solution.py:90
  48.5 20.1 %collective-permute-start.5 = (bf16[64,4096]{1,0:T(8,128)(2,1)S(1)}, bf16[64,4096]{1,0:T(8,128)(2,1)S(1)}, u32[]{:S(2)}, u32[]{:S(2)}) collective-permute-start(bf16[64,4096]{1,0:T(8,128)(2,1)S(1)} %reshape_squeeze.7.refs_2_), channel_id=1, source_target_pairs={{0,64},{32,96},{64,128},{96,160},{128,192},{160,224},{192,0},{224,... | collective-permute-start | bytes 1572872 | tf_op jit(solution)/shard_map/ppermute | solution.py:90
  48.9 20.6 %collective-permute-start.6 = (bf16[64,4096]{1,0:T(8,128)(2,1)S(1)}, bf16[64,4096]{1,0:T(8,128)(2,1)S(1)}, u32[]{:S(2)}, u32[]{:S(2)}) collective-permute-start(bf16[64,4096]{1,0:T(8,128)(2,1)S(1)} %reshape_squeeze.6.refs_0_), channel_id=1, source_target_pairs={{0,192},{32,224},{64,0},{96,32},{128,64},{160,96},{192,128},{224,1... | collective-permute-start | bytes 1572872 | tf_op jit(solution)/shard_map/ppermute | solution.py:90
  69.5 4.9 %collective-permute-start.11 = (bf16[64,4096]{1,0:T(8,128)(2,1)S(1)}, bf16[64,4096]{1,0:T(8,128)(2,1)S(1)}, u32[]{:S(2)}, u32[]{:S(2)}) collective-permute-start(bf16[64,4096]{1,0:T(8,128)(2,1)S(1)} %collective-permute-done.4.refs_4_), channel_id=1, source_target_pairs={{0,32},{32,0},{64,96},{96,64},{128,160},{160,128},{192,224},{224,1... | collective-permute-start | bytes 1572872 | tf_op jit(solution)/shard_map/ppermute | solution.py:97
  70.0 4.4 %collective-permute-start.12 = (bf16[64,4096]{1,0:T(8,128)(2,1)S(1)}, bf16[64,4096]{1,0:T(8,128)(2,1)S(1)}, u32[]{:S(2)}, u32[]{:S(2)}) collective-permute-start(bf16[64,4096]{1,0:T(8,128)(2,1)S(1)} %collective-permute-done.5.refs_5_), channel_id=1, source_target_pairs={{0,32},{32,0},{64,96},{96,64},{128,160},{160,128},{192,224},{224,1... | collective-permute-start | bytes 1572872 | tf_op jit(solution)/shard_map/ppermute | solution.py:97
  70.0 4.4 %collective-permute-start.9 = (bf16[64,4096]{1,0:T(8,128)(2,1)S(1)}, bf16[64,4096]{1,0:T(8,128)(2,1)S(1)}, u32[]{:S(2)}, u32[]{:S(2)}) collective-permute-start(bf16[64,4096]{1,0:T(8,128)(2,1)S(1)} %collective-permute-done.6.refs_0_), channel_id=1, source_target_pairs={{0,32},{32,0},{64,96},{96,64},{128,160},{160,128},{192,224},{224,1... | collective-permute-start | bytes 1572872 | tf_op jit(solution)/shard_map/ppermute | solution.py:97
  70.5 15.0 %collective-permute-start.7 = (bf16[64,4096]{1,0:T(8,128)(2,1)S(1)}, bf16[64,4096]{1,0:T(8,128)(2,1)S(1)}, u32[]{:S(2)}, u32[]{:S(2)}) collective-permute-start(bf16[64,4096]{1,0:T(8,128)(2,1)S(1)} %collective-permute-done.3.refs_1_), channel_id=1, source_target_pairs={{0,64},{32,96},{64,128},{96,160},{128,192},{160,224},{192,0},{224,... | collective-permute-start | bytes 1572872 | tf_op jit(solution)/shard_map/ppermute | solution.py:90
  72.1 13.7 %collective-permute-start.8 = (bf16[64,4096]{1,0:T(8,128)(2,1)S(1)}, bf16[64,4096]{1,0:T(8,128)(2,1)S(1)}, u32[]{:S(2)}, u32[]{:S(2)}) collective-permute-start(bf16[64,4096]{1,0:T(8,128)(2,1)S(1)} %collective-permute-done.4.refs_4_), channel_id=1, source_target_pairs={{0,192},{32,224},{64,0},{96,32},{128,64},{160,96},{192,128},{224,1... | collective-permute-start | bytes 1572872 | tf_op jit(solution)/shard_map/ppermute | solution.py:90
  85.9 19.7 %collective-permute-start = (bf16[64,4096]{1,0:T(8,128)(2,1)S(1)}, bf16[64,4096]{1,0:T(8,128)(2,1)S(1)}, u32[]{:S(2)}, u32[]{:S(2)}) collective-permute-start(bf16[64,4096]{1,0:T(8,128)(2,1)S(1)} %reshape_squeeze.6.refs_0_), channel_id=1, source_target_pairs={{0,32},{32,0},{64,96},{96,64},{128,160},{160,128},{192,224},{224,1... | collective-permute-start | bytes 1572872 | tf_op jit(solution)/shard_map/ppermute | solution.py:97
  86.4 19.8 %collective-permute-start.1 = (bf16[64,4096]{1,0:T(8,128)(2,1)S(1)}, bf16[64,4096]{1,0:T(8,128)(2,1)S(1)}, u32[]{:S(2)}, u32[]{:S(2)}) collective-permute-start(bf16[64,4096]{1,0:T(8,128)(2,1)S(1)} %reshape_squeeze.7.refs_2_), channel_id=1, source_target_pairs={{0,32},{32,0},{64,96},{96,64},{128,160},{160,128},{192,224},{224,1... | collective-permute-start | bytes 1572872 | tf_op jit(solution)/shard_map/ppermute | solution.py:97
  86.4 13.7 %collective-permute-start.20 = (bf16[64,4096]{1,0:T(8,128)(2,1)S(1)}, bf16[64,4096]{1,0:T(8,128)(2,1)S(1)}, u32[]{:S(2)}, u32[]{:S(2)}) collective-permute-start(bf16[64,4096]{1,0:T(8,128)(2,1)S(1)} %get-tuple-element.62), channel_id=1, source_target_pairs={{0,32},{32,0},{64,96},{96,64},{128,160},{160,128},{192,224},{224,1... | collective-permute-start | bytes 1572872 | tf_op jit(solution)/shard_map/ppermute | solution.py:97
  86.9 3.9 %collective-permute-start.14 = (bf16[64,4096]{1,0:T(8,128)(2,1)S(1)}, bf16[64,4096]{1,0:T(8,128)(2,1)S(1)}, u32[]{:S(2)}, u32[]{:S(2)}) collective-permute-start(bf16[64,4096]{1,0:T(8,128)(2,1)S(1)} %collective-permute-done.7.refs_0_), channel_id=1, source_target_pairs={{0,32},{32,0},{64,96},{96,64},{128,160},{160,128},{192,224},{224,1... | collective-permute-start | bytes 1572872 | tf_op jit(solution)/shard_map/ppermute | solution.py:97
  87.8 6.7 %collective-permute-start.15 = (bf16[64,4096]{1,0:T(8,128)(2,1)S(1)}, bf16[64,4096]{1,0:T(8,128)(2,1)S(1)}, u32[]{:S(2)}, u32[]{:S(2)}) collective-permute-start(bf16[64,4096]{1,0:T(8,128)(2,1)S(1)} %collective-permute-done.8.refs_2_), channel_id=1, source_target_pairs={{0,32},{32,0},{64,96},{96,64},{128,160},{160,128},{192,224},{224,1... | collective-permute-start | bytes 1572872 | tf_op jit(solution)/shard_map/ppermute | solution.py:97
  90.8 20.9 %collective-permute-start.23 = (bf16[64,4096]{1,0:T(8,128)(2,1)S(1)}, bf16[64,4096]{1,0:T(8,128)(2,1)S(1)}, u32[]{:S(2)}, u32[]{:S(2)}) collective-permute-start(bf16[64,4096]{1,0:T(8,128)(2,1)S(1)} %add_convert_fusion.4), channel_id=1, source_target_pairs={{0,192},{32,224},{64,0},{96,32},{128,64},{160,96},{192,128},{224,1... | collective-permute-start | bytes 1572872 | tf_op jit(solution)/shard_map/ppermute | solution.py:90
  100.2 16.0 %collective-permute-start.21 = (bf16[64,4096]{1,0:T(8,128)(2,1)S(1)}, bf16[64,4096]{1,0:T(8,128)(2,1)S(1)}, u32[]{:S(2)}, u32[]{:S(2)}) collective-permute-start(bf16[64,4096]{1,0:T(8,128)(2,1)S(1)} %add_convert_fusion.5), channel_id=1, source_target_pairs={{0,64},{32,96},{64,128},{96,160},{128,192},{160,224},{192,0},{224,... | collective-permute-start | bytes 1572872 | tf_op jit(solution)/shard_map/ppermute | solution.py:90
  103.9 14.0 %collective-permute-start.19 = (bf16[64,4096]{1,0:T(8,128)(2,1)S(1)}, bf16[64,4096]{1,0:T(8,128)(2,1)S(1)}, u32[]{:S(2)}, u32[]{:S(2)}) collective-permute-start(bf16[64,4096]{1,0:T(8,128)(2,1)S(1)} %add_convert_fusion.6), channel_id=1, source_target_pairs={{0,192},{32,224},{64,0},{96,32},{128,64},{160,96},{192,128},{224,1... | collective-permute-start | bytes 1572872 | tf_op jit(solution)/shard_map/ppermute | solution.py:90
  105.6 21.5 %collective-permute-start.17 = (bf16[64,4096]{1,0:T(8,128)(2,1)S(1)}, bf16[64,4096]{1,0:T(8,128)(2,1)S(1)}, u32[]{:S(2)}, u32[]{:S(2)}) collective-permute-start(bf16[64,4096]{1,0:T(8,128)(2,1)S(1)} %add_convert_fusion.7), channel_id=1, source_target_pairs={{0,64},{32,96},{64,128},{96,160},{128,192},{160,224},{192,0},{224,... | collective-permute-start | bytes 1572872 | tf_op jit(solution)/shard_map/ppermute | solution.py:90
  106.2 20.9 %collective-permute-start.13 = (bf16[64,4096]{1,0:T(8,128)(2,1)S(1)}, bf16[64,4096]{1,0:T(8,128)(2,1)S(1)}, u32[]{:S(2)}, u32[]{:S(2)}) collective-permute-start(bf16[64,4096]{1,0:T(8,128)(2,1)S(1)} %get-tuple-element.54), channel_id=1, source_target_pairs={{0,32},{32,0},{64,96},{96,64},{128,160},{160,128},{192,224},{224,1... | collective-permute-start | bytes 1572872 | tf_op jit(solution)/shard_map/ppermute | solution.py:97
  111.7 19.9 %collective-permute-start.2 = (bf16[64,4096]{1,0:T(8,128)(2,1)S(1)}, bf16[64,4096]{1,0:T(8,128)(2,1)S(1)}, u32[]{:S(2)}, u32[]{:S(2)}) collective-permute-start(bf16[64,4096]{1,0:T(8,128)(2,1)S(1)} %get-tuple-element.40), channel_id=1, source_target_pairs={{0,32},{32,0},{64,96},{96,64},{128,160},{160,128},{192,224},{224,1... | collective-permute-start | bytes 1572872 | tf_op jit(solution)/shard_map/ppermute | solution.py:97
  116.2 26.8 %collective-permute-start.25 = (bf16[64,4096]{1,0:T(8,128)(2,1)S(1)}, bf16[64,4096]{1,0:T(8,128)(2,1)}, u32[]{:S(2)}, u32[]{:S(2)}) collective-permute-start(bf16[64,4096]{1,0:T(8,128)(2,1)S(1)} %get-tuple-element.68), channel_id=1, source_target_pairs={{0,32},{32,0},{64,96},{96,64},{128,160},{160,128},{192,224},{224,1... | collective-permute-start | bytes 1572872 | tf_op jit(solution)/shard_map/ppermute | solution.py:97
  117.9 9.5 %collective-permute-start.26 = (bf16[64,4096]{1,0:T(8,128)(2,1)S(1)}, bf16[64,4096]{1,0:T(8,128)(2,1)S(1)}, u32[]{:S(2)}, u32[]{:S(2)}) collective-permute-start(bf16[64,4096]{1,0:T(8,128)(2,1)S(1)} %get-tuple-element.71), channel_id=1, source_target_pairs={{0,32},{32,0},{64,96},{96,64},{128,160},{160,128},{192,224},{224,1... | collective-permute-start | bytes 1572872 | tf_op jit(solution)/shard_map/ppermute | solution.py:97
  127.3 14.8 %collective-permute-start.24 = (bf16[64,4096]{1,0:T(8,128)(2,1)S(1)}, bf16[64,4096]{1,0:T(8,128)(2,1)S(1)}, u32[]{:S(2)}, u32[]{:S(2)}) collective-permute-start(bf16[64,4096]{1,0:T(8,128)(2,1)S(1)} %add_convert_fusion.3), channel_id=1, source_target_pairs={{0,64},{32,96},{64,128},{96,160},{128,192},{160,224},{192,0},{224,... | collective-permute-start | bytes 1572872 | tf_op jit(solution)/shard_map/ppermute | solution.py:90
  128.4 14.6 %collective-permute-start.27 = (bf16[64,4096]{1,0:T(8,128)(2,1)}, bf16[64,4096]{1,0:T(8,128)(2,1)}, u32[]{:S(2)}, u32[]{:S(2)}) collective-permute-start(bf16[64,4096]{1,0:T(8,128)(2,1)} %add_convert_fusion.1), channel_id=1, source_target_pairs={{0,192},{32,224},{64,0},{96,32},{128,64},{160,96},{192,128},{224,1... | collective-permute-start | bytes 1572872 | tf_op jit(solution)/shard_map/ppermute | solution.py:90
  (5 other events, 11.0 us)

commit v4 on v2

v4 whole, which is shorter than its diff:
```python
import functools

import jax
import jax.numpy as jnp
from jax import lax
from jax.experimental import pallas as pl
from jax.experimental.pallas import tpu as pltpu
from jax.sharding import PartitionSpec as P


def expert_kernel(count, *refs):
    pieces, (gate_ref, up_ref, down_ref), outs = refs[:count], refs[count : count + 3], refs[count + 3 :]
    rows = jnp.concatenate([ref[...] for ref in pieces], axis=0)
    transposed = (((1,), (1,)), ((), ()))
    gate_act = lax.dot_general(rows, gate_ref[0], transposed, preferred_element_type=jnp.float32)
    up_act = lax.dot_general(rows, up_ref[0], transposed, preferred_element_type=jnp.float32)
    hidden = (gate_act / (1.0 + jnp.exp(-gate_act)) * up_act).astype(jnp.bfloat16)
    width = down_ref.shape[2]
    step = min(512, width)
    for start in range(0, width, step):
        columns = slice(start, start + step)
        out = jnp.dot(
            hidden, down_ref[0, :, columns], preferred_element_type=jnp.float32
        ).astype(jnp.bfloat16)
        row = 0
        for ref in outs:
            ref[:, columns] = out[row : row + ref.shape[0]]
            row += ref.shape[0]


def expert_rows(pieces, heights, index, gate_weight, up_weight, down_weight):
    width = pieces[0].shape[1]
    height = sum(heights)
    hidden = gate_weight.shape[1]
    count = len(pieces)
    whole = pl.BlockSpec(memory_space=pltpu.VMEM)
    weight = pl.BlockSpec((1, hidden, width), lambda i: (index, 0, 0))
    return pl.pallas_call(
        functools.partial(expert_kernel, count),
        grid=(1,),
        in_specs=[whole] * count + [weight] * 3,
        out_specs=[whole] * len(heights),
        out_shape=[pltpu.VMEM((part, width), jnp.bfloat16) for part in heights],
        cost_estimate=pl.CostEstimate(
            flops=6 * height * hidden * width,
            bytes_accessed=6 * hidden * width + 4 * height * width,
            transcendentals=height * hidden,
        ),
        compiler_params=pltpu.CompilerParams(vmem_limit_bytes=24 * 1024 * 1024),
    )(
        *(pltpu.with_memory_space_constraint(piece, pltpu.VMEM) for piece in pieces),
        *(
            pltpu.with_memory_space_constraint(value, pltpu.HBM)
            for value in (gate_weight, up_weight, down_weight)
        ),
    )


def body(tokens, gate_values, expert_ids, gate_weight, up_weight, down_weight):
    dp_count = lax.axis_size("dp")
    ring = dp_count // 2
    assert ring == 4 and gate_weight.shape[0] == 2
    column_count = lax.axis_size("expert")
    per_device = gate_weight.shape[0]
    expert_count = per_device * column_count
    token_rows, model_width = tokens.shape
    top_count = expert_ids.shape[1]
    capacity = max(2, (5 * token_rows * top_count + 4 * expert_count - 1) // (4 * expert_count))
    chunk_rows = column_count * capacity

    def along_ring(value, step):
        return lax.ppermute(
            value,
            "dp",
            [(2 * y + c, 2 * ((y + step) % ring) + c) for y in range(ring) for c in range(2)],
        )

    def across(value):
        return lax.ppermute(
            value, "dp", [(2 * y + c, 2 * y + 1 - c) for y in range(ring) for c in range(2)]
        )

    slots = expert_count * capacity
    slot = jnp.arange(slots, dtype=jnp.int32)
    chose = expert_ids[:, :, None] == (slot // capacity)[None, None, :]
    hit = jnp.any(chose, axis=1)
    earlier = jnp.arange(token_rows)[None, :] < jnp.arange(token_rows)[:, None]
    ranked = jnp.sum((earlier[:, :, None] & hit[None, :, :]).astype(jnp.int32), axis=1)
    taken = hit & (ranked == (slot % capacity)[None, :])
    chosen = taken.astype(jnp.bfloat16)
    chosen = chosen.reshape(token_rows, column_count, per_device, capacity)
    sent0, sent1 = lax.optimization_barrier(
        tuple(
            jnp.einsum(
                "tcr,td->crd", chosen[:, :, index], tokens, preferred_element_type=jnp.float32
            ).astype(jnp.bfloat16)
            for index in range(2)
        )
    )

    def columns(value):
        return lax.all_to_all(value, "expert", split_axis=0, concat_axis=0, tiled=True)

    def add(*values):
        total = values[0].astype(jnp.float32)
        for value in values[1:]:
            total = total + value.astype(jnp.float32)
        return total.astype(jnp.bfloat16)

    tie = lax.optimization_barrier

    def after_all(value, *others):
        return tie((value, *others))[0]

    n = chunk_rows
    half = n // 2

    def facing(before, after):
        return along_ring(before[:half], 1), along_ring(after[half:], -1)

    def experts(index, own, after, before, low, high):
        near = [own, after, before, low, high]
        far = [across(piece) for piece in (low, high, own, after, before)]
        return expert_rows(
            near + far, (4 * n, n, 3 * n), index, gate_weight, up_weight, down_weight
        )

    mine, for_after, for_before = (slice(k * n, (k + 1) * n) for k in range(3))
    low, high = slice(0, half), slice(half, n)

    def outward(kept, paired):
        kept = kept[3 * n :]
        return (
            along_ring(add(kept[low], paired[low]), 1),
            along_ring(add(kept[high], paired[high]), -1),
        )

    def homeward(kept, paired, to_after, to_before):
        to_after = jnp.pad(to_after.astype(jnp.float32), ((0, half), (0, 0)))
        to_before = jnp.pad(to_before.astype(jnp.float32), ((half, 0), (0, 0)))
        return (
            along_ring(add(kept[for_after], paired[for_after], to_after), 1),
            along_ring(add(kept[for_before], paired[for_before], to_before), -1),
        )

    def returned(kept, paired, home, *others):
        total = add(kept[mine], paired[mine], *home)
        if others:
            total = after_all(total, *others)
        return columns(total.reshape(column_count, capacity, model_width))

    arrived0 = columns(sent0)
    own0 = arrived0.reshape(n, model_width)
    before0, after0 = along_ring(own0, 1), along_ring(own0, -1)
    own1 = columns(after_all(sent1, arrived0)).reshape(n, model_width)
    facing0 = facing(before0, after0)

    before1, after1 = along_ring(own1, 1), along_ring(own1, -1)
    kept0, outer0, inner0 = experts(0, own0, after0, before0, *facing0)
    before1, after1, kept0, outer0, inner0 = tie((before1, after1, kept0, outer0, inner0))
    facing1 = facing(before1, after1)
    out0 = outward(kept0, across(outer0))
    inner0 = across(inner0)
    facing1, out0 = tie((facing1, out0))
    home0 = homeward(kept0, inner0, *out0)
    kept1, outer1, inner1 = experts(1, own1, after1, before1, *facing1)
    home0, kept1, outer1, inner1 = tie((home0, kept1, outer1, inner1))
    out1 = outward(kept1, across(outer1))
    inner1 = across(inner1)
    back0 = returned(kept0, inner0, home0)
    home1 = homeward(kept1, inner1, *out1)
    back1 = returned(kept1, inner1, home1, back0)

    chose, taken, gate_values = after_all((chose, taken, gate_values), home0)
    gates = jnp.sum(jnp.where(chose, gate_values.astype(jnp.float32)[:, :, None], 0.0), axis=1)
    weights = jnp.where(taken, gates, 0.0).astype(jnp.bfloat16)
    weights = weights.reshape(token_rows, column_count, per_device, capacity)
    mixed_out = jnp.zeros((token_rows, model_width), jnp.float32)
    for index, back in enumerate((back0, back1)):
        mixed_out = mixed_out + jnp.einsum(
            "tcr,crd->td", weights[:, :, index], back, preferred_element_type=jnp.float32
        )
    return mixed_out.astype(jnp.bfloat16)


def solution(mesh):
    return jax.shard_map(
        body,
        mesh=mesh,
        in_specs=(
            P(("dp", "expert"), None),
            P(("dp", "expert"), None),
            P(("dp", "expert"), None),
            P("expert", "dp", None),
            P("expert", "dp", None),
            P("expert", "dp", None),
        ),
        out_specs=P(("dp", "expert"), None),
        check_vma=False,
    )
```

time: 190 us -> 176 us (0.926)
  waiting for transfers between devices: 107 us -> 75.3 us
  blocking collectives: 0 us -> 28.2 us
  Pallas kernels: 18 us -> 11.9 us
  starting transfers between devices: 48.5 us -> 44.6 us
    all_to_all x0 -> x1, blocking collectives: none -> 28.2 us  [columns(): lax.all_to_all(value, 'expert', split_axis=0, concat_axis=0, tiled=True)]
    ppermute x12 -> x16, waiting for transfers between devices: 68.6 us -> 42.8 us  [along_ring(): lax.ppermute(value, 'dp', [(2 * y + c, 2 * ((y + step) % ring) + c) for y...]
    all_to_all x4 -> x3, starting transfers between devices: 34.2 us -> 21 us  [columns(): lax.all_to_all(value, 'expert', split_axis=0, concat_axis=0, tiled=True)]
    ppermute x12 -> x16, starting transfers between devices: 13.6 us -> 21.6 us  [along_ring(): lax.ppermute(value, 'dp', [(2 * y + c, 2 * ((y + step) % ring) + c) for y...]
    all_to_all x4 -> x3, waiting for transfers between devices: 35.2 us -> 27.9 us  [columns(): lax.all_to_all(value, 'expert', split_axis=0, concat_axis=0, tiled=True)]
    pallas_call x2, Pallas kernels: 18 us -> 11.9 us  [expert_rows(): pl.pallas_call(functools.partial(expert_kernel, count), grid=(1,), in_spe...]
    convert_element_type x4 -> x1, local copies, waits for them, and re-layouts: 2.9 us -> 0.12 us  [body(): weights = jnp.where(taken, gates, 0.0).astype(jnp.bfloat16)]
    ppermute x10 -> x14, waiting for transfers between devices: 3.07 us -> 4.56 us  [across(): lax.ppermute(value, 'dp', [(2 * y + c, 2 * y + 1 - c) for y in range(ring...]
  transfers between devices with their start and end apart: 26 -> 33, of which waited for: 15 -> 18; matrix products, arithmetic and copies ran while one was open for 5% -> 4% of each run, Pallas kernels for 10% -> 7%
where the time goes in v4:
time: 176 us; the launch traced here: 175 us
  waiting for transfers between devices  75.3 us (43%)
  starting transfers between devices  44.6 us (25%)
  blocking collectives  28.2 us (16%)
  Pallas kernels  11.9 us (7%)
  local copies, waits for them, and re-layouts  7.9 us (4%)
  other arithmetic  4.96 us (3%)
  matrix products  2.11 us (1%)
    ppermute x16, waiting for transfers between devices, along_ring(): lax.ppermute(value, 'dp', [(2 * y + c, 2 * ((y + step) % ring) + c) for y...  42.8 us
    all_to_all x1, blocking collectives, columns(): lax.all_to_all(value, 'expert', split_axis=0, concat_axis=0, tiled=True)  28.2 us
    all_to_all x3, waiting for transfers between devices, columns(): lax.all_to_all(value, 'expert', split_axis=0, concat_axis=0, tiled=True)  27.9 us
    ppermute x16, starting transfers between devices, along_ring(): lax.ppermute(value, 'dp', [(2 * y + c, 2 * ((y + step) % ring) + c) for y...  21.6 us
    all_to_all x3, starting transfers between devices, columns(): lax.all_to_all(value, 'expert', split_axis=0, concat_axis=0, tiled=True)  21 us
    pallas_call x2, Pallas kernels, expert_rows(): pl.pallas_call(functools.partial(expert_kernel, count), grid=(1,), in_spe...  11.9 us
    ppermute x14, waiting for transfers between devices, across(): lax.ppermute(value, 'dp', [(2 * y + c, 2 * y + 1 - c) for y in range(ring...  4.56 us
    convert_element_type x6, other arithmetic, add(): return total.astype(jnp.bfloat16)  3.95 us
  transfers between devices with their start and end apart: 33, of which 18 were waited for; matrix products, arithmetic and copies ran while one was open for 4% of the time, Pallas kernels for 7%

profile of v4, /device:TPU:2, one launch (start us, length us, event | category | flops | bytes accessed | tf_op | source)
XLA Modules:
  0.0 175.3 jit_solution(9923287880938752635)
XLA Ops:
  2.6 28.2 %all_to_all.20 = bf16[32,2,4096]{2,1,0:T(2,128)(2,1)S(1)} all-to-all(bf16[32,2,4096]{2,1,0:T(2,128)(2,1)S(1)} %copy.33), channel_id=1, replica_groups=mesh['dp'=8,'expert'=32] {'expert'}, dimensions={0} | all-to-all | bytes 1048576 | tf_op jit(solution)/shard_map/all_to_all | solution.py:102
  32.2 5.6 %all-to-all-start.1 = ((bf16[32,2,4096]{2,1,0:T(2,128)(2,1)}), bf16[32,2,4096]{2,1,0:T(2,128)(2,1)}, u32[]{:S(2)}, u32[]{:S(2)}) async-start(bf16[32,2,4096]{2,1,0:T(2,128)(2,1)} %copy.34), calls=%async_computation.1 | async-start | bytes 1048576 | tf_op jit(solution)/shard_map/all_to_all | solution.py:102
  38.0 1.7 collective-permute-start.3
  39.7 1.7 collective-permute-start.2
  41.4 10.2 %collective-permute-done.3.refs_2_ = bf16[64,4096]{1,0:T(8,128)(2,1)S(1)} collective-permute-done((bf16[64,4096]{1,0:T(8,128)(2,1)S(1)}, bf16[64,4096]{1,0:T(8,128)(2,1)S(1)}, u32[]{:S(2)}, u32[]{:S(2)}) %collective-permute-start.3) | collective-permute-done | bytes 524320 | tf_op jit(solution)/shard_map/ppermute | solution.py:72
  52.7 2.9 %collective-permute-start.5 = (bf16[32,4096]{1,0:T(8,128)(2,1)}, bf16[32,4096]{1,0:T(8,128)(2,1)}, u32[]{:S(2)}, u32[]{:S(2)}) collective-permute-start(bf16[32,4096]{1,0:T(8,128)(2,1)} %slice.121), channel_id=1, source_target_pairs={{0,192},{32,224},{64,0},{96,32},{128,64},{160,96},{192,128},{224,1... | collective-permute-start | bytes 786440 | tf_op jit(solution)/shard_map/ppermute | solution.py:72
  55.6 3.6 %collective-permute-done.4.refs_3_ = bf16[32,4096]{1,0:T(8,128)(2,1)S(1)} collective-permute-done((bf16[32,4096]{1,0:T(8,128)(2,1)S(1)}, bf16[32,4096]{1,0:T(8,128)(2,1)S(1)}, u32[]{:S(2)}, u32[]{:S(2)}) %collective-permute-start.4) | collective-permute-done | bytes 262176 | tf_op jit(solution)/shard_map/ppermute | solution.py:72
  63.2 1.7 collective-permute-done.7.refs_6_
  64.9 6.1 %shard_map.64 = (bf16[256,4096]{1,0:T(8,128)(2,1)S(1)}, bf16[64,4096]{1,0:T(8,128)(2,1)S(1)}, bf16[192,4096]{1,0:T(8,128)(2,1)S(1)}) custom-call(bf16[64,4096]{1,0:T(8,128)(2,1)S(1)} %reshape.62.refs_0_, bf16[64,4096]{1,0:T(8,128)(2,1)S(1)} %collective-permute-done.2.refs_1_, bf16[64,4096]{1,0:T(8,128)(2,1)S(1)} %collective-permute-done.3.refs_2_, ...), custom_call_target="tpu_custom_call" | custom-call | flops 2415919104 | bytes 13107200 | tf_op jit(solution)/shard_map/pallas_call | solution.py:38
  71.0 4.4 %collective-permute-done.1.refs_1_ = bf16[64,4096]{1,0:T(8,128)(2,1)S(1)} collective-permute-done((bf16[64,4096]{1,0:T(8,128)(2,1)S(1)}, bf16[64,4096]{1,0:T(8,128)(2,1)S(1)}, u32[]{:S(2)}, u32[]{:S(2)}) %collective-permute-start.1) | collective-permute-done | bytes 524320 | tf_op jit(solution)/shard_map/ppermute | solution.py:72
  77.8 1.7 collective-permute-start.12
  81.8 4.9 %collective-permute-done.13.refs_4_ = bf16[32,4096]{1,0:T(8,128)(2,1)S(1)} collective-permute-done((bf16[32,4096]{1,0:T(8,128)(2,1)S(1)}, bf16[32,4096]{1,0:T(8,128)(2,1)S(1)}, u32[]{:S(2)}, u32[]{:S(2)}) %collective-permute-start.13) | collective-permute-done | bytes 262176 | tf_op jit(solution)/shard_map/ppermute | solution.py:72
  88.3 3.1 %collective-permute-done.16 = bf16[32,4096]{1,0:T(8,128)(2,1)S(1)} collective-permute-done((bf16[32,4096]{1,0:T(8,128)(2,1)S(1)}, bf16[32,4096]{1,0:T(8,128)(2,1)S(1)}, u32[]{:S(2)}, u32[]{:S(2)}) %collective-permute-start.16) | collective-permute-done | bytes 262176 | tf_op jit(solution)/shard_map/ppermute | solution.py:72
  93.3 1.8 %collective-permute-start.17 = (bf16[64,4096]{1,0:T(8,128)(2,1)S(1)}, bf16[64,4096]{1,0:T(8,128)(2,1)S(1)}, u32[]{:S(2)}, u32[]{:S(2)}) collective-permute-start(bf16[64,4096]{1,0:T(8,128)(2,1)S(1)} %get-tuple-element.62), channel_id=1, source_target_pairs={{0,64},{32,96},{64,128},{96,160},{128,192},{160,224},{192,0},{224,... | collective-permute-start | bytes 1572872 | tf_op jit(solution)/shard_map/ppermute | solution.py:72
  97.1 5.8 %shard_map.65 = (bf16[256,4096]{1,0:T(8,128)(2,1)S(1)}, bf16[64,4096]{1,0:T(8,128)(2,1)S(1)}, bf16[192,4096]{1,0:T(8,128)(2,1)S(1)}) custom-call(bf16[64,4096]{1,0:T(8,128)(2,1)S(1)} %reshape.61.refs_0_, bf16[64,4096]{1,0:T(8,128)(2,1)S(1)} %collective-permute-done.1.refs_1_, bf16[64,4096]{1,0:T(8,128)(2,1)S(1)} %collective-permute-done.refs_2_, ...), custom_call_target="tpu_custom_call" | custom-call | flops 2415919104 | bytes 13107200 | tf_op jit(solution)/shard_map/pallas_call | solution.py:38
  102.9 3.3 %collective-permute-done.18 = bf16[64,4096]{1,0:T(8,128)(2,1)S(1)} collective-permute-done((bf16[64,4096]{1,0:T(8,128)(2,1)S(1)}, bf16[64,4096]{1,0:T(8,128)(2,1)S(1)}, u32[]{:S(2)}, u32[]{:S(2)}) %collective-permute-start.18) | collective-permute-done | bytes 524320 | tf_op jit(solution)/shard_map/ppermute | solution.py:72
  106.2 2.4 %collective-permute-done.17 = bf16[64,4096]{1,0:T(8,128)(2,1)S(1)} collective-permute-done((bf16[64,4096]{1,0:T(8,128)(2,1)S(1)}, bf16[64,4096]{1,0:T(8,128)(2,1)S(1)}, u32[]{:S(2)}, u32[]{:S(2)}) %collective-permute-start.17) | collective-permute-done | bytes 524320 | tf_op jit(solution)/shard_map/ppermute | solution.py:72
  110.7 3.2 %collective-permute-start.28 = (bf16[32,4096]{1,0:T(8,128)(2,1)S(1)}, bf16[32,4096]{1,0:T(8,128)(2,1)S(1)}, u32[]{:S(2)}, u32[]{:S(2)}) collective-permute-start(bf16[32,4096]{1,0:T(8,128)(2,1)S(1)} %get-tuple-element.64), channel_id=1, source_target_pairs={{0,192},{32,224},{64,0},{96,32},{128,64},{160,96},{192,128},{224,1... | collective-permute-start | bytes 786440 | tf_op jit(solution)/shard_map/ppermute | solution.py:72
  114.0 6.3 %collective-permute-done.26 = bf16[32,4096]{1,0:T(8,128)(2,1)S(1)} collective-permute-done((bf16[32,4096]{1,0:T(8,128)(2,1)S(1)}, bf16[32,4096]{1,0:T(8,128)(2,1)S(1)}, u32[]{:S(2)}, u32[]{:S(2)}) %collective-permute-start.26) | collective-permute-done | bytes 262176 | tf_op jit(solution)/shard_map/ppermute | solution.py:72
  121.8 3.2 %collective-permute-start.29 = (bf16[64,4096]{1,0:T(8,128)(2,1)}, bf16[64,4096]{1,0:T(8,128)(2,1)}, u32[]{:S(2)}, u32[]{:S(2)}) collective-permute-start(bf16[64,4096]{1,0:T(8,128)(2,1)} %get-tuple-element.60), channel_id=1, source_target_pairs={{0,192},{32,224},{64,0},{96,32},{128,64},{160,96},{192,128},{224,1... | collective-permute-start | bytes 1572872 | tf_op jit(solution)/shard_map/ppermute | solution.py:72
  126.4 9.8 %all-to-all-start.2 = ((bf16[32,2,4096]{2,1,0:T(2,128)(2,1)}), bf16[32,2,4096]{2,1,0:T(2,128)(2,1)S(1)}, u32[]{:S(2)}, u32[]{:S(2)}) async-start(bf16[32,2,4096]{2,1,0:T(2,128)(2,1)} %reshape.64), calls=%async_computation.2 | async-start | bytes 1048576 | tf_op jit(solution)/shard_map/all_to_all | solution.py:102
  138.7 13.2 %all-to-all-done.2 = bf16[32,2,4096]{2,1,0:T(2,128)(2,1)S(1)} async-done(((bf16[32,2,4096]{2,1,0:T(2,128)(2,1)}), bf16[32,2,4096]{2,1,0:T(2,128)(2,1)S(1)}, u32[]{:S(2)}, u32[]{:S(2)}) %all-to-all-start.2) | async-done | bytes 524320 | tf_op jit(solution)/shard_map/all_to_all | solution.py:102
  153.1 5.6 %all-to-all-start.3 = ((bf16[32,2,4096]{2,1,0:T(2,128)(2,1)}), bf16[32,2,4096]{2,1,0:T(2,128)(2,1)S(1)}, u32[]{:S(2)}, u32[]{:S(2)}) async-start(bf16[32,2,4096]{2,1,0:T(2,128)(2,1)} %reshape.65), calls=%async_computation.3 | async-start | bytes 1048576 | tf_op jit(solution)/shard_map/all_to_all | solution.py:102
  159.5 14.7 %all-to-all-done.3 = bf16[32,2,4096]{2,1,0:T(2,128)(2,1)S(1)} async-done(((bf16[32,2,4096]{2,1,0:T(2,128)(2,1)}), bf16[32,2,4096]{2,1,0:T(2,128)(2,1)S(1)}, u32[]{:S(2)}, u32[]{:S(2)}) %all-to-all-start.3) | async-done | bytes 524320 | tf_op jit(solution)/shard_map/all_to_all | solution.py:102
  (93 shorter events, 29.6 us)
Async XLA Ops:
  32.2 27.6 %all-to-all-start.1 = ((bf16[32,2,4096]{2,1,0:T(2,128)(2,1)}), bf16[32,2,4096]{2,1,0:T(2,128)(2,1)}, u32[]{:S(2)}, u32[]{:S(2)}) async-start(bf16[32,2,4096]{2,1,0:T(2,128)(2,1)} %copy.34), calls=%async_computation.1 | async-start | bytes 1048576 | tf_op jit(solution)/shard_map/all_to_all | solution.py:102
  38.0 13.6 %collective-permute-start.3 = (bf16[64,4096]{1,0:T(8,128)(2,1)S(1)}, bf16[64,4096]{1,0:T(8,128)(2,1)S(1)}, u32[]{:S(2)}, u32[]{:S(2)}) collective-permute-start(bf16[64,4096]{1,0:T(8,128)(2,1)S(1)} %reshape.62.refs_0_), channel_id=1, source_target_pairs={{0,64},{32,96},{64,128},{96,160},{128,192},{160,224},{192,0},{224,... | collective-permute-start | bytes 1572872 | tf_op jit(solution)/shard_map/ppermute | solution.py:72
  39.7 12.3 %collective-permute-start.2 = (bf16[64,4096]{1,0:T(8,128)(2,1)S(1)}, bf16[64,4096]{1,0:T(8,128)(2,1)S(1)}, u32[]{:S(2)}, u32[]{:S(2)}) collective-permute-start(bf16[64,4096]{1,0:T(8,128)(2,1)S(1)} %reshape.62.refs_0_), channel_id=1, source_target_pairs={{0,192},{32,224},{64,0},{96,32},{128,64},{160,96},{192,128},{224,1... | collective-permute-start | bytes 1572872 | tf_op jit(solution)/shard_map/ppermute | solution.py:72
  41.4 19.7 %collective-permute-start.8 = (bf16[64,4096]{1,0:T(8,128)(2,1)S(1)}, bf16[64,4096]{1,0:T(8,128)(2,1)S(1)}, u32[]{:S(2)}, u32[]{:S(2)}) collective-permute-start(bf16[64,4096]{1,0:T(8,128)(2,1)S(1)} %reshape.62.refs_0_), channel_id=1, source_target_pairs={{0,32},{32,0},{64,96},{96,64},{128,160},{160,128},{192,224},{224,1... | collective-permute-start | bytes 1572872 | tf_op jit(solution)/shard_map/ppermute | solution.py:79
  51.6 7.7 %collective-permute-start.4 = (bf16[32,4096]{1,0:T(8,128)(2,1)S(1)}, bf16[32,4096]{1,0:T(8,128)(2,1)S(1)}, u32[]{:S(2)}, u32[]{:S(2)}) collective-permute-start(bf16[32,4096]{1,0:T(8,128)(2,1)S(1)} %slice.120), channel_id=1, source_target_pairs={{0,64},{32,96},{64,128},{96,160},{128,192},{160,224},{192,0},{224,... | collective-permute-start | bytes 786440 | tf_op jit(solution)/shard_map/ppermute | solution.py:72
  52.7 9.0 %collective-permute-start.5 = (bf16[32,4096]{1,0:T(8,128)(2,1)}, bf16[32,4096]{1,0:T(8,128)(2,1)}, u32[]{:S(2)}, u32[]{:S(2)}) collective-permute-start(bf16[32,4096]{1,0:T(8,128)(2,1)} %slice.121), channel_id=1, source_target_pairs={{0,192},{32,224},{64,0},{96,32},{128,64},{160,96},{192,128},{224,1... | collective-permute-start | bytes 786440 | tf_op jit(solution)/shard_map/ppermute | solution.py:72
  61.0 14.4 %collective-permute-start.1 = (bf16[64,4096]{1,0:T(8,128)(2,1)S(1)}, bf16[64,4096]{1,0:T(8,128)(2,1)S(1)}, u32[]{:S(2)}, u32[]{:S(2)}) collective-permute-start(bf16[64,4096]{1,0:T(8,128)(2,1)S(1)} %reshape.61.refs_0_), channel_id=1, source_target_pairs={{0,192},{32,224},{64,0},{96,32},{128,64},{160,96},{192,128},{224,1... | collective-permute-start | bytes 1572872 | tf_op jit(solution)/shard_map/ppermute | solution.py:72
  61.7 15.3 %collective-permute-start = (bf16[64,4096]{1,0:T(8,128)(2,1)S(1)}, bf16[64,4096]{1,0:T(8,128)(2,1)S(1)}, u32[]{:S(2)}, u32[]{:S(2)}) collective-permute-start(bf16[64,4096]{1,0:T(8,128)(2,1)S(1)} %reshape.61.refs_0_), channel_id=1, source_target_pairs={{0,64},{32,96},{64,128},{96,160},{128,192},{160,224},{192,0},{224,... | collective-permute-start | bytes 1572872 | tf_op jit(solution)/shard_map/ppermute | solution.py:72
  76.9 15.8 %collective-permute-start.11 = (bf16[192,4096]{1,0:T(8,128)(2,1)S(1)}, bf16[192,4096]{1,0:T(8,128)(2,1)S(1)}, u32[]{:S(2)}, u32[]{:S(2)}) collective-permute-start(bf16[192,4096]{1,0:T(8,128)(2,1)S(1)} %get-tuple-element.39), channel_id=1, source_target_pairs={{0,32},{32,0},{64,96},{96,64},{128,160},{160,128},{192,224},{224,1... | collective-permute-start | bytes 4718600 | tf_op jit(solution)/shard_map/ppermute | solution.py:79
  77.5 9.3 %collective-permute-start.13 = (bf16[32,4096]{1,0:T(8,128)(2,1)S(1)}, bf16[32,4096]{1,0:T(8,128)(2,1)S(1)}, u32[]{:S(2)}, u32[]{:S(2)}) collective-permute-start(bf16[32,4096]{1,0:T(8,128)(2,1)S(1)} %slice.97), channel_id=1, source_target_pairs={{0,192},{32,224},{64,0},{96,32},{128,64},{160,96},{192,128},{224,1... | collective-permute-start | bytes 786440 | tf_op jit(solution)/shard_map/ppermute | solution.py:72
  77.8 10.4 %collective-permute-start.12 = (bf16[32,4096]{1,0:T(8,128)(2,1)S(1)}, bf16[32,4096]{1,0:T(8,128)(2,1)S(1)}, u32[]{:S(2)}, u32[]{:S(2)}) collective-permute-start(bf16[32,4096]{1,0:T(8,128)(2,1)S(1)} %slice.96), channel_id=1, source_target_pairs={{0,64},{32,96},{64,128},{96,160},{128,192},{160,224},{192,0},{224,... | collective-permute-start | bytes 786440 | tf_op jit(solution)/shard_map/ppermute | solution.py:72
  79.7 11.7 %collective-permute-start.16 = (bf16[32,4096]{1,0:T(8,128)(2,1)S(1)}, bf16[32,4096]{1,0:T(8,128)(2,1)S(1)}, u32[]{:S(2)}, u32[]{:S(2)}) collective-permute-start(bf16[32,4096]{1,0:T(8,128)(2,1)S(1)} %get-tuple-element.65), channel_id=1, source_target_pairs={{0,192},{32,224},{64,0},{96,32},{128,64},{160,96},{192,128},{224,1... | collective-permute-start | bytes 786440 | tf_op jit(solution)/shard_map/ppermute | solution.py:72
  81.3 11.4 %collective-permute-start.15 = (bf16[32,4096]{1,0:T(8,128)(2,1)S(1)}, bf16[32,4096]{1,0:T(8,128)(2,1)S(1)}, u32[]{:S(2)}, u32[]{:S(2)}) collective-permute-start(bf16[32,4096]{1,0:T(8,128)(2,1)S(1)} %get-tuple-element.66), channel_id=1, source_target_pairs={{0,64},{32,96},{64,128},{96,160},{128,192},{160,224},{192,0},{224,... | collective-permute-start | bytes 786440 | tf_op jit(solution)/shard_map/ppermute | solution.py:72
  86.7 8.4 %collective-permute-start.21 = (bf16[64,4096]{1,0:T(8,128)(2,1)S(1)}, bf16[64,4096]{1,0:T(8,128)(2,1)S(1)}, u32[]{:S(2)}, u32[]{:S(2)}) collective-permute-start(bf16[64,4096]{1,0:T(8,128)(2,1)S(1)} %reshape.61.refs_0_), channel_id=1, source_target_pairs={{0,32},{32,0},{64,96},{96,64},{128,160},{160,128},{192,224},{224,1... | collective-permute-start | bytes 1572872 | tf_op jit(solution)/shard_map/ppermute | solution.py:79
  88.3 6.9 %collective-permute-start.23 = (bf16[64,4096]{1,0:T(8,128)(2,1)S(1)}, bf16[64,4096]{1,0:T(8,128)(2,1)S(1)}, u32[]{:S(2)}, u32[]{:S(2)}) collective-permute-start(bf16[64,4096]{1,0:T(8,128)(2,1)S(1)} %collective-permute-done.refs_2_), channel_id=1, source_target_pairs={{0,32},{32,0},{64,96},{96,64},{128,160},{160,128},{192,224},{224,1... | collective-permute-start | bytes 1572872 | tf_op jit(solution)/shard_map/ppermute | solution.py:79
  93.1 13.1 %collective-permute-start.18 = (bf16[64,4096]{1,0:T(8,128)(2,1)S(1)}, bf16[64,4096]{1,0:T(8,128)(2,1)S(1)}, u32[]{:S(2)}, u32[]{:S(2)}) collective-permute-start(bf16[64,4096]{1,0:T(8,128)(2,1)S(1)} %get-tuple-element.61), channel_id=1, source_target_pairs={{0,192},{32,224},{64,0},{96,32},{128,64},{160,96},{192,128},{224,1... | collective-permute-start | bytes 1572872 | tf_op jit(solution)/shard_map/ppermute | solution.py:72
  93.3 15.3 %collective-permute-start.17 = (bf16[64,4096]{1,0:T(8,128)(2,1)S(1)}, bf16[64,4096]{1,0:T(8,128)(2,1)S(1)}, u32[]{:S(2)}, u32[]{:S(2)}) collective-permute-start(bf16[64,4096]{1,0:T(8,128)(2,1)S(1)} %get-tuple-element.62), channel_id=1, source_target_pairs={{0,64},{32,96},{64,128},{96,160},{128,192},{160,224},{192,0},{224,... | collective-permute-start | bytes 1572872 | tf_op jit(solution)/shard_map/ppermute | solution.py:72
  108.6 11.7 %collective-permute-start.24 = (bf16[192,4096]{1,0:T(8,128)(2,1)S(1)}, bf16[192,4096]{1,0:T(8,128)(2,1)S(1)}, u32[]{:S(2)}, u32[]{:S(2)}) collective-permute-start(bf16[192,4096]{1,0:T(8,128)(2,1)S(1)} %get-tuple-element.56), channel_id=1, source_target_pairs={{0,32},{32,0},{64,96},{96,64},{128,160},{160,128},{192,224},{224,1... | collective-permute-start | bytes 4718600 | tf_op jit(solution)/shard_map/ppermute | solution.py:79
  110.6 9.6 %collective-permute-start.26 = (bf16[32,4096]{1,0:T(8,128)(2,1)S(1)}, bf16[32,4096]{1,0:T(8,128)(2,1)S(1)}, u32[]{:S(2)}, u32[]{:S(2)}) collective-permute-start(bf16[32,4096]{1,0:T(8,128)(2,1)S(1)} %get-tuple-element.63), channel_id=1, source_target_pairs={{0,64},{32,96},{64,128},{96,160},{128,192},{160,224},{192,0},{224,... | collective-permute-start | bytes 786440 | tf_op jit(solution)/shard_map/ppermute | solution.py:72
  110.7 9.5 %collective-permute-start.28 = (bf16[32,4096]{1,0:T(8,128)(2,1)S(1)}, bf16[32,4096]{1,0:T(8,128)(2,1)S(1)}, u32[]{:S(2)}, u32[]{:S(2)}) collective-permute-start(bf16[32,4096]{1,0:T(8,128)(2,1)S(1)} %get-tuple-element.64), channel_id=1, source_target_pairs={{0,192},{32,224},{64,0},{96,32},{128,64},{160,96},{192,128},{224,1... | collective-permute-start | bytes 786440 | tf_op jit(solution)/shard_map/ppermute | solution.py:72
  121.8 14.6 %collective-permute-start.27 = (bf16[64,4096]{1,0:T(8,128)(2,1)}, bf16[64,4096]{1,0:T(8,128)(2,1)S(1)}, u32[]{:S(2)}, u32[]{:S(2)}) collective-permute-start(bf16[64,4096]{1,0:T(8,128)(2,1)} %get-tuple-element.59), channel_id=1, source_target_pairs={{0,64},{32,96},{64,128},{96,160},{128,192},{160,224},{192,0},{224,... | collective-permute-start | bytes 1572872 | tf_op jit(solution)/shard_map/ppermute | solution.py:72
  121.8 15.3 %collective-permute-start.29 = (bf16[64,4096]{1,0:T(8,128)(2,1)}, bf16[64,4096]{1,0:T(8,128)(2,1)}, u32[]{:S(2)}, u32[]{:S(2)}) collective-permute-start(bf16[64,4096]{1,0:T(8,128)(2,1)} %get-tuple-element.60), channel_id=1, source_target_pairs={{0,192},{32,224},{64,0},{96,32},{128,64},{160,96},{192,128},{224,1... | collective-permute-start | bytes 1572872 | tf_op jit(solution)/shard_map/ppermute | solution.py:72
  126.4 25.5 %all-to-all-start.2 = ((bf16[32,2,4096]{2,1,0:T(2,128)(2,1)}), bf16[32,2,4096]{2,1,0:T(2,128)(2,1)S(1)}, u32[]{:S(2)}, u32[]{:S(2)}) async-start(bf16[32,2,4096]{2,1,0:T(2,128)(2,1)} %reshape.64), calls=%async_computation.2 | async-start | bytes 1048576 | tf_op jit(solution)/shard_map/all_to_all | solution.py:102
  153.1 21.2 %all-to-all-start.3 = ((bf16[32,2,4096]{2,1,0:T(2,128)(2,1)}), bf16[32,2,4096]{2,1,0:T(2,128)(2,1)S(1)}, u32[]{:S(2)}, u32[]{:S(2)}) async-start(bf16[32,2,4096]{2,1,0:T(2,128)(2,1)} %reshape.65), calls=%async_computation.3 | async-start | bytes 1048576 | tf_op jit(solution)/shard_map/all_to_all | solution.py:102
  (13 other events, 54.8 us)

commit v5 on v4

--- a/solution.py
+++ b/solution.py
@@ -157,16 +157,16 @@
 
     before1, after1 = along_ring(own1, 1), along_ring(own1, -1)
     kept0, outer0, inner0 = experts(0, own0, after0, before0, *facing0)
-    before1, after1, kept0, outer0, inner0 = tie((before1, after1, kept0, outer0, inner0))
+    outer0, inner0 = across(outer0), across(inner0)
+    before1, after1, kept0 = tie((before1, after1, kept0))
     facing1 = facing(before1, after1)
-    out0 = outward(kept0, across(outer0))
-    inner0 = across(inner0)
+    out0 = outward(kept0, outer0)
     facing1, out0 = tie((facing1, out0))
     home0 = homeward(kept0, inner0, *out0)
     kept1, outer1, inner1 = experts(1, own1, after1, before1, *facing1)
-    home0, kept1, outer1, inner1 = tie((home0, kept1, outer1, inner1))
-    out1 = outward(kept1, across(outer1))
-    inner1 = across(inner1)
+    outer1, inner1 = across(outer1), across(inner1)
+    home0, kept1 = tie((home0, kept1))
+    out1 = outward(kept1, outer1)
     back0 = returned(kept0, inner0, home0)
     home1 = homeward(kept1, inner1, *out1)
     back1 = returned(kept1, inner1, home1, back0)

time: 176 us -> 165 us (0.938)
  waiting for transfers between devices: 75.3 us -> 62.9 us
  starting transfers between devices: 44.6 us -> 46.5 us
    ppermute x16, waiting for transfers between devices: 42.8 us -> 33.3 us  [along_ring(): lax.ppermute(value, 'dp', [(2 * y + c, 2 * ((y + step) % ring) + c) for y...]
    ppermute x14, waiting for transfers between devices: 4.56 us -> 0.04 us  [across(): lax.ppermute(value, 'dp', [(2 * y + c, 2 * y + 1 - c) for y in range(ring...]
  transfers between devices with their start and end apart: 33 -> 33, of which waited for: 18 -> 14; matrix products, arithmetic and copies ran while one was open for 4% -> 4% of each run, Pallas kernels for 7% -> 7%
where the time goes in v5:
time: 165 us; the launch traced here: 164 us
  waiting for transfers between devices  62.9 us (38%)
  starting transfers between devices  46.5 us (28%)
  blocking collectives  28.2 us (17%)
  Pallas kernels  12 us (7%)
  local copies, waits for them, and re-layouts  7.2 us (4%)
  other arithmetic  4.96 us (3%)
  matrix products  2.11 us (1%)
    ppermute x16, waiting for transfers between devices, along_ring(): lax.ppermute(value, 'dp', [(2 * y + c, 2 * ((y + step) % ring) + c) for y...  33.3 us
    all_to_all x3, waiting for transfers between devices, columns(): lax.all_to_all(value, 'expert', split_axis=0, concat_axis=0, tiled=True)  29.5 us
    all_to_all x1, blocking collectives, columns(): lax.all_to_all(value, 'expert', split_axis=0, concat_axis=0, tiled=True)  28.2 us
    all_to_all x3, starting transfers between devices, columns(): lax.all_to_all(value, 'expert', split_axis=0, concat_axis=0, tiled=True)  22.1 us
    ppermute x16, starting transfers between devices, along_ring(): lax.ppermute(value, 'dp', [(2 * y + c, 2 * ((y + step) % ring) + c) for y...  21.7 us
    pallas_call x2, Pallas kernels, expert_rows(): pl.pallas_call(functools.partial(expert_kernel, count), grid=(1,), in_spe...  12 us
    convert_element_type x6, other arithmetic, add(): return total.astype(jnp.bfloat16)  3.95 us
  transfers between devices with their start and end apart: 33, of which 14 were waited for; matrix products, arithmetic and copies ran while one was open for 4% of the time, Pallas kernels for 7%

profile of v5, /device:TPU:2, one launch (start us, length us, event | category | flops | bytes accessed | tf_op | source)
XLA Modules:
  0.0 164.2 jit_solution(584930511875995206)
XLA Ops:
  2.6 28.2 %all_to_all.20 = bf16[32,2,4096]{2,1,0:T(2,128)(2,1)S(1)} all-to-all(bf16[32,2,4096]{2,1,0:T(2,128)(2,1)S(1)} %copy.33), channel_id=1, replica_groups=mesh['dp'=8,'expert'=32] {'expert'}, dimensions={0} | all-to-all | bytes 1048576 | tf_op jit(solution)/shard_map/all_to_all | solution.py:102
  35.7 5.6 %all-to-all-start.1 = ((bf16[32,2,4096]{2,1,0:T(2,128)(2,1)}), bf16[32,2,4096]{2,1,0:T(2,128)(2,1)}, u32[]{:S(2)}, u32[]{:S(2)}) async-start(bf16[32,2,4096]{2,1,0:T(2,128)(2,1)} %copy.34), calls=%async_computation.1 | async-start | bytes 1048576 | tf_op jit(solution)/shard_map/all_to_all | solution.py:102
  41.4 3.4 %collective-permute-done.3.refs_2_ = bf16[64,4096]{1,0:T(8,128)(2,1)S(1)} collective-permute-done((bf16[64,4096]{1,0:T(8,128)(2,1)S(1)}, bf16[64,4096]{1,0:T(8,128)(2,1)S(1)}, u32[]{:S(2)}, u32[]{:S(2)}) %collective-permute-start.3) | collective-permute-done | bytes 524320 | tf_op jit(solution)/shard_map/ppermute | solution.py:72
  45.3 3.0 %collective-permute-start.5 = (bf16[32,4096]{1,0:T(8,128)(2,1)S(1)}, bf16[32,4096]{1,0:T(8,128)(2,1)}, u32[]{:S(2)}, u32[]{:S(2)}) collective-permute-start(bf16[32,4096]{1,0:T(8,128)(2,1)S(1)} %slice.121), channel_id=1, source_target_pairs={{0,192},{32,224},{64,0},{96,32},{128,64},{160,96},{192,128},{224,1... | collective-permute-start | bytes 786440 | tf_op jit(solution)/shard_map/ppermute | solution.py:72
  48.8 3.7 %collective-permute-done.4.refs_3_ = bf16[32,4096]{1,0:T(8,128)(2,1)S(1)} collective-permute-done((bf16[32,4096]{1,0:T(8,128)(2,1)S(1)}, bf16[32,4096]{1,0:T(8,128)(2,1)S(1)}, u32[]{:S(2)}, u32[]{:S(2)}) %collective-permute-start.4) | collective-permute-done | bytes 262176 | tf_op jit(solution)/shard_map/ppermute | solution.py:72
  53.0 3.9 %all-to-all-done.1 = bf16[32,2,4096]{2,1,0:T(2,128)(2,1)} async-done(((bf16[32,2,4096]{2,1,0:T(2,128)(2,1)}), bf16[32,2,4096]{2,1,0:T(2,128)(2,1)}, u32[]{:S(2)}, u32[]{:S(2)}) %all-to-all-start.1) | async-done | bytes 524320 | tf_op jit(solution)/shard_map/all_to_all | solution.py:102
  58.2 1.7 %collective-permute-start.1 = (bf16[64,4096]{1,0:T(8,128)(2,1)S(1)}, bf16[64,4096]{1,0:T(8,128)(2,1)S(1)}, u32[]{:S(2)}, u32[]{:S(2)}) collective-permute-start(bf16[64,4096]{1,0:T(8,128)(2,1)S(1)} %reshape.61.refs_0_), channel_id=1, source_target_pairs={{0,192},{32,224},{64,0},{96,32},{128,64},{160,96},{192,128},{224,1... | collective-permute-start | bytes 1572872 | tf_op jit(solution)/shard_map/ppermute | solution.py:72
  60.3 6.2 %shard_map.64 = (bf16[256,4096]{1,0:T(8,128)(2,1)S(1)}, bf16[64,4096]{1,0:T(8,128)(2,1)S(1)}, bf16[192,4096]{1,0:T(8,128)(2,1)S(1)}) custom-call(bf16[64,4096]{1,0:T(8,128)(2,1)S(1)} %reshape.62.refs_0_, bf16[64,4096]{1,0:T(8,128)(2,1)S(1)} %collective-permute-done.2.refs_1_, bf16[64,4096]{1,0:T(8,128)(2,1)S(1)} %collective-permute-done.3.refs_2_, ...), custom_call_target="tpu_custom_call" | custom-call | flops 2415919104 | bytes 13107200 | tf_op jit(solution)/shard_map/pallas_call | solution.py:38
  67.1 2.1 %collective-permute-done.1.refs_1_ = bf16[64,4096]{1,0:T(8,128)(2,1)S(1)} collective-permute-done((bf16[64,4096]{1,0:T(8,128)(2,1)S(1)}, bf16[64,4096]{1,0:T(8,128)(2,1)S(1)}, u32[]{:S(2)}, u32[]{:S(2)}) %collective-permute-start.1) | collective-permute-done | bytes 524320 | tf_op jit(solution)/shard_map/ppermute | solution.py:72
  69.2 3.4 %collective-permute-done.refs_2_ = bf16[64,4096]{1,0:T(8,128)(2,1)S(1)} collective-permute-done((bf16[64,4096]{1,0:T(8,128)(2,1)S(1)}, bf16[64,4096]{1,0:T(8,128)(2,1)S(1)}, u32[]{:S(2)}, u32[]{:S(2)}) %collective-permute-start) | collective-permute-done | bytes 524320 | tf_op jit(solution)/shard_map/ppermute | solution.py:72
  73.0 1.7 %collective-permute-start.12 = (bf16[32,4096]{1,0:T(8,128)(2,1)S(1)}, bf16[32,4096]{1,0:T(8,128)(2,1)S(1)}, u32[]{:S(2)}, u32[]{:S(2)}) collective-permute-start(bf16[32,4096]{1,0:T(8,128)(2,1)S(1)} %slice.96), channel_id=1, source_target_pairs={{0,64},{32,96},{64,128},{96,160},{128,192},{160,224},{192,0},{224,... | collective-permute-start | bytes 786440 | tf_op jit(solution)/shard_map/ppermute | solution.py:72
  77.0 3.5 %collective-permute-done.13.refs_4_ = bf16[32,4096]{1,0:T(8,128)(2,1)S(1)} collective-permute-done((bf16[32,4096]{1,0:T(8,128)(2,1)S(1)}, bf16[32,4096]{1,0:T(8,128)(2,1)S(1)}, u32[]{:S(2)}, u32[]{:S(2)}) %collective-permute-start.13) | collective-permute-done | bytes 262176 | tf_op jit(solution)/shard_map/ppermute | solution.py:72
  80.5 1.8 %collective-permute-done.12.refs_3_ = bf16[32,4096]{1,0:T(8,128)(2,1)S(1)} collective-permute-done((bf16[32,4096]{1,0:T(8,128)(2,1)S(1)}, bf16[32,4096]{1,0:T(8,128)(2,1)S(1)}, u32[]{:S(2)}, u32[]{:S(2)}) %collective-permute-start.12) | collective-permute-done | bytes 262176 | tf_op jit(solution)/shard_map/ppermute | solution.py:72
  83.3 1.8 %collective-permute-done.15 = bf16[32,4096]{1,0:T(8,128)(2,1)S(1)} collective-permute-done((bf16[32,4096]{1,0:T(8,128)(2,1)S(1)}, bf16[32,4096]{1,0:T(8,128)(2,1)S(1)}, u32[]{:S(2)}, u32[]{:S(2)}) %collective-permute-start.15) | collective-permute-done | bytes 262176 | tf_op jit(solution)/shard_map/ppermute | solution.py:72
  88.0 5.8 %shard_map.65 = (bf16[256,4096]{1,0:T(8,128)(2,1)S(1)}, bf16[64,4096]{1,0:T(8,128)(2,1)S(1)}, bf16[192,4096]{1,0:T(8,128)(2,1)S(1)}) custom-call(bf16[64,4096]{1,0:T(8,128)(2,1)S(1)} %reshape.61.refs_0_, bf16[64,4096]{1,0:T(8,128)(2,1)S(1)} %collective-permute-done.1.refs_1_, bf16[64,4096]{1,0:T(8,128)(2,1)S(1)} %collective-permute-done.refs_2_, ...), custom_call_target="tpu_custom_call" | custom-call | flops 2415919104 | bytes 13107200 | tf_op jit(solution)/shard_map/pallas_call | solution.py:38
  94.4 5.4 %collective-permute-done.18 = bf16[64,4096]{1,0:T(8,128)(2,1)S(1)} collective-permute-done((bf16[64,4096]{1,0:T(8,128)(2,1)S(1)}, bf16[64,4096]{1,0:T(8,128)(2,1)S(1)}, u32[]{:S(2)}, u32[]{:S(2)}) %collective-permute-start.18) | collective-permute-done | bytes 524320 | tf_op jit(solution)/shard_map/ppermute | solution.py:72
  99.8 1.7 %collective-permute-done.17 = bf16[64,4096]{1,0:T(8,128)(2,1)S(1)} collective-permute-done((bf16[64,4096]{1,0:T(8,128)(2,1)S(1)}, bf16[64,4096]{1,0:T(8,128)(2,1)S(1)}, u32[]{:S(2)}, u32[]{:S(2)}) %collective-permute-start.17) | collective-permute-done | bytes 524320 | tf_op jit(solution)/shard_map/ppermute | solution.py:72
  101.8 3.2 %collective-permute-start.28 = (bf16[32,4096]{1,0:T(8,128)(2,1)S(1)}, bf16[32,4096]{1,0:T(8,128)(2,1)S(1)}, u32[]{:S(2)}, u32[]{:S(2)}) collective-permute-start(bf16[32,4096]{1,0:T(8,128)(2,1)S(1)} %get-tuple-element.56), channel_id=1, source_target_pairs={{0,192},{32,224},{64,0},{96,32},{128,64},{160,96},{192,128},{224,1... | collective-permute-start | bytes 786440 | tf_op jit(solution)/shard_map/ppermute | solution.py:72
  105.0 5.5 %collective-permute-done.26 = bf16[32,4096]{1,0:T(8,128)(2,1)S(1)} collective-permute-done((bf16[32,4096]{1,0:T(8,128)(2,1)S(1)}, bf16[32,4096]{1,0:T(8,128)(2,1)S(1)}, u32[]{:S(2)}, u32[]{:S(2)}) %collective-permute-start.26) | collective-permute-done | bytes 262176 | tf_op jit(solution)/shard_map/ppermute | solution.py:72
  112.0 3.2 %collective-permute-start.29 = (bf16[64,4096]{1,0:T(8,128)(2,1)}, bf16[64,4096]{1,0:T(8,128)(2,1)}, u32[]{:S(2)}, u32[]{:S(2)}) collective-permute-start(bf16[64,4096]{1,0:T(8,128)(2,1)} %get-tuple-element.52), channel_id=1, source_target_pairs={{0,192},{32,224},{64,0},{96,32},{128,64},{160,96},{192,128},{224,1... | collective-permute-start | bytes 1572872 | tf_op jit(solution)/shard_map/ppermute | solution.py:72
  116.6 10.9 %all-to-all-start.2 = ((bf16[32,2,4096]{2,1,0:T(2,128)(2,1)}), bf16[32,2,4096]{2,1,0:T(2,128)(2,1)S(1)}, u32[]{:S(2)}, u32[]{:S(2)}) async-start(bf16[32,2,4096]{2,1,0:T(2,128)(2,1)} %reshape.64), calls=%async_computation.2 | async-start | bytes 1048576 | tf_op jit(solution)/shard_map/all_to_all | solution.py:102
  129.9 12.4 %all-to-all-done.2 = bf16[32,2,4096]{2,1,0:T(2,128)(2,1)S(1)} async-done(((bf16[32,2,4096]{2,1,0:T(2,128)(2,1)}), bf16[32,2,4096]{2,1,0:T(2,128)(2,1)S(1)}, u32[]{:S(2)}, u32[]{:S(2)}) %all-to-all-start.2) | async-done | bytes 524320 | tf_op jit(solution)/shard_map/all_to_all | solution.py:102
  143.5 5.6 %all-to-all-start.3 = ((bf16[32,2,4096]{2,1,0:T(2,128)(2,1)}), bf16[32,2,4096]{2,1,0:T(2,128)(2,1)S(1)}, u32[]{:S(2)}, u32[]{:S(2)}) async-start(bf16[32,2,4096]{2,1,0:T(2,128)(2,1)} %reshape.65), calls=%async_computation.3 | async-start | bytes 1048576 | tf_op jit(solution)/shard_map/all_to_all | solution.py:102
  149.9 13.3 %all-to-all-done.3 = bf16[32,2,4096]{2,1,0:T(2,128)(2,1)S(1)} async-done(((bf16[32,2,4096]{2,1,0:T(2,128)(2,1)}), bf16[32,2,4096]{2,1,0:T(2,128)(2,1)S(1)}, u32[]{:S(2)}, u32[]{:S(2)}) %all-to-all-start.3) | async-done | bytes 524320 | tf_op jit(solution)/shard_map/all_to_all | solution.py:102
  (93 shorter events, 26.9 us)
Async XLA Ops:
  31.1 13.8 %collective-permute-start.3 = (bf16[64,4096]{1,0:T(8,128)(2,1)S(1)}, bf16[64,4096]{1,0:T(8,128)(2,1)S(1)}, u32[]{:S(2)}, u32[]{:S(2)}) collective-permute-start(bf16[64,4096]{1,0:T(8,128)(2,1)S(1)} %reshape.62.refs_0_), channel_id=1, source_target_pairs={{0,64},{32,96},{64,128},{96,160},{128,192},{160,224},{192,0},{224,... | collective-permute-start | bytes 1572872 | tf_op jit(solution)/shard_map/ppermute | solution.py:72
  32.7 12.5 %collective-permute-start.2 = (bf16[64,4096]{1,0:T(8,128)(2,1)S(1)}, bf16[64,4096]{1,0:T(8,128)(2,1)S(1)}, u32[]{:S(2)}, u32[]{:S(2)}) collective-permute-start(bf16[64,4096]{1,0:T(8,128)(2,1)S(1)} %reshape.62.refs_0_), channel_id=1, source_target_pairs={{0,192},{32,224},{64,0},{96,32},{128,64},{160,96},{192,128},{224,1... | collective-permute-start | bytes 1572872 | tf_op jit(solution)/shard_map/ppermute | solution.py:72
  35.7 21.2 %all-to-all-start.1 = ((bf16[32,2,4096]{2,1,0:T(2,128)(2,1)}), bf16[32,2,4096]{2,1,0:T(2,128)(2,1)}, u32[]{:S(2)}, u32[]{:S(2)}) async-start(bf16[32,2,4096]{2,1,0:T(2,128)(2,1)} %copy.34), calls=%async_computation.1 | async-start | bytes 1048576 | tf_op jit(solution)/shard_map/all_to_all | solution.py:102
  41.3 16.8 %collective-permute-start.8 = (bf16[64,4096]{1,0:T(8,128)(2,1)S(1)}, bf16[64,4096]{1,0:T(8,128)(2,1)S(1)}, u32[]{:S(2)}, u32[]{:S(2)}) collective-permute-start(bf16[64,4096]{1,0:T(8,128)(2,1)S(1)} %reshape.62.refs_0_), channel_id=1, source_target_pairs={{0,32},{32,0},{64,96},{96,64},{128,160},{160,128},{192,224},{224,1... | collective-permute-start | bytes 1572872 | tf_op jit(solution)/shard_map/ppermute | solution.py:79
  48.3 12.0 %collective-permute-start.10 = (bf16[64,4096]{1,0:T(8,128)(2,1)S(1)}, bf16[64,4096]{1,0:T(8,128)(2,1)S(1)}, u32[]{:S(2)}, u32[]{:S(2)}) collective-permute-start(bf16[64,4096]{1,0:T(8,128)(2,1)S(1)} %collective-permute-done.3.refs_2_), channel_id=1, source_target_pairs={{0,32},{32,0},{64,96},{96,64},{128,160},{160,128},{192,224},{224,1... | collective-permute-start | bytes 1572872 | tf_op jit(solution)/shard_map/ppermute | solution.py:79
  48.3 12.0 %collective-permute-start.9 = (bf16[64,4096]{1,0:T(8,128)(2,1)S(1)}, bf16[64,4096]{1,0:T(8,128)(2,1)}, u32[]{:S(2)}, u32[]{:S(2)}) collective-permute-start(bf16[64,4096]{1,0:T(8,128)(2,1)S(1)} %collective-permute-done.2.refs_1_), channel_id=1, source_target_pairs={{0,32},{32,0},{64,96},{96,64},{128,160},{160,128},{192,224},{224,1... | collective-permute-start | bytes 1572872 | tf_op jit(solution)/shard_map/ppermute | solution.py:79
  58.2 11.0 %collective-permute-start.1 = (bf16[64,4096]{1,0:T(8,128)(2,1)S(1)}, bf16[64,4096]{1,0:T(8,128)(2,1)S(1)}, u32[]{:S(2)}, u32[]{:S(2)}) collective-permute-start(bf16[64,4096]{1,0:T(8,128)(2,1)S(1)} %reshape.61.refs_0_), channel_id=1, source_target_pairs={{0,192},{32,224},{64,0},{96,32},{128,64},{160,96},{192,128},{224,1... | collective-permute-start | bytes 1572872 | tf_op jit(solution)/shard_map/ppermute | solution.py:72
  59.9 12.7 %collective-permute-start = (bf16[64,4096]{1,0:T(8,128)(2,1)S(1)}, bf16[64,4096]{1,0:T(8,128)(2,1)S(1)}, u32[]{:S(2)}, u32[]{:S(2)}) collective-permute-start(bf16[64,4096]{1,0:T(8,128)(2,1)S(1)} %reshape.61.refs_0_), channel_id=1, source_target_pairs={{0,64},{32,96},{64,128},{96,160},{128,192},{160,224},{192,0},{224,... | collective-permute-start | bytes 1572872 | tf_op jit(solution)/shard_map/ppermute | solution.py:72
  66.5 8.2 %collective-permute-start.14 = (bf16[64,4096]{1,0:T(8,128)(2,1)S(1)}, bf16[64,4096]{1,0:T(8,128)(2,1)S(1)}, u32[]{:S(2)}, u32[]{:S(2)}) collective-permute-start(bf16[64,4096]{1,0:T(8,128)(2,1)S(1)} %get-tuple-element.36), channel_id=1, source_target_pairs={{0,32},{32,0},{64,96},{96,64},{128,160},{160,128},{192,224},{224,1... | collective-permute-start | bytes 1572872 | tf_op jit(solution)/shard_map/ppermute | solution.py:79
  66.6 18.4 %collective-permute-start.11 = (bf16[192,4096]{1,0:T(8,128)(2,1)S(1)}, bf16[192,4096]{1,0:T(8,128)(2,1)S(1)}, u32[]{:S(2)}, u32[]{:S(2)}) collective-permute-start(bf16[192,4096]{1,0:T(8,128)(2,1)S(1)} %get-tuple-element.33), channel_id=1, source_target_pairs={{0,32},{32,0},{64,96},{96,64},{128,160},{160,128},{192,224},{224,1... | collective-permute-start | bytes 4718600 | tf_op jit(solution)/shard_map/ppermute | solution.py:79
  72.6 7.8 %collective-permute-start.13 = (bf16[32,4096]{1,0:T(8,128)(2,1)S(1)}, bf16[32,4096]{1,0:T(8,128)(2,1)S(1)}, u32[]{:S(2)}, u32[]{:S(2)}) collective-permute-start(bf16[32,4096]{1,0:T(8,128)(2,1)S(1)} %slice.97), channel_id=1, source_target_pairs={{0,192},{32,224},{64,0},{96,32},{128,64},{160,96},{192,128},{224,1... | collective-permute-start | bytes 786440 | tf_op jit(solution)/shard_map/ppermute | solution.py:72
  73.0 9.2 %collective-permute-start.12 = (bf16[32,4096]{1,0:T(8,128)(2,1)S(1)}, bf16[32,4096]{1,0:T(8,128)(2,1)S(1)}, u32[]{:S(2)}, u32[]{:S(2)}) collective-permute-start(bf16[32,4096]{1,0:T(8,128)(2,1)S(1)} %slice.96), channel_id=1, source_target_pairs={{0,64},{32,96},{64,128},{96,160},{128,192},{160,224},{192,0},{224,... | collective-permute-start | bytes 786440 | tf_op jit(solution)/shard_map/ppermute | solution.py:72
  74.9 8.4 %collective-permute-start.16 = (bf16[32,4096]{1,0:T(8,128)(2,1)S(1)}, bf16[32,4096]{1,0:T(8,128)(2,1)S(1)}, u32[]{:S(2)}, u32[]{:S(2)}) collective-permute-start(bf16[32,4096]{1,0:T(8,128)(2,1)S(1)} %get-tuple-element.57), channel_id=1, source_target_pairs={{0,192},{32,224},{64,0},{96,32},{128,64},{160,96},{192,128},{224,1... | collective-permute-start | bytes 786440 | tf_op jit(solution)/shard_map/ppermute | solution.py:72
  76.4 8.6 %collective-permute-start.15 = (bf16[32,4096]{1,0:T(8,128)(2,1)S(1)}, bf16[32,4096]{1,0:T(8,128)(2,1)S(1)}, u32[]{:S(2)}, u32[]{:S(2)}) collective-permute-start(bf16[32,4096]{1,0:T(8,128)(2,1)S(1)} %get-tuple-element.58), channel_id=1, source_target_pairs={{0,64},{32,96},{64,128},{96,160},{128,192},{160,224},{192,0},{224,... | collective-permute-start | bytes 786440 | tf_op jit(solution)/shard_map/ppermute | solution.py:72
  85.9 13.9 %collective-permute-start.18 = (bf16[64,4096]{1,0:T(8,128)(2,1)S(1)}, bf16[64,4096]{1,0:T(8,128)(2,1)S(1)}, u32[]{:S(2)}, u32[]{:S(2)}) collective-permute-start(bf16[64,4096]{1,0:T(8,128)(2,1)S(1)} %get-tuple-element.53), channel_id=1, source_target_pairs={{0,192},{32,224},{64,0},{96,32},{128,64},{160,96},{192,128},{224,1... | collective-permute-start | bytes 1572872 | tf_op jit(solution)/shard_map/ppermute | solution.py:72
  86.4 15.2 %collective-permute-start.17 = (bf16[64,4096]{1,0:T(8,128)(2,1)S(1)}, bf16[64,4096]{1,0:T(8,128)(2,1)S(1)}, u32[]{:S(2)}, u32[]{:S(2)}) collective-permute-start(bf16[64,4096]{1,0:T(8,128)(2,1)S(1)} %get-tuple-element.54), channel_id=1, source_target_pairs={{0,64},{32,96},{64,128},{96,160},{128,192},{160,224},{192,0},{224,... | collective-permute-start | bytes 1572872 | tf_op jit(solution)/shard_map/ppermute | solution.py:72
  93.8 7.7 %collective-permute-start.25 = (bf16[64,4096]{1,0:T(8,128)(2,1)S(1)}, bf16[64,4096]{1,0:T(8,128)(2,1)S(1)}, u32[]{:S(2)}, u32[]{:S(2)}) collective-permute-start(bf16[64,4096]{1,0:T(8,128)(2,1)S(1)} %get-tuple-element.49), channel_id=1, source_target_pairs={{0,32},{32,0},{64,96},{96,64},{128,160},{160,128},{192,224},{224,1... | collective-permute-start | bytes 1572872 | tf_op jit(solution)/shard_map/ppermute | solution.py:79
  93.9 16.6 %collective-permute-start.24 = (bf16[192,4096]{1,0:T(8,128)(2,1)S(1)}, bf16[192,4096]{1,0:T(8,128)(2,1)S(1)}, u32[]{:S(2)}, u32[]{:S(2)}) collective-permute-start(bf16[192,4096]{1,0:T(8,128)(2,1)S(1)} %get-tuple-element.48), channel_id=1, source_target_pairs={{0,32},{32,0},{64,96},{96,64},{128,160},{160,128},{192,224},{224,1... | collective-permute-start | bytes 4718600 | tf_op jit(solution)/shard_map/ppermute | solution.py:79
  101.7 8.8 %collective-permute-start.26 = (bf16[32,4096]{1,0:T(8,128)(2,1)S(1)}, bf16[32,4096]{1,0:T(8,128)(2,1)S(1)}, u32[]{:S(2)}, u32[]{:S(2)}) collective-permute-start(bf16[32,4096]{1,0:T(8,128)(2,1)S(1)} %get-tuple-element.55), channel_id=1, source_target_pairs={{0,64},{32,96},{64,128},{96,160},{128,192},{160,224},{192,0},{224,... | collective-permute-start | bytes 786440 | tf_op jit(solution)/shard_map/ppermute | solution.py:72
  101.8 8.7 %collective-permute-start.28 = (bf16[32,4096]{1,0:T(8,128)(2,1)S(1)}, bf16[32,4096]{1,0:T(8,128)(2,1)S(1)}, u32[]{:S(2)}, u32[]{:S(2)}) collective-permute-start(bf16[32,4096]{1,0:T(8,128)(2,1)S(1)} %get-tuple-element.56), channel_id=1, source_target_pairs={{0,192},{32,224},{64,0},{96,32},{128,64},{160,96},{192,128},{224,1... | collective-permute-start | bytes 786440 | tf_op jit(solution)/shard_map/ppermute | solution.py:72
  112.0 15.5 %collective-permute-start.27 = (bf16[64,4096]{1,0:T(8,128)(2,1)}, bf16[64,4096]{1,0:T(8,128)(2,1)S(1)}, u32[]{:S(2)}, u32[]{:S(2)}) collective-permute-start(bf16[64,4096]{1,0:T(8,128)(2,1)} %get-tuple-element.51), channel_id=1, source_target_pairs={{0,64},{32,96},{64,128},{96,160},{128,192},{160,224},{192,0},{224,... | collective-permute-start | bytes 1572872 | tf_op jit(solution)/shard_map/ppermute | solution.py:72
  112.0 16.3 %collective-permute-start.29 = (bf16[64,4096]{1,0:T(8,128)(2,1)}, bf16[64,4096]{1,0:T(8,128)(2,1)}, u32[]{:S(2)}, u32[]{:S(2)}) collective-permute-start(bf16[64,4096]{1,0:T(8,128)(2,1)} %get-tuple-element.52), channel_id=1, source_target_pairs={{0,192},{32,224},{64,0},{96,32},{128,64},{160,96},{192,128},{224,1... | collective-permute-start | bytes 1572872 | tf_op jit(solution)/shard_map/ppermute | solution.py:72
  116.6 25.7 %all-to-all-start.2 = ((bf16[32,2,4096]{2,1,0:T(2,128)(2,1)}), bf16[32,2,4096]{2,1,0:T(2,128)(2,1)S(1)}, u32[]{:S(2)}, u32[]{:S(2)}) async-start(bf16[32,2,4096]{2,1,0:T(2,128)(2,1)} %reshape.64), calls=%async_computation.2 | async-start | bytes 1048576 | tf_op jit(solution)/shard_map/all_to_all | solution.py:102
  143.5 19.7 %all-to-all-start.3 = ((bf16[32,2,4096]{2,1,0:T(2,128)(2,1)}), bf16[32,2,4096]{2,1,0:T(2,128)(2,1)S(1)}, u32[]{:S(2)}, u32[]{:S(2)}) async-start(bf16[32,2,4096]{2,1,0:T(2,128)(2,1)} %reshape.65), calls=%async_computation.3 | async-start | bytes 1048576 | tf_op jit(solution)/shard_map/all_to_all | solution.py:102
  (13 other events, 75.6 us)

commit v6 on v5

--- a/solution.py
+++ b/solution.py
@@ -92,8 +92,13 @@
     sent0, sent1 = lax.optimization_barrier(
         tuple(
             jnp.einsum(
-                "tcr,td->crd", chosen[:, :, index], tokens, preferred_element_type=jnp.float32
-            ).astype(jnp.bfloat16)
+                "ts,td->sd",
+                chosen[:, :, index].reshape(token_rows, chunk_rows),
+                tokens,
+                preferred_element_type=jnp.float32,
+            )
+            .astype(jnp.bfloat16)
+            .reshape(column_count, capacity, model_width)
             for index in range(2)
         )
     )
@@ -144,10 +149,10 @@
         )
 
     def returned(kept, paired, home, *others):
-        total = add(kept[mine], paired[mine], *home)
+        total = add(kept[mine], paired[mine], *home).reshape(column_count, capacity, model_width)
         if others:
             total = after_all(total, *others)
-        return columns(total.reshape(column_count, capacity, model_width))
+        return columns(total)
 
     arrived0 = columns(sent0)
     own0 = arrived0.reshape(n, model_width)
@@ -167,20 +172,23 @@
     outer1, inner1 = across(outer1), across(inner1)
     home0, kept1 = tie((home0, kept1))
     out1 = outward(kept1, outer1)
-    back0 = returned(kept0, inner0, home0)
-    home1 = homeward(kept1, inner1, *out1)
-    back1 = returned(kept1, inner1, home1, back0)
-
-    chose, taken, gate_values = after_all((chose, taken, gate_values), home0)
+    chose, taken, gate_values = after_all((chose, taken, gate_values), out0)
     gates = jnp.sum(jnp.where(chose, gate_values.astype(jnp.float32)[:, :, None], 0.0), axis=1)
     weights = jnp.where(taken, gates, 0.0).astype(jnp.bfloat16)
     weights = weights.reshape(token_rows, column_count, per_device, capacity)
-    mixed_out = jnp.zeros((token_rows, model_width), jnp.float32)
-    for index, back in enumerate((back0, back1)):
-        mixed_out = mixed_out + jnp.einsum(
-            "tcr,crd->td", weights[:, :, index], back, preferred_element_type=jnp.float32
-        )
-    return mixed_out.astype(jnp.bfloat16)
+
+    def weighted(index, back):
+        return jnp.einsum(
+            "ts,sd->td",
+            weights[:, :, index].reshape(token_rows, chunk_rows),
+            back.reshape(chunk_rows, model_width),
+            preferred_element_type=jnp.float32,
+        )
+
+    mixed0 = weighted(0, returned(kept0, inner0, home0))
+    home1 = homeward(kept1, inner1, *out1)
+    mixed1 = weighted(1, returned(kept1, inner1, home1, mixed0))
+    return (mixed0 + mixed1).astype(jnp.bfloat16)
 
 
 def solution(mesh):

time: 165 us -> 159 us (0.964)
  waiting for transfers between devices: 62.9 us -> 34.3 us
  blocking collectives: 28.2 us -> 52.3 us
  starting transfers between devices: 46.5 us -> 44.1 us
  other arithmetic: 4.96 us -> 6.9 us
  local copies, waits for them, and re-layouts: 7.2 us -> 5.36 us
    all_to_all x1 -> x2, blocking collectives: 28.2 us -> 52.3 us  [columns(): lax.all_to_all(value, 'expert', split_axis=0, concat_axis=0, tiled=True)]
    all_to_all x3 -> x2, waiting for transfers between devices: 29.5 us -> 12.6 us  [columns(): lax.all_to_all(value, 'expert', split_axis=0, concat_axis=0, tiled=True)]
    ppermute x16, waiting for transfers between devices: 33.3 us -> 21.6 us  [along_ring(): lax.ppermute(value, 'dp', [(2 * y + c, 2 * ((y + step) % ring) + c) for y...]
    all_to_all x3 -> x2, starting transfers between devices: 22.1 us -> 14.6 us  [columns(): lax.all_to_all(value, 'expert', split_axis=0, concat_axis=0, tiled=True)]
    ppermute x16, starting transfers between devices: 21.7 us -> 26.5 us  [along_ring(): lax.ppermute(value, 'dp', [(2 * y + c, 2 * ((y + step) % ring) + c) for y...]
    optimization_barrier x2 -> x0, local copies, waits for them, and re-layouts: 1.88 us -> none  [the longest x1 1.34 us: after_all(): return tie((value, *others))[0]]
    convert_element_type x6, other arithmetic: 3.95 us -> 5.74 us  [add(): return total.astype(jnp.bfloat16)]
    reshape x2 -> x6, local copies, waits for them, and re-layouts: 2.27 us -> 3.33 us  [the longest x2 1.47 us: returned(): add(kept[mine], paired[mine], *home)]
  transfers between devices with their start and end apart: 33 -> 32, of which waited for: 14 -> 11; matrix products, arithmetic and copies ran while one was open for 4% -> 5% of each run, Pallas kernels for 7% -> 8%
where the time goes in v6:
time: 159 us; the launch traced here: 158 us
  blocking collectives  52.3 us (33%)
  starting transfers between devices  44.1 us (28%)
  waiting for transfers between devices  34.3 us (22%)
  Pallas kernels  13.1 us (8%)
  other arithmetic  6.9 us (4%)
  local copies, waits for them, and re-layouts  5.36 us (3%)
  matrix products  1.64 us (1%)
    all_to_all x2, blocking collectives, columns(): lax.all_to_all(value, 'expert', split_axis=0, concat_axis=0, tiled=True)  52.3 us
    ppermute x16, starting transfers between devices, along_ring(): lax.ppermute(value, 'dp', [(2 * y + c, 2 * ((y + step) % ring) + c) for y...  26.5 us
    ppermute x16, waiting for transfers between devices, along_ring(): lax.ppermute(value, 'dp', [(2 * y + c, 2 * ((y + step) % ring) + c) for y...  21.6 us
    all_to_all x2, starting transfers between devices, columns(): lax.all_to_all(value, 'expert', split_axis=0, concat_axis=0, tiled=True)  14.6 us
    pallas_call x2, Pallas kernels, expert_rows(): pl.pallas_call(functools.partial(expert_kernel, count), grid=(1,), in_spe...  13.1 us
    all_to_all x2, waiting for transfers between devices, columns(): lax.all_to_all(value, 'expert', split_axis=0, concat_axis=0, tiled=True)  12.6 us
    convert_element_type x6, other arithmetic, add(): return total.astype(jnp.bfloat16)  5.74 us
  transfers between devices with their start and end apart: 32, of which 11 were waited for; matrix products, arithmetic and copies ran while one was open for 5% of the time, Pallas kernels for 8%

profile of v6, /device:TPU:2, one launch (start us, length us, event | category | flops | bytes accessed | tf_op | source)
XLA Modules:
  0.0 158.0 jit_solution(9840344042245457093)
XLA Ops:
  3.5 28.2 %all_to_all.20 = bf16[32,2,4096]{2,1,0:T(2,128)(2,1)S(1)} all-to-all(bf16[32,2,4096]{2,1,0:T(2,128)(2,1)S(1)} %reshape.73), channel_id=1, replica_groups=mesh['dp'=8,'expert'=32] {'expert'}, dimensions={0} | all-to-all | bytes 1048576 | tf_op jit(solution)/shard_map/all_to_all | solution.py:107
  31.9 1.7 %collective-permute-start.3 = (bf16[64,4096]{1,0:T(8,128)(2,1)S(1)}, bf16[64,4096]{1,0:T(8,128)(2,1)S(1)}, u32[]{:S(2)}, u32[]{:S(2)}) collective-permute-start(bf16[64,4096]{1,0:T(8,128)(2,1)S(1)} %reshape.76.refs_0_), channel_id=1, source_target_pairs={{0,64},{32,96},{64,128},{96,160},{128,192},{160,224},{192,0},{224,... | collective-permute-start | bytes 1572872 | tf_op jit(solution)/shard_map/ppermute | solution.py:72
  33.6 1.7 %collective-permute-start.2 = (bf16[64,4096]{1,0:T(8,128)(2,1)S(1)}, bf16[64,4096]{1,0:T(8,128)(2,1)S(1)}, u32[]{:S(2)}, u32[]{:S(2)}) collective-permute-start(bf16[64,4096]{1,0:T(8,128)(2,1)S(1)} %reshape.76.refs_0_), channel_id=1, source_target_pairs={{0,192},{32,224},{64,0},{96,32},{128,64},{160,96},{192,128},{224,1... | collective-permute-start | bytes 1572872 | tf_op jit(solution)/shard_map/ppermute | solution.py:72
  35.2 5.6 %all-to-all-start.1 = ((bf16[32,2,4096]{2,1,0:T(2,128)(2,1)}), bf16[32,2,4096]{2,1,0:T(2,128)(2,1)}, u32[]{:S(2)}, u32[]{:S(2)}) async-start(bf16[32,2,4096]{2,1,0:T(2,128)(2,1)} %reshape.74), calls=%async_computation.1 | async-start | bytes 1048576 | tf_op jit(solution)/shard_map/all_to_all | solution.py:107
  41.0 4.7 %collective-permute-done.3.refs_2_ = bf16[64,4096]{1,0:T(8,128)(2,1)S(1)} collective-permute-done((bf16[64,4096]{1,0:T(8,128)(2,1)S(1)}, bf16[64,4096]{1,0:T(8,128)(2,1)S(1)}, u32[]{:S(2)}, u32[]{:S(2)}) %collective-permute-start.3) | collective-permute-done | bytes 524320 | tf_op jit(solution)/shard_map/ppermute | solution.py:72
  46.1 3.0 %collective-permute-start.5 = (bf16[32,4096]{1,0:T(8,128)(2,1)S(1)}, bf16[32,4096]{1,0:T(8,128)(2,1)}, u32[]{:S(2)}, u32[]{:S(2)}) collective-permute-start(bf16[32,4096]{1,0:T(8,128)(2,1)S(1)} %slice.121), channel_id=1, source_target_pairs={{0,192},{32,224},{64,0},{96,32},{128,64},{160,96},{192,128},{224,1... | collective-permute-start | bytes 786440 | tf_op jit(solution)/shard_map/ppermute | solution.py:72
  49.6 3.7 %collective-permute-done.4.refs_3_ = bf16[32,4096]{1,0:T(8,128)(2,1)S(1)} collective-permute-done((bf16[32,4096]{1,0:T(8,128)(2,1)S(1)}, bf16[32,4096]{1,0:T(8,128)(2,1)S(1)}, u32[]{:S(2)}, u32[]{:S(2)}) %collective-permute-start.4) | collective-permute-done | bytes 262176 | tf_op jit(solution)/shard_map/ppermute | solution.py:72
  53.9 2.5 %all-to-all-done.1 = bf16[32,2,4096]{2,1,0:T(2,128)(2,1)} async-done(((bf16[32,2,4096]{2,1,0:T(2,128)(2,1)}), bf16[32,2,4096]{2,1,0:T(2,128)(2,1)}, u32[]{:S(2)}, u32[]{:S(2)}) %all-to-all-start.1) | async-done | bytes 524320 | tf_op jit(solution)/shard_map/all_to_all | solution.py:107
  58.0 3.0 %collective-permute-start.1 = (bf16[64,4096]{1,0:T(8,128)(2,1)S(1)}, bf16[64,4096]{1,0:T(8,128)(2,1)S(1)}, u32[]{:S(2)}, u32[]{:S(2)}) collective-permute-start(bf16[64,4096]{1,0:T(8,128)(2,1)S(1)} %reshape.75.refs_0_), channel_id=1, source_target_pairs={{0,192},{32,224},{64,0},{96,32},{128,64},{160,96},{192,128},{224,1... | collective-permute-start | bytes 1572872 | tf_op jit(solution)/shard_map/ppermute | solution.py:72
  61.0 6.2 %shard_map.64 = (bf16[256,4096]{1,0:T(8,128)(2,1)S(1)}, bf16[64,4096]{1,0:T(8,128)(2,1)S(1)}, bf16[192,4096]{1,0:T(8,128)(2,1)S(1)}) custom-call(bf16[64,4096]{1,0:T(8,128)(2,1)S(1)} %reshape.76.refs_0_, bf16[64,4096]{1,0:T(8,128)(2,1)S(1)} %collective-permute-done.2.refs_1_, bf16[64,4096]{1,0:T(8,128)(2,1)S(1)} %collective-permute-done.3.refs_2_, ...), custom_call_target="tpu_custom_call" | custom-call | flops 2415919104 | bytes 13107200 | tf_op jit(solution)/shard_map/pallas_call | solution.py:38
  67.8 2.9 %collective-permute-done.refs_2_ = bf16[64,4096]{1,0:T(8,128)(2,1)S(1)} collective-permute-done((bf16[64,4096]{1,0:T(8,128)(2,1)S(1)}, bf16[64,4096]{1,0:T(8,128)(2,1)S(1)}, u32[]{:S(2)}, u32[]{:S(2)}) %collective-permute-start) | collective-permute-done | bytes 524320 | tf_op jit(solution)/shard_map/ppermute | solution.py:72
  72.0 2.2 %collective-permute-start.12 = (bf16[32,4096]{1,0:T(8,128)(2,1)S(1)}, bf16[32,4096]{1,0:T(8,128)(2,1)S(1)}, u32[]{:S(2)}, u32[]{:S(2)}) collective-permute-start(bf16[32,4096]{1,0:T(8,128)(2,1)S(1)} %slice.95), channel_id=1, source_target_pairs={{0,192},{32,224},{64,0},{96,32},{128,64},{160,96},{192,128},{224,1... | collective-permute-start | bytes 786440 | tf_op jit(solution)/shard_map/ppermute | solution.py:72
  74.4 3.2 %collective-permute-start.15 = (bf16[32,4096]{1,0:T(8,128)(2,1)S(1)}, bf16[32,4096]{1,0:T(8,128)(2,1)S(1)}, u32[]{:S(2)}, u32[]{:S(2)}) collective-permute-start(bf16[32,4096]{1,0:T(8,128)(2,1)S(1)} %get-tuple-element.57), channel_id=1, source_target_pairs={{0,192},{32,224},{64,0},{96,32},{128,64},{160,96},{192,128},{224,1... | collective-permute-start | bytes 786440 | tf_op jit(solution)/shard_map/ppermute | solution.py:72
  77.6 2.9 %collective-permute-done.11.refs_3_ = bf16[32,4096]{1,0:T(8,128)(2,1)S(1)} collective-permute-done((bf16[32,4096]{1,0:T(8,128)(2,1)S(1)}, bf16[32,4096]{1,0:T(8,128)(2,1)S(1)}, u32[]{:S(2)}, u32[]{:S(2)}) %collective-permute-start.11) | collective-permute-done | bytes 262176 | tf_op jit(solution)/shard_map/ppermute | solution.py:72
  81.1 2.3 %collective-permute-done.14 = bf16[32,4096]{1,0:T(8,128)(2,1)S(1)} collective-permute-done((bf16[32,4096]{1,0:T(8,128)(2,1)S(1)}, bf16[32,4096]{1,0:T(8,128)(2,1)S(1)}, u32[]{:S(2)}, u32[]{:S(2)}) %collective-permute-start.14) | collective-permute-done | bytes 262176 | tf_op jit(solution)/shard_map/ppermute | solution.py:72
  84.6 1.8 %collective-permute-start.17 = (bf16[64,4096]{1,0:T(8,128)(2,1)S(1)}, bf16[64,4096]{1,0:T(8,128)(2,1)S(1)}, u32[]{:S(2)}, u32[]{:S(2)}) collective-permute-start(bf16[64,4096]{1,0:T(8,128)(2,1)S(1)} %get-tuple-element.54), channel_id=1, source_target_pairs={{0,64},{32,96},{64,128},{96,160},{128,192},{160,224},{192,0},{224,... | collective-permute-start | bytes 1572872 | tf_op jit(solution)/shard_map/ppermute | solution.py:72
  87.9 6.9 %shard_map.65 = (bf16[256,4096]{1,0:T(8,128)(2,1)S(1)}, bf16[64,4096]{1,0:T(8,128)(2,1)S(1)}, bf16[192,4096]{1,0:T(8,128)(2,1)}) custom-call(bf16[64,4096]{1,0:T(8,128)(2,1)S(1)} %reshape.75.refs_0_, bf16[64,4096]{1,0:T(8,128)(2,1)S(1)} %collective-permute-done.1.refs_1_, bf16[64,4096]{1,0:T(8,128)(2,1)S(1)} %collective-permute-done.refs_2_, ...), custom_call_target="tpu_custom_call" | custom-call | flops 2415919104 | bytes 13107200 | tf_op jit(solution)/shard_map/pallas_call | solution.py:38
  95.6 4.3 %collective-permute-done.17 = bf16[64,4096]{1,0:T(8,128)(2,1)S(1)} collective-permute-done((bf16[64,4096]{1,0:T(8,128)(2,1)S(1)}, bf16[64,4096]{1,0:T(8,128)(2,1)S(1)}, u32[]{:S(2)}, u32[]{:S(2)}) %collective-permute-start.17) | collective-permute-done | bytes 524320 | tf_op jit(solution)/shard_map/ppermute | solution.py:72
  101.5 2.5 %collective-permute-start.28 = (bf16[32,4096]{1,0:T(8,128)(2,1)S(1)}, bf16[32,4096]{1,0:T(8,128)(2,1)S(1)}, u32[]{:S(2)}, u32[]{:S(2)}) collective-permute-start(bf16[32,4096]{1,0:T(8,128)(2,1)S(1)} %get-tuple-element.56), channel_id=1, source_target_pairs={{0,192},{32,224},{64,0},{96,32},{128,64},{160,96},{192,128},{224,1... | collective-permute-start | bytes 786440 | tf_op jit(solution)/shard_map/ppermute | solution.py:72
  105.4 8.9 %all-to-all-start.2 = ((bf16[32,2,4096]{2,1,0:T(2,128)(2,1)}), bf16[32,2,4096]{2,1,0:T(2,128)(2,1)S(1)}, u32[]{:S(2)}, u32[]{:S(2)}) async-start(bf16[32,2,4096]{2,1,0:T(2,128)(2,1)} %reshape.78), calls=%async_computation.2 | async-start | bytes 1048576 | tf_op jit(solution)/shard_map/all_to_all | solution.py:107
  114.4 2.6 %add_convert_fusion.2 = (bf16[64,4096]{1,0:T(8,128)(2,1)}, bf16[64,4096]{1,0:T(8,128)(2,1)}) fusion(bf16[192,4096]{1,0:T(8,128)(2,1)} %collective-permute-done.24, bf16[32,4096]{1,0:T(8,128)(2,1)S(1)} %collective-permute-done.26, bf16[256,4096]{1,0:T(8,128)(2,1)S(1)} %get-tuple-element.47, bf16[32,4096]{1,0:T(8,128)(2,1)S(1)} %collective-permute-done.28), kind=kLoop, calls=%fused_computation.6 | loop fusion | flops 3145728 | bytes 3670016 | tf_op jit(solution)/shard_map/convert_element_type | solution.py:113
  116.9 3.2 %collective-permute-start.29 = (bf16[64,4096]{1,0:T(8,128)(2,1)}, bf16[64,4096]{1,0:T(8,128)(2,1)}, u32[]{:S(2)}, u32[]{:S(2)}) collective-permute-start(bf16[64,4096]{1,0:T(8,128)(2,1)} %get-tuple-element.52), channel_id=1, source_target_pairs={{0,192},{32,224},{64,0},{96,32},{128,64},{160,96},{192,128},{224,1... | collective-permute-start | bytes 1572872 | tf_op jit(solution)/shard_map/ppermute | solution.py:72
  120.3 10.1 %all-to-all-done.2 = bf16[32,2,4096]{2,1,0:T(2,128)(2,1)S(1)} async-done(((bf16[32,2,4096]{2,1,0:T(2,128)(2,1)}), bf16[32,2,4096]{2,1,0:T(2,128)(2,1)S(1)}, u32[]{:S(2)}, u32[]{:S(2)}) %all-to-all-start.2) | async-done | bytes 524320 | tf_op jit(solution)/shard_map/all_to_all | solution.py:107
  132.8 24.1 %all_to_all.21 = bf16[32,2,4096]{2,1,0:T(2,128)(2,1)S(1)} all-to-all(bf16[32,2,4096]{2,1,0:T(2,128)(2,1)S(1)} %reshape.80), channel_id=1, replica_groups=mesh['dp'=8,'expert'=32] {'expert'}, dimensions={0} | all-to-all | bytes 1048576 | tf_op jit(solution)/shard_map/all_to_all | solution.py:107
  (89 shorter events, 19.3 us)
Async XLA Ops:
  31.9 13.8 %collective-permute-start.3 = (bf16[64,4096]{1,0:T(8,128)(2,1)S(1)}, bf16[64,4096]{1,0:T(8,128)(2,1)S(1)}, u32[]{:S(2)}, u32[]{:S(2)}) collective-permute-start(bf16[64,4096]{1,0:T(8,128)(2,1)S(1)} %reshape.76.refs_0_), channel_id=1, source_target_pairs={{0,64},{32,96},{64,128},{96,160},{128,192},{160,224},{192,0},{224,... | collective-permute-start | bytes 1572872 | tf_op jit(solution)/shard_map/ppermute | solution.py:72
  33.6 12.5 %collective-permute-start.2 = (bf16[64,4096]{1,0:T(8,128)(2,1)S(1)}, bf16[64,4096]{1,0:T(8,128)(2,1)S(1)}, u32[]{:S(2)}, u32[]{:S(2)}) collective-permute-start(bf16[64,4096]{1,0:T(8,128)(2,1)S(1)} %reshape.76.refs_0_), channel_id=1, source_target_pairs={{0,192},{32,224},{64,0},{96,32},{128,64},{160,96},{192,128},{224,1... | collective-permute-start | bytes 1572872 | tf_op jit(solution)/shard_map/ppermute | solution.py:72
  35.2 21.2 %all-to-all-start.1 = ((bf16[32,2,4096]{2,1,0:T(2,128)(2,1)}), bf16[32,2,4096]{2,1,0:T(2,128)(2,1)}, u32[]{:S(2)}, u32[]{:S(2)}) async-start(bf16[32,2,4096]{2,1,0:T(2,128)(2,1)} %reshape.74), calls=%async_computation.1 | async-start | bytes 1048576 | tf_op jit(solution)/shard_map/all_to_all | solution.py:107
  40.9 16.8 %collective-permute-start.8 = (bf16[64,4096]{1,0:T(8,128)(2,1)S(1)}, bf16[64,4096]{1,0:T(8,128)(2,1)S(1)}, u32[]{:S(2)}, u32[]{:S(2)}) collective-permute-start(bf16[64,4096]{1,0:T(8,128)(2,1)S(1)} %reshape.76.refs_0_), channel_id=1, source_target_pairs={{0,32},{32,0},{64,96},{96,64},{128,160},{160,128},{192,224},{224,1... | collective-permute-start | bytes 1572872 | tf_op jit(solution)/shard_map/ppermute | solution.py:79
  45.7 7.7 %collective-permute-start.4 = (bf16[32,4096]{1,0:T(8,128)(2,1)S(1)}, bf16[32,4096]{1,0:T(8,128)(2,1)S(1)}, u32[]{:S(2)}, u32[]{:S(2)}) collective-permute-start(bf16[32,4096]{1,0:T(8,128)(2,1)S(1)} %slice.120), channel_id=1, source_target_pairs={{0,64},{32,96},{64,128},{96,160},{128,192},{160,224},{192,0},{224,... | collective-permute-start | bytes 786440 | tf_op jit(solution)/shard_map/ppermute | solution.py:72
  46.1 7.2 %collective-permute-start.5 = (bf16[32,4096]{1,0:T(8,128)(2,1)S(1)}, bf16[32,4096]{1,0:T(8,128)(2,1)}, u32[]{:S(2)}, u32[]{:S(2)}) collective-permute-start(bf16[32,4096]{1,0:T(8,128)(2,1)S(1)} %slice.121), channel_id=1, source_target_pairs={{0,192},{32,224},{64,0},{96,32},{128,64},{160,96},{192,128},{224,1... | collective-permute-start | bytes 786440 | tf_op jit(solution)/shard_map/ppermute | solution.py:72
  49.1 11.9 %collective-permute-start.10 = (bf16[64,4096]{1,0:T(8,128)(2,1)S(1)}, bf16[64,4096]{1,0:T(8,128)(2,1)S(1)}, u32[]{:S(2)}, u32[]{:S(2)}) collective-permute-start(bf16[64,4096]{1,0:T(8,128)(2,1)S(1)} %collective-permute-done.3.refs_2_), channel_id=1, source_target_pairs={{0,32},{32,0},{64,96},{96,64},{128,160},{160,128},{192,224},{224,1... | collective-permute-start | bytes 1572872 | tf_op jit(solution)/shard_map/ppermute | solution.py:79
  49.1 11.9 %collective-permute-start.9 = (bf16[64,4096]{1,0:T(8,128)(2,1)S(1)}, bf16[64,4096]{1,0:T(8,128)(2,1)}, u32[]{:S(2)}, u32[]{:S(2)}) collective-permute-start(bf16[64,4096]{1,0:T(8,128)(2,1)S(1)} %collective-permute-done.2.refs_1_), channel_id=1, source_target_pairs={{0,32},{32,0},{64,96},{96,64},{128,160},{160,128},{192,224},{224,1... | collective-permute-start | bytes 1572872 | tf_op jit(solution)/shard_map/ppermute | solution.py:79
  53.4 7.6 %collective-permute-start.7 = (bf16[32,4096]{1,0:T(8,128)(2,1)}, bf16[32,4096]{1,0:T(8,128)(2,1)}, u32[]{:S(2)}, u32[]{:S(2)}) collective-permute-start(bf16[32,4096]{1,0:T(8,128)(2,1)} %collective-permute-done.5.refs_4_), channel_id=1, source_target_pairs={{0,32},{32,0},{64,96},{96,64},{128,160},{160,128},{192,224},{224,1... | collective-permute-start | bytes 786440 | tf_op jit(solution)/shard_map/ppermute | solution.py:79
  57.7 13.1 %collective-permute-start = (bf16[64,4096]{1,0:T(8,128)(2,1)S(1)}, bf16[64,4096]{1,0:T(8,128)(2,1)S(1)}, u32[]{:S(2)}, u32[]{:S(2)}) collective-permute-start(bf16[64,4096]{1,0:T(8,128)(2,1)S(1)} %reshape.75.refs_0_), channel_id=1, source_target_pairs={{0,64},{32,96},{64,128},{96,160},{128,192},{160,224},{192,0},{224,... | collective-permute-start | bytes 1572872 | tf_op jit(solution)/shard_map/ppermute | solution.py:72
  58.0 12.8 %collective-permute-start.1 = (bf16[64,4096]{1,0:T(8,128)(2,1)S(1)}, bf16[64,4096]{1,0:T(8,128)(2,1)S(1)}, u32[]{:S(2)}, u32[]{:S(2)}) collective-permute-start(bf16[64,4096]{1,0:T(8,128)(2,1)S(1)} %reshape.75.refs_0_), channel_id=1, source_target_pairs={{0,192},{32,224},{64,0},{96,32},{128,64},{160,96},{192,128},{224,1... | collective-permute-start | bytes 1572872 | tf_op jit(solution)/shard_map/ppermute | solution.py:72
  67.3 16.6 %collective-permute-start.16 = (bf16[192,4096]{1,0:T(8,128)(2,1)S(1)}, bf16[192,4096]{1,0:T(8,128)(2,1)S(1)}, u32[]{:S(2)}, u32[]{:S(2)}) collective-permute-start(bf16[192,4096]{1,0:T(8,128)(2,1)S(1)} %get-tuple-element.41), channel_id=1, source_target_pairs={{0,32},{32,0},{64,96},{96,64},{128,160},{160,128},{192,224},{224,1... | collective-permute-start | bytes 4718600 | tf_op jit(solution)/shard_map/ppermute | solution.py:79
  70.8 9.8 %collective-permute-start.11 = (bf16[32,4096]{1,0:T(8,128)(2,1)S(1)}, bf16[32,4096]{1,0:T(8,128)(2,1)S(1)}, u32[]{:S(2)}, u32[]{:S(2)}) collective-permute-start(bf16[32,4096]{1,0:T(8,128)(2,1)S(1)} %slice.94), channel_id=1, source_target_pairs={{0,64},{32,96},{64,128},{96,160},{128,192},{160,224},{192,0},{224,... | collective-permute-start | bytes 786440 | tf_op jit(solution)/shard_map/ppermute | solution.py:72
  72.0 8.9 %collective-permute-start.12 = (bf16[32,4096]{1,0:T(8,128)(2,1)S(1)}, bf16[32,4096]{1,0:T(8,128)(2,1)S(1)}, u32[]{:S(2)}, u32[]{:S(2)}) collective-permute-start(bf16[32,4096]{1,0:T(8,128)(2,1)S(1)} %slice.95), channel_id=1, source_target_pairs={{0,192},{32,224},{64,0},{96,32},{128,64},{160,96},{192,128},{224,1... | collective-permute-start | bytes 786440 | tf_op jit(solution)/shard_map/ppermute | solution.py:72
  74.3 9.1 %collective-permute-start.14 = (bf16[32,4096]{1,0:T(8,128)(2,1)S(1)}, bf16[32,4096]{1,0:T(8,128)(2,1)S(1)}, u32[]{:S(2)}, u32[]{:S(2)}) collective-permute-start(bf16[32,4096]{1,0:T(8,128)(2,1)S(1)} %get-tuple-element.58), channel_id=1, source_target_pairs={{0,64},{32,96},{64,128},{96,160},{128,192},{160,224},{192,0},{224,... | collective-permute-start | bytes 786440 | tf_op jit(solution)/shard_map/ppermute | solution.py:72
  74.4 9.3 %collective-permute-start.15 = (bf16[32,4096]{1,0:T(8,128)(2,1)S(1)}, bf16[32,4096]{1,0:T(8,128)(2,1)S(1)}, u32[]{:S(2)}, u32[]{:S(2)}) collective-permute-start(bf16[32,4096]{1,0:T(8,128)(2,1)S(1)} %get-tuple-element.57), channel_id=1, source_target_pairs={{0,192},{32,224},{64,0},{96,32},{128,64},{160,96},{192,128},{224,1... | collective-permute-start | bytes 786440 | tf_op jit(solution)/shard_map/ppermute | solution.py:72
  84.6 15.3 %collective-permute-start.17 = (bf16[64,4096]{1,0:T(8,128)(2,1)S(1)}, bf16[64,4096]{1,0:T(8,128)(2,1)S(1)}, u32[]{:S(2)}, u32[]{:S(2)}) collective-permute-start(bf16[64,4096]{1,0:T(8,128)(2,1)S(1)} %get-tuple-element.54), channel_id=1, source_target_pairs={{0,64},{32,96},{64,128},{96,160},{128,192},{160,224},{192,0},{224,... | collective-permute-start | bytes 1572872 | tf_op jit(solution)/shard_map/ppermute | solution.py:72
  86.4 13.6 %collective-permute-start.18 = (bf16[64,4096]{1,0:T(8,128)(2,1)S(1)}, bf16[64,4096]{1,0:T(8,128)(2,1)S(1)}, u32[]{:S(2)}, u32[]{:S(2)}) collective-permute-start(bf16[64,4096]{1,0:T(8,128)(2,1)S(1)} %get-tuple-element.53), channel_id=1, source_target_pairs={{0,192},{32,224},{64,0},{96,32},{128,64},{160,96},{192,128},{224,1... | collective-permute-start | bytes 1572872 | tf_op jit(solution)/shard_map/ppermute | solution.py:72
  95.0 19.4 %collective-permute-start.24 = (bf16[192,4096]{1,0:T(8,128)(2,1)}, bf16[192,4096]{1,0:T(8,128)(2,1)}, u32[]{:S(2)}, u32[]{:S(2)}) collective-permute-start(bf16[192,4096]{1,0:T(8,128)(2,1)} %get-tuple-element.48), channel_id=1, source_target_pairs={{0,32},{32,0},{64,96},{96,64},{128,160},{160,128},{192,224},{224,1... | collective-permute-start | bytes 4718600 | tf_op jit(solution)/shard_map/ppermute | solution.py:79
  100.8 13.6 %collective-permute-start.26 = (bf16[32,4096]{1,0:T(8,128)(2,1)}, bf16[32,4096]{1,0:T(8,128)(2,1)S(1)}, u32[]{:S(2)}, u32[]{:S(2)}) collective-permute-start(bf16[32,4096]{1,0:T(8,128)(2,1)} %get-tuple-element.55), channel_id=1, source_target_pairs={{0,64},{32,96},{64,128},{96,160},{128,192},{160,224},{192,0},{224,... | collective-permute-start | bytes 786440 | tf_op jit(solution)/shard_map/ppermute | solution.py:72
  101.5 12.8 %collective-permute-start.28 = (bf16[32,4096]{1,0:T(8,128)(2,1)S(1)}, bf16[32,4096]{1,0:T(8,128)(2,1)S(1)}, u32[]{:S(2)}, u32[]{:S(2)}) collective-permute-start(bf16[32,4096]{1,0:T(8,128)(2,1)S(1)} %get-tuple-element.56), channel_id=1, source_target_pairs={{0,192},{32,224},{64,0},{96,32},{128,64},{160,96},{192,128},{224,1... | collective-permute-start | bytes 786440 | tf_op jit(solution)/shard_map/ppermute | solution.py:72
  105.4 25.0 %all-to-all-start.2 = ((bf16[32,2,4096]{2,1,0:T(2,128)(2,1)}), bf16[32,2,4096]{2,1,0:T(2,128)(2,1)S(1)}, u32[]{:S(2)}, u32[]{:S(2)}) async-start(bf16[32,2,4096]{2,1,0:T(2,128)(2,1)} %reshape.78), calls=%async_computation.2 | async-start | bytes 1048576 | tf_op jit(solution)/shard_map/all_to_all | solution.py:107
  116.9 13.9 %collective-permute-start.27 = (bf16[64,4096]{1,0:T(8,128)(2,1)}, bf16[64,4096]{1,0:T(8,128)(2,1)}, u32[]{:S(2)}, u32[]{:S(2)}) collective-permute-start(bf16[64,4096]{1,0:T(8,128)(2,1)} %get-tuple-element.51), channel_id=1, source_target_pairs={{0,64},{32,96},{64,128},{96,160},{128,192},{160,224},{192,0},{224,... | collective-permute-start | bytes 1572872 | tf_op jit(solution)/shard_map/ppermute | solution.py:72
  116.9 13.9 %collective-permute-start.29 = (bf16[64,4096]{1,0:T(8,128)(2,1)}, bf16[64,4096]{1,0:T(8,128)(2,1)}, u32[]{:S(2)}, u32[]{:S(2)}) collective-permute-start(bf16[64,4096]{1,0:T(8,128)(2,1)} %get-tuple-element.52), channel_id=1, source_target_pairs={{0,192},{32,224},{64,0},{96,32},{128,64},{160,96},{192,128},{224,1... | collective-permute-start | bytes 1572872 | tf_op jit(solution)/shard_map/ppermute | solution.py:72
  (10 other events, 48.8 us)

commit v7 on v6

--- a/solution.py
+++ b/solution.py
@@ -34,7 +34,9 @@
     hidden = gate_weight.shape[1]
     count = len(pieces)
     whole = pl.BlockSpec(memory_space=pltpu.VMEM)
-    weight = pl.BlockSpec((1, hidden, width), lambda i: (index, 0, 0))
+    weight = pl.BlockSpec(
+        (1, hidden, width), lambda i: (index, 0, 0), pipeline_mode=pl.Buffered(1)
+    )
     return pl.pallas_call(
         functools.partial(expert_kernel, count),
         grid=(1,),
@@ -46,7 +48,7 @@
             bytes_accessed=6 * hidden * width + 4 * height * width,
             transcendentals=height * hidden,
         ),
-        compiler_params=pltpu.CompilerParams(vmem_limit_bytes=24 * 1024 * 1024),
+        compiler_params=pltpu.CompilerParams(vmem_limit_bytes=15 * 1024 * 1024),
     )(
         *(pltpu.with_memory_space_constraint(piece, pltpu.VMEM) for piece in pieces),
         *(
@@ -89,18 +91,16 @@
     taken = hit & (ranked == (slot % capacity)[None, :])
     chosen = taken.astype(jnp.bfloat16)
     chosen = chosen.reshape(token_rows, column_count, per_device, capacity)
-    sent0, sent1 = lax.optimization_barrier(
-        tuple(
-            jnp.einsum(
-                "ts,td->sd",
-                chosen[:, :, index].reshape(token_rows, chunk_rows),
-                tokens,
-                preferred_element_type=jnp.float32,
-            )
-            .astype(jnp.bfloat16)
-            .reshape(column_count, capacity, model_width)
-            for index in range(2)
-        )
+    sent0, sent1 = (
+        jnp.einsum(
+            "ts,td->sd",
+            chosen[:, :, index].reshape(token_rows, chunk_rows),
+            tokens,
+            preferred_element_type=jnp.float32,
+        )
+        .astype(jnp.bfloat16)
+        .reshape(column_count, capacity, model_width)
+        for index in range(2)
     )
 
     def columns(value):
@@ -154,10 +154,10 @@
             total = after_all(total, *others)
         return columns(total)
 
-    arrived0 = columns(sent0)
+    arrived0, sent1 = tie((columns(sent0), sent1))
     own0 = arrived0.reshape(n, model_width)
     before0, after0 = along_ring(own0, 1), along_ring(own0, -1)
-    own1 = columns(after_all(sent1, arrived0)).reshape(n, model_width)
+    own1 = columns(sent1).reshape(n, model_width)
     facing0 = facing(before0, after0)
 
     before1, after1 = along_ring(own1, 1), along_ring(own1, -1)

time: 159 us -> 159 us (level)
  blocking collectives: 52.3 us -> 24.1 us
  waiting for transfers between devices: 34.3 us -> 49.7 us
  starting transfers between devices: 44.1 us -> 55.7 us
    all_to_all x2 -> x1, blocking collectives: 52.3 us -> 24.1 us  [columns(): lax.all_to_all(value, 'expert', split_axis=0, concat_axis=0, tiled=True)]
    all_to_all x2 -> x3, waiting for transfers between devices: 12.6 us -> 28 us  [columns(): lax.all_to_all(value, 'expert', split_axis=0, concat_axis=0, tiled=True)]
    all_to_all x2 -> x3, starting transfers between devices: 14.6 us -> 26.2 us  [columns(): lax.all_to_all(value, 'expert', split_axis=0, concat_axis=0, tiled=True)]
  transfers between devices with their start and end apart: 32 -> 33, of which waited for: 11 -> 11; matrix products, arithmetic and copies ran while one was open for 5% -> 6% of each run, Pallas kernels for 8% -> 8%
where the time goes in v7:
time: 159 us; the launch traced here: 158 us
  starting transfers between devices  55.7 us (35%)
  waiting for transfers between devices  49.7 us (31%)
  blocking collectives  24.1 us (15%)
  Pallas kernels  13.2 us (8%)
  other arithmetic  6.89 us (4%)
  local copies, waits for them, and re-layouts  6.18 us (4%)
  matrix products  1.64 us (1%)
    all_to_all x3, waiting for transfers between devices, columns(): lax.all_to_all(value, 'expert', split_axis=0, concat_axis=0, tiled=True)  28 us
    ppermute x16, starting transfers between devices, along_ring(): lax.ppermute(value, 'dp', [(2 * y + c, 2 * ((y + step) % ring) + c) for y...  26.5 us
    all_to_all x3, starting transfers between devices, columns(): lax.all_to_all(value, 'expert', split_axis=0, concat_axis=0, tiled=True)  26.2 us
    all_to_all x1, blocking collectives, columns(): lax.all_to_all(value, 'expert', split_axis=0, concat_axis=0, tiled=True)  24.1 us
    ppermute x16, waiting for transfers between devices, along_ring(): lax.ppermute(value, 'dp', [(2 * y + c, 2 * ((y + step) % ring) + c) for y...  21.6 us
    pallas_call x2, Pallas kernels, expert_rows(): pl.pallas_call(functools.partial(expert_kernel, count), grid=(1,), in_spe...  13.2 us
    convert_element_type x6, other arithmetic, add(): return total.astype(jnp.bfloat16)  5.73 us
  transfers between devices with their start and end apart: 33, of which 11 were waited for; matrix products, arithmetic and copies ran while one was open for 6% of the time, Pallas kernels for 8%

profile of v7, /device:TPU:2, one launch (start us, length us, event | category | flops | bytes accessed | tf_op | source)
XLA Modules:
  0.0 157.6 jit_solution(17268817085622069488)
XLA Ops:
  2.8 11.6 %all-to-all-start = ((bf16[32,2,4096]{2,1,0:T(2,128)(2,1)}), bf16[32,2,4096]{2,1,0:T(2,128)(2,1)S(1)}, u32[]{:S(2)}, u32[]{:S(2)}) async-start(bf16[32,2,4096]{2,1,0:T(2,128)(2,1)} %reshape.73), calls=%async_computation | async-start | bytes 1048576 | tf_op jit(solution)/shard_map/all_to_all | solution.py:107
  15.9 15.4 %all-to-all-done = bf16[32,2,4096]{2,1,0:T(2,128)(2,1)S(1)} async-done(((bf16[32,2,4096]{2,1,0:T(2,128)(2,1)}), bf16[32,2,4096]{2,1,0:T(2,128)(2,1)S(1)}, u32[]{:S(2)}, u32[]{:S(2)}) %all-to-all-start) | async-done | bytes 524320 | tf_op jit(solution)/shard_map/all_to_all | solution.py:107
  33.2 1.7 %collective-permute-start.2 = (bf16[64,4096]{1,0:T(8,128)(2,1)S(1)}, bf16[64,4096]{1,0:T(8,128)(2,1)S(1)}, u32[]{:S(2)}, u32[]{:S(2)}) collective-permute-start(bf16[64,4096]{1,0:T(8,128)(2,1)S(1)} %reshape.76.refs_0_), channel_id=1, source_target_pairs={{0,192},{32,224},{64,0},{96,32},{128,64},{160,96},{192,128},{224,1... | collective-permute-start | bytes 1572872 | tf_op jit(solution)/shard_map/ppermute | solution.py:74
  34.8 5.6 %all-to-all-start.1 = ((bf16[32,2,4096]{2,1,0:T(2,128)(2,1)}), bf16[32,2,4096]{2,1,0:T(2,128)(2,1)}, u32[]{:S(2)}, u32[]{:S(2)}) async-start(bf16[32,2,4096]{2,1,0:T(2,128)(2,1)} %reshape.74), calls=%async_computation.1 | async-start | bytes 1048576 | tf_op jit(solution)/shard_map/all_to_all | solution.py:107
  40.5 4.7 %collective-permute-done.3.refs_2_ = bf16[64,4096]{1,0:T(8,128)(2,1)S(1)} collective-permute-done((bf16[64,4096]{1,0:T(8,128)(2,1)S(1)}, bf16[64,4096]{1,0:T(8,128)(2,1)S(1)}, u32[]{:S(2)}, u32[]{:S(2)}) %collective-permute-start.3) | collective-permute-done | bytes 524320 | tf_op jit(solution)/shard_map/ppermute | solution.py:74
  45.7 3.0 %collective-permute-start.5 = (bf16[32,4096]{1,0:T(8,128)(2,1)S(1)}, bf16[32,4096]{1,0:T(8,128)(2,1)}, u32[]{:S(2)}, u32[]{:S(2)}) collective-permute-start(bf16[32,4096]{1,0:T(8,128)(2,1)S(1)} %slice.121), channel_id=1, source_target_pairs={{0,192},{32,224},{64,0},{96,32},{128,64},{160,96},{192,128},{224,1... | collective-permute-start | bytes 786440 | tf_op jit(solution)/shard_map/ppermute | solution.py:74
  49.2 3.7 %collective-permute-done.4.refs_3_ = bf16[32,4096]{1,0:T(8,128)(2,1)S(1)} collective-permute-done((bf16[32,4096]{1,0:T(8,128)(2,1)S(1)}, bf16[32,4096]{1,0:T(8,128)(2,1)S(1)}, u32[]{:S(2)}, u32[]{:S(2)}) %collective-permute-start.4) | collective-permute-done | bytes 262176 | tf_op jit(solution)/shard_map/ppermute | solution.py:74
  53.5 2.5 %all-to-all-done.1 = bf16[32,2,4096]{2,1,0:T(2,128)(2,1)} async-done(((bf16[32,2,4096]{2,1,0:T(2,128)(2,1)}), bf16[32,2,4096]{2,1,0:T(2,128)(2,1)}, u32[]{:S(2)}, u32[]{:S(2)}) %all-to-all-start.1) | async-done | bytes 524320 | tf_op jit(solution)/shard_map/all_to_all | solution.py:107
  57.6 3.0 %collective-permute-start.1 = (bf16[64,4096]{1,0:T(8,128)(2,1)S(1)}, bf16[64,4096]{1,0:T(8,128)(2,1)S(1)}, u32[]{:S(2)}, u32[]{:S(2)}) collective-permute-start(bf16[64,4096]{1,0:T(8,128)(2,1)S(1)} %reshape.75.refs_0_), channel_id=1, source_target_pairs={{0,192},{32,224},{64,0},{96,32},{128,64},{160,96},{192,128},{224,1... | collective-permute-start | bytes 1572872 | tf_op jit(solution)/shard_map/ppermute | solution.py:74
  60.6 6.2 %shard_map.64 = (bf16[256,4096]{1,0:T(8,128)(2,1)S(1)}, bf16[64,4096]{1,0:T(8,128)(2,1)S(1)}, bf16[192,4096]{1,0:T(8,128)(2,1)S(1)}) custom-call(bf16[64,4096]{1,0:T(8,128)(2,1)S(1)} %reshape.76.refs_0_, bf16[64,4096]{1,0:T(8,128)(2,1)S(1)} %collective-permute-done.2.refs_1_, bf16[64,4096]{1,0:T(8,128)(2,1)S(1)} %collective-permute-done.3.refs_2_, ...), custom_call_target="tpu_custom_call" | custom-call | flops 2415919104 | bytes 13107200 | tf_op jit(solution)/shard_map/pallas_call | solution.py:40
  67.4 2.9 %collective-permute-done.refs_2_ = bf16[64,4096]{1,0:T(8,128)(2,1)S(1)} collective-permute-done((bf16[64,4096]{1,0:T(8,128)(2,1)S(1)}, bf16[64,4096]{1,0:T(8,128)(2,1)S(1)}, u32[]{:S(2)}, u32[]{:S(2)}) %collective-permute-start) | collective-permute-done | bytes 524320 | tf_op jit(solution)/shard_map/ppermute | solution.py:74
  71.6 2.2 %collective-permute-start.12 = (bf16[32,4096]{1,0:T(8,128)(2,1)S(1)}, bf16[32,4096]{1,0:T(8,128)(2,1)S(1)}, u32[]{:S(2)}, u32[]{:S(2)}) collective-permute-start(bf16[32,4096]{1,0:T(8,128)(2,1)S(1)} %slice.95), channel_id=1, source_target_pairs={{0,192},{32,224},{64,0},{96,32},{128,64},{160,96},{192,128},{224,1... | collective-permute-start | bytes 786440 | tf_op jit(solution)/shard_map/ppermute | solution.py:74
  74.0 3.2 %collective-permute-start.15 = (bf16[32,4096]{1,0:T(8,128)(2,1)S(1)}, bf16[32,4096]{1,0:T(8,128)(2,1)S(1)}, u32[]{:S(2)}, u32[]{:S(2)}) collective-permute-start(bf16[32,4096]{1,0:T(8,128)(2,1)S(1)} %get-tuple-element.55), channel_id=1, source_target_pairs={{0,192},{32,224},{64,0},{96,32},{128,64},{160,96},{192,128},{224,1... | collective-permute-start | bytes 786440 | tf_op jit(solution)/shard_map/ppermute | solution.py:74
  77.2 2.9 %collective-permute-done.11.refs_3_ = bf16[32,4096]{1,0:T(8,128)(2,1)S(1)} collective-permute-done((bf16[32,4096]{1,0:T(8,128)(2,1)S(1)}, bf16[32,4096]{1,0:T(8,128)(2,1)S(1)}, u32[]{:S(2)}, u32[]{:S(2)}) %collective-permute-start.11) | collective-permute-done | bytes 262176 | tf_op jit(solution)/shard_map/ppermute | solution.py:74
  80.7 2.3 %collective-permute-done.14 = bf16[32,4096]{1,0:T(8,128)(2,1)S(1)} collective-permute-done((bf16[32,4096]{1,0:T(8,128)(2,1)S(1)}, bf16[32,4096]{1,0:T(8,128)(2,1)S(1)}, u32[]{:S(2)}, u32[]{:S(2)}) %collective-permute-start.14) | collective-permute-done | bytes 262176 | tf_op jit(solution)/shard_map/ppermute | solution.py:74
  84.2 1.8 %collective-permute-start.17 = (bf16[64,4096]{1,0:T(8,128)(2,1)S(1)}, bf16[64,4096]{1,0:T(8,128)(2,1)S(1)}, u32[]{:S(2)}, u32[]{:S(2)}) collective-permute-start(bf16[64,4096]{1,0:T(8,128)(2,1)S(1)} %get-tuple-element.52), channel_id=1, source_target_pairs={{0,64},{32,96},{64,128},{96,160},{128,192},{160,224},{192,0},{224,... | collective-permute-start | bytes 1572872 | tf_op jit(solution)/shard_map/ppermute | solution.py:74
  87.5 6.9 %shard_map.65 = (bf16[256,4096]{1,0:T(8,128)(2,1)S(1)}, bf16[64,4096]{1,0:T(8,128)(2,1)S(1)}, bf16[192,4096]{1,0:T(8,128)(2,1)}) custom-call(bf16[64,4096]{1,0:T(8,128)(2,1)S(1)} %reshape.75.refs_0_, bf16[64,4096]{1,0:T(8,128)(2,1)S(1)} %collective-permute-done.1.refs_1_, bf16[64,4096]{1,0:T(8,128)(2,1)S(1)} %collective-permute-done.refs_2_, ...), custom_call_target="tpu_custom_call" | custom-call | flops 2415919104 | bytes 13107200 | tf_op jit(solution)/shard_map/pallas_call | solution.py:40
  95.2 4.3 %collective-permute-done.17 = bf16[64,4096]{1,0:T(8,128)(2,1)S(1)} collective-permute-done((bf16[64,4096]{1,0:T(8,128)(2,1)S(1)}, bf16[64,4096]{1,0:T(8,128)(2,1)S(1)}, u32[]{:S(2)}, u32[]{:S(2)}) %collective-permute-start.17) | collective-permute-done | bytes 524320 | tf_op jit(solution)/shard_map/ppermute | solution.py:74
  101.1 2.5 %collective-permute-start.28 = (bf16[32,4096]{1,0:T(8,128)(2,1)S(1)}, bf16[32,4096]{1,0:T(8,128)(2,1)S(1)}, u32[]{:S(2)}, u32[]{:S(2)}) collective-permute-start(bf16[32,4096]{1,0:T(8,128)(2,1)S(1)} %get-tuple-element.54), channel_id=1, source_target_pairs={{0,192},{32,224},{64,0},{96,32},{128,64},{160,96},{192,128},{224,1... | collective-permute-start | bytes 786440 | tf_op jit(solution)/shard_map/ppermute | solution.py:74
  105.0 8.9 %all-to-all-start.2 = ((bf16[32,2,4096]{2,1,0:T(2,128)(2,1)}), bf16[32,2,4096]{2,1,0:T(2,128)(2,1)S(1)}, u32[]{:S(2)}, u32[]{:S(2)}) async-start(bf16[32,2,4096]{2,1,0:T(2,128)(2,1)} %reshape.78), calls=%async_computation.2 | async-start | bytes 1048576 | tf_op jit(solution)/shard_map/all_to_all | solution.py:107
  114.0 2.5 %add_convert_fusion.2 = (bf16[64,4096]{1,0:T(8,128)(2,1)}, bf16[64,4096]{1,0:T(8,128)(2,1)}) fusion(bf16[192,4096]{1,0:T(8,128)(2,1)} %collective-permute-done.24, bf16[32,4096]{1,0:T(8,128)(2,1)S(1)} %collective-permute-done.26, bf16[256,4096]{1,0:T(8,128)(2,1)S(1)} %get-tuple-element.45, bf16[32,4096]{1,0:T(8,128)(2,1)S(1)} %collective-permute-done.28), kind=kLoop, calls=%fused_computation.6 | loop fusion | flops 3145728 | bytes 3670016 | tf_op jit(solution)/shard_map/convert_element_type | solution.py:113
  116.5 3.2 %collective-permute-start.29 = (bf16[64,4096]{1,0:T(8,128)(2,1)}, bf16[64,4096]{1,0:T(8,128)(2,1)}, u32[]{:S(2)}, u32[]{:S(2)}) collective-permute-start(bf16[64,4096]{1,0:T(8,128)(2,1)} %get-tuple-element.50), channel_id=1, source_target_pairs={{0,192},{32,224},{64,0},{96,32},{128,64},{160,96},{192,128},{224,1... | collective-permute-start | bytes 1572872 | tf_op jit(solution)/shard_map/ppermute | solution.py:74
  119.9 10.1 %all-to-all-done.2 = bf16[32,2,4096]{2,1,0:T(2,128)(2,1)S(1)} async-done(((bf16[32,2,4096]{2,1,0:T(2,128)(2,1)}), bf16[32,2,4096]{2,1,0:T(2,128)(2,1)S(1)}, u32[]{:S(2)}, u32[]{:S(2)}) %all-to-all-start.2) | async-done | bytes 524320 | tf_op jit(solution)/shard_map/all_to_all | solution.py:107
  132.5 24.1 %all_to_all.20 = bf16[32,2,4096]{2,1,0:T(2,128)(2,1)S(1)} all-to-all(bf16[32,2,4096]{2,1,0:T(2,128)(2,1)S(1)} %reshape.80), channel_id=1, replica_groups=mesh['dp'=8,'expert'=32] {'expert'}, dimensions={0} | all-to-all | bytes 1048576 | tf_op jit(solution)/shard_map/all_to_all | solution.py:107
  (90 shorter events, 21.8 us)
Async XLA Ops:
  2.8 28.5 %all-to-all-start = ((bf16[32,2,4096]{2,1,0:T(2,128)(2,1)}), bf16[32,2,4096]{2,1,0:T(2,128)(2,1)S(1)}, u32[]{:S(2)}, u32[]{:S(2)}) async-start(bf16[32,2,4096]{2,1,0:T(2,128)(2,1)} %reshape.73), calls=%async_computation | async-start | bytes 1048576 | tf_op jit(solution)/shard_map/all_to_all | solution.py:107
  31.5 13.8 %collective-permute-start.3 = (bf16[64,4096]{1,0:T(8,128)(2,1)S(1)}, bf16[64,4096]{1,0:T(8,128)(2,1)S(1)}, u32[]{:S(2)}, u32[]{:S(2)}) collective-permute-start(bf16[64,4096]{1,0:T(8,128)(2,1)S(1)} %reshape.76.refs_0_), channel_id=1, source_target_pairs={{0,64},{32,96},{64,128},{96,160},{128,192},{160,224},{192,0},{224,... | collective-permute-start | bytes 1572872 | tf_op jit(solution)/shard_map/ppermute | solution.py:74
  33.2 12.5 %collective-permute-start.2 = (bf16[64,4096]{1,0:T(8,128)(2,1)S(1)}, bf16[64,4096]{1,0:T(8,128)(2,1)S(1)}, u32[]{:S(2)}, u32[]{:S(2)}) collective-permute-start(bf16[64,4096]{1,0:T(8,128)(2,1)S(1)} %reshape.76.refs_0_), channel_id=1, source_target_pairs={{0,192},{32,224},{64,0},{96,32},{128,64},{160,96},{192,128},{224,1... | collective-permute-start | bytes 1572872 | tf_op jit(solution)/shard_map/ppermute | solution.py:74
  34.8 21.2 %all-to-all-start.1 = ((bf16[32,2,4096]{2,1,0:T(2,128)(2,1)}), bf16[32,2,4096]{2,1,0:T(2,128)(2,1)}, u32[]{:S(2)}, u32[]{:S(2)}) async-start(bf16[32,2,4096]{2,1,0:T(2,128)(2,1)} %reshape.74), calls=%async_computation.1 | async-start | bytes 1048576 | tf_op jit(solution)/shard_map/all_to_all | solution.py:107
  40.4 16.8 %collective-permute-start.8 = (bf16[64,4096]{1,0:T(8,128)(2,1)S(1)}, bf16[64,4096]{1,0:T(8,128)(2,1)S(1)}, u32[]{:S(2)}, u32[]{:S(2)}) collective-permute-start(bf16[64,4096]{1,0:T(8,128)(2,1)S(1)} %reshape.76.refs_0_), channel_id=1, source_target_pairs={{0,32},{32,0},{64,96},{96,64},{128,160},{160,128},{192,224},{224,1... | collective-permute-start | bytes 1572872 | tf_op jit(solution)/shard_map/ppermute | solution.py:81
  45.3 7.7 %collective-permute-start.4 = (bf16[32,4096]{1,0:T(8,128)(2,1)S(1)}, bf16[32,4096]{1,0:T(8,128)(2,1)S(1)}, u32[]{:S(2)}, u32[]{:S(2)}) collective-permute-start(bf16[32,4096]{1,0:T(8,128)(2,1)S(1)} %slice.120), channel_id=1, source_target_pairs={{0,64},{32,96},{64,128},{96,160},{128,192},{160,224},{192,0},{224,... | collective-permute-start | bytes 786440 | tf_op jit(solution)/shard_map/ppermute | solution.py:74
  48.7 11.9 %collective-permute-start.10 = (bf16[64,4096]{1,0:T(8,128)(2,1)S(1)}, bf16[64,4096]{1,0:T(8,128)(2,1)S(1)}, u32[]{:S(2)}, u32[]{:S(2)}) collective-permute-start(bf16[64,4096]{1,0:T(8,128)(2,1)S(1)} %collective-permute-done.3.refs_2_), channel_id=1, source_target_pairs={{0,32},{32,0},{64,96},{96,64},{128,160},{160,128},{192,224},{224,1... | collective-permute-start | bytes 1572872 | tf_op jit(solution)/shard_map/ppermute | solution.py:81
  48.7 11.9 %collective-permute-start.9 = (bf16[64,4096]{1,0:T(8,128)(2,1)S(1)}, bf16[64,4096]{1,0:T(8,128)(2,1)}, u32[]{:S(2)}, u32[]{:S(2)}) collective-permute-start(bf16[64,4096]{1,0:T(8,128)(2,1)S(1)} %collective-permute-done.2.refs_1_), channel_id=1, source_target_pairs={{0,32},{32,0},{64,96},{96,64},{128,160},{160,128},{192,224},{224,1... | collective-permute-start | bytes 1572872 | tf_op jit(solution)/shard_map/ppermute | solution.py:81
  53.0 7.6 %collective-permute-start.7 = (bf16[32,4096]{1,0:T(8,128)(2,1)}, bf16[32,4096]{1,0:T(8,128)(2,1)}, u32[]{:S(2)}, u32[]{:S(2)}) collective-permute-start(bf16[32,4096]{1,0:T(8,128)(2,1)} %collective-permute-done.5.refs_4_), channel_id=1, source_target_pairs={{0,32},{32,0},{64,96},{96,64},{128,160},{160,128},{192,224},{224,1... | collective-permute-start | bytes 786440 | tf_op jit(solution)/shard_map/ppermute | solution.py:81
  57.2 13.1 %collective-permute-start = (bf16[64,4096]{1,0:T(8,128)(2,1)S(1)}, bf16[64,4096]{1,0:T(8,128)(2,1)S(1)}, u32[]{:S(2)}, u32[]{:S(2)}) collective-permute-start(bf16[64,4096]{1,0:T(8,128)(2,1)S(1)} %reshape.75.refs_0_), channel_id=1, source_target_pairs={{0,64},{32,96},{64,128},{96,160},{128,192},{160,224},{192,0},{224,... | collective-permute-start | bytes 1572872 | tf_op jit(solution)/shard_map/ppermute | solution.py:74
  57.6 12.8 %collective-permute-start.1 = (bf16[64,4096]{1,0:T(8,128)(2,1)S(1)}, bf16[64,4096]{1,0:T(8,128)(2,1)S(1)}, u32[]{:S(2)}, u32[]{:S(2)}) collective-permute-start(bf16[64,4096]{1,0:T(8,128)(2,1)S(1)} %reshape.75.refs_0_), channel_id=1, source_target_pairs={{0,192},{32,224},{64,0},{96,32},{128,64},{160,96},{192,128},{224,1... | collective-permute-start | bytes 1572872 | tf_op jit(solution)/shard_map/ppermute | solution.py:74
  66.9 16.6 %collective-permute-start.16 = (bf16[192,4096]{1,0:T(8,128)(2,1)S(1)}, bf16[192,4096]{1,0:T(8,128)(2,1)S(1)}, u32[]{:S(2)}, u32[]{:S(2)}) collective-permute-start(bf16[192,4096]{1,0:T(8,128)(2,1)S(1)} %get-tuple-element.39), channel_id=1, source_target_pairs={{0,32},{32,0},{64,96},{96,64},{128,160},{160,128},{192,224},{224,1... | collective-permute-start | bytes 4718600 | tf_op jit(solution)/shard_map/ppermute | solution.py:81
  70.4 9.8 %collective-permute-start.11 = (bf16[32,4096]{1,0:T(8,128)(2,1)S(1)}, bf16[32,4096]{1,0:T(8,128)(2,1)S(1)}, u32[]{:S(2)}, u32[]{:S(2)}) collective-permute-start(bf16[32,4096]{1,0:T(8,128)(2,1)S(1)} %slice.94), channel_id=1, source_target_pairs={{0,64},{32,96},{64,128},{96,160},{128,192},{160,224},{192,0},{224,... | collective-permute-start | bytes 786440 | tf_op jit(solution)/shard_map/ppermute | solution.py:74
  71.6 8.9 %collective-permute-start.12 = (bf16[32,4096]{1,0:T(8,128)(2,1)S(1)}, bf16[32,4096]{1,0:T(8,128)(2,1)S(1)}, u32[]{:S(2)}, u32[]{:S(2)}) collective-permute-start(bf16[32,4096]{1,0:T(8,128)(2,1)S(1)} %slice.95), channel_id=1, source_target_pairs={{0,192},{32,224},{64,0},{96,32},{128,64},{160,96},{192,128},{224,1... | collective-permute-start | bytes 786440 | tf_op jit(solution)/shard_map/ppermute | solution.py:74
  73.9 9.1 %collective-permute-start.14 = (bf16[32,4096]{1,0:T(8,128)(2,1)S(1)}, bf16[32,4096]{1,0:T(8,128)(2,1)S(1)}, u32[]{:S(2)}, u32[]{:S(2)}) collective-permute-start(bf16[32,4096]{1,0:T(8,128)(2,1)S(1)} %get-tuple-element.56), channel_id=1, source_target_pairs={{0,64},{32,96},{64,128},{96,160},{128,192},{160,224},{192,0},{224,... | collective-permute-start | bytes 786440 | tf_op jit(solution)/shard_map/ppermute | solution.py:74
  74.0 9.3 %collective-permute-start.15 = (bf16[32,4096]{1,0:T(8,128)(2,1)S(1)}, bf16[32,4096]{1,0:T(8,128)(2,1)S(1)}, u32[]{:S(2)}, u32[]{:S(2)}) collective-permute-start(bf16[32,4096]{1,0:T(8,128)(2,1)S(1)} %get-tuple-element.55), channel_id=1, source_target_pairs={{0,192},{32,224},{64,0},{96,32},{128,64},{160,96},{192,128},{224,1... | collective-permute-start | bytes 786440 | tf_op jit(solution)/shard_map/ppermute | solution.py:74
  84.2 15.3 %collective-permute-start.17 = (bf16[64,4096]{1,0:T(8,128)(2,1)S(1)}, bf16[64,4096]{1,0:T(8,128)(2,1)S(1)}, u32[]{:S(2)}, u32[]{:S(2)}) collective-permute-start(bf16[64,4096]{1,0:T(8,128)(2,1)S(1)} %get-tuple-element.52), channel_id=1, source_target_pairs={{0,64},{32,96},{64,128},{96,160},{128,192},{160,224},{192,0},{224,... | collective-permute-start | bytes 1572872 | tf_op jit(solution)/shard_map/ppermute | solution.py:74
  86.0 13.6 %collective-permute-start.18 = (bf16[64,4096]{1,0:T(8,128)(2,1)S(1)}, bf16[64,4096]{1,0:T(8,128)(2,1)S(1)}, u32[]{:S(2)}, u32[]{:S(2)}) collective-permute-start(bf16[64,4096]{1,0:T(8,128)(2,1)S(1)} %get-tuple-element.51), channel_id=1, source_target_pairs={{0,192},{32,224},{64,0},{96,32},{128,64},{160,96},{192,128},{224,1... | collective-permute-start | bytes 1572872 | tf_op jit(solution)/shard_map/ppermute | solution.py:74
  94.6 19.4 %collective-permute-start.24 = (bf16[192,4096]{1,0:T(8,128)(2,1)}, bf16[192,4096]{1,0:T(8,128)(2,1)}, u32[]{:S(2)}, u32[]{:S(2)}) collective-permute-start(bf16[192,4096]{1,0:T(8,128)(2,1)} %get-tuple-element.46), channel_id=1, source_target_pairs={{0,32},{32,0},{64,96},{96,64},{128,160},{160,128},{192,224},{224,1... | collective-permute-start | bytes 4718600 | tf_op jit(solution)/shard_map/ppermute | solution.py:81
  100.4 13.6 %collective-permute-start.26 = (bf16[32,4096]{1,0:T(8,128)(2,1)}, bf16[32,4096]{1,0:T(8,128)(2,1)S(1)}, u32[]{:S(2)}, u32[]{:S(2)}) collective-permute-start(bf16[32,4096]{1,0:T(8,128)(2,1)} %get-tuple-element.53), channel_id=1, source_target_pairs={{0,64},{32,96},{64,128},{96,160},{128,192},{160,224},{192,0},{224,... | collective-permute-start | bytes 786440 | tf_op jit(solution)/shard_map/ppermute | solution.py:74
  101.1 12.8 %collective-permute-start.28 = (bf16[32,4096]{1,0:T(8,128)(2,1)S(1)}, bf16[32,4096]{1,0:T(8,128)(2,1)S(1)}, u32[]{:S(2)}, u32[]{:S(2)}) collective-permute-start(bf16[32,4096]{1,0:T(8,128)(2,1)S(1)} %get-tuple-element.54), channel_id=1, source_target_pairs={{0,192},{32,224},{64,0},{96,32},{128,64},{160,96},{192,128},{224,1... | collective-permute-start | bytes 786440 | tf_op jit(solution)/shard_map/ppermute | solution.py:74
  105.0 25.0 %all-to-all-start.2 = ((bf16[32,2,4096]{2,1,0:T(2,128)(2,1)}), bf16[32,2,4096]{2,1,0:T(2,128)(2,1)S(1)}, u32[]{:S(2)}, u32[]{:S(2)}) async-start(bf16[32,2,4096]{2,1,0:T(2,128)(2,1)} %reshape.78), calls=%async_computation.2 | async-start | bytes 1048576 | tf_op jit(solution)/shard_map/all_to_all | solution.py:107
  116.5 14.0 %collective-permute-start.27 = (bf16[64,4096]{1,0:T(8,128)(2,1)}, bf16[64,4096]{1,0:T(8,128)(2,1)}, u32[]{:S(2)}, u32[]{:S(2)}) collective-permute-start(bf16[64,4096]{1,0:T(8,128)(2,1)} %get-tuple-element.49), channel_id=1, source_target_pairs={{0,64},{32,96},{64,128},{96,160},{128,192},{160,224},{192,0},{224,... | collective-permute-start | bytes 1572872 | tf_op jit(solution)/shard_map/ppermute | solution.py:74
  116.5 14.0 %collective-permute-start.29 = (bf16[64,4096]{1,0:T(8,128)(2,1)}, bf16[64,4096]{1,0:T(8,128)(2,1)}, u32[]{:S(2)}, u32[]{:S(2)}) collective-permute-start(bf16[64,4096]{1,0:T(8,128)(2,1)} %get-tuple-element.50), channel_id=1, source_target_pairs={{0,192},{32,224},{64,0},{96,32},{128,64},{160,96},{192,128},{224,1... | collective-permute-start | bytes 1572872 | tf_op jit(solution)/shard_map/ppermute | solution.py:74
  (11 other events, 56.1 us)
